TPU v7x, 512 devices: a whole 4x4x16 slice. The times are simulated.
512 devices in a mesh: cuts: 8 (over z_lo), fsdp: 64 (over x, z_hi, y, core).
Axes of the slice: x: 4, y: 4, z: 16 (z_hi: 2, z_lo: 8; z = z_hi * 8 + z_lo), core: 2. Of those that a mesh axis runs over, the one named last changes fastest.
Arguments:
- activations: bfloat16 [81920, 1536], P(('cuts', 'fsdp')), may hold values from -6 to 6
- cotangent: bfloat16 [81920, 2048], P(('cuts', 'fsdp')), may hold values from -0.01953125 to 0.01953125
- weights: bfloat16 [1536, 2048], P('fsdp'), may hold values from -0.15625 to 0.15625
- first_moment: float32 [1536, 2048], P('fsdp'), may hold values from -4 to 4
- second_moment: float32 [1536, 2048], P('fsdp'), may hold values from 0.05 to 2
- residue: float32 [8, 1536, 2048], P('cuts', 'fsdp'), may hold values from -3 to 3
Outputs:
- projected: bfloat16 [81920, 2048], P(('cuts', 'fsdp'))
- new_first: float32 [1536, 2048], P('fsdp')
- new_second: float32 [1536, 2048], P('fsdp')
All inputs are finite; a program needn't handle non-finite values.
Results may differ from a plain program's by a relative error of at most 0.0049.
Values may be sent and summed in bfloat16 or wider, within the bound.
No kernel may reach another device: no remote copies, remote signals or barrier semaphores. Data moves between devices by JAX's collectives and lax.ppermute only.
A program may use at most 64 MiB of HBM per device.

v0:
```python
import jax
import jax.numpy as jnp
from jax import lax
from jax.sharding import PartitionSpec as P

HEAD_SIZE = 256


def relay(activations, cot_part, weight_part, first_part, second_part, residue_part):
    fsdp_count = lax.axis_size("fsdp")
    own_rows = weight_part.shape[0]
    width = cot_part.shape[1]
    heads = width // HEAD_SIZE
    term = lax.dot_general(
        activations, cot_part, (((0,), (0,)), ((), ())), preferred_element_type=jnp.float32
    )
    pieces = term.astype(jnp.bfloat16).reshape(fsdp_count, own_rows, width)
    arrived = lax.all_to_all(pieces, "fsdp", split_axis=0, concat_axis=0, tiled=True)
    slice_grad = jnp.sum(arrived, axis=0, dtype=jnp.float32)
    combined = slice_grad + residue_part[0]
    blocks = combined.reshape(own_rows, heads, HEAD_SIZE)
    scale_low = (jnp.max(jnp.abs(blocks), axis=-1) + 1e-06).astype(jnp.bfloat16)
    scale = scale_low.astype(jnp.float32)
    codes = (blocks / scale[..., None]).astype(jnp.bfloat16)
    all_codes, all_scales = (
        lax.all_gather(codes, "cuts", axis=0, tiled=True),
        lax.all_gather(scale_low, "cuts", axis=0, tiled=True),
    )
    cut_count = lax.axis_size("cuts")
    decoded = all_codes.reshape(cut_count, own_rows, heads, HEAD_SIZE).astype(jnp.float32)
    weighted = (
        decoded * all_scales.reshape(cut_count, own_rows, heads).astype(jnp.float32)[..., None]
    )
    grad = jnp.sum(weighted, axis=0)
    grad = grad.reshape(own_rows, width)
    new_first = 0.9 * first_part + 0.1 * grad
    new_second = 0.95 * second_part + 0.05 * grad * grad
    update = new_first / (1.0 - 0.9**10) / (jnp.sqrt(new_second / (1.0 - 0.95**10)) + 1e-08)
    new_weights = (weight_part.astype(jnp.float32) * (1.0 - 0.002 * 0.1) - 0.002 * update).astype(
        jnp.bfloat16
    )
    projected = jnp.dot(
        activations,
        lax.all_gather(new_weights, "fsdp", axis=0, tiled=True),
        preferred_element_type=jnp.float32,
    )
    return (projected.astype(jnp.bfloat16), new_first, new_second)


def shards(activations, cotangent, weights, first_moment, second_moment, residue):
    return relay(activations, cotangent, weights, first_moment, second_moment, residue)


def solution(mesh):
    in_specs = (
        P(("cuts", "fsdp"), None),
        P(("cuts", "fsdp"), None),
        P("fsdp", None),
        P("fsdp", None),
        P("fsdp", None),
        P("cuts", "fsdp", None),
    )
    out_specs = (P(("cuts", "fsdp"), None), P("fsdp", None), P("fsdp", None))
    return jax.shard_map(shards, mesh=mesh, in_specs=in_specs, out_specs=out_specs, check_vma=False)
```

profile of v0, /device:TPU:1, one launch (start us, length us, event | category | flops | bytes accessed | tf_op | source)
XLA Modules:
  0.0 568.2 jit_solution(5722564977853573995)
XLA Ops:
  7.2 0.0 copy-start
  7.2 1.1 copy-done
  8.3 5.5 convolution_convert_fusion
  13.8 0.0 copy-start.4
  13.8 22.5 %all-to-all-start = ((bf16[64,24,2048]{2,1,0:T(8,128)(2,1)}), bf16[64,24,2048]{2,1,0:T(8,128)(2,1)}, u32[]{:S(2)}, u32[]{:S(2)}) async-start(bf16[64,24,2048]{2,1,0:T(8,128)(2,1)} %bitcast.20), calls=%async_computation | async-start | bytes 12582912 | tf_op jit(solution)/shard_map/all_to_all | solution.py:18
  36.3 0.0 copy-start.2
  36.3 0.0 copy-start.3
  36.4 0.0 copy-start.5
  36.4 0.0 copy-start.1
  36.4 0.0 all-gather.3.cloned.1.call-start
  36.4 0.0 copy-done.4
  36.4 0.1 copy.14
  36.5 170.1 %all-to-all-done = bf16[64,24,2048]{2,1,0:T(8,128)(2,1)} async-done(((bf16[64,24,2048]{2,1,0:T(8,128)(2,1)}), bf16[64,24,2048]{2,1,0:T(8,128)(2,1)}, u32[]{:S(2)}, u32[]{:S(2)}) %all-to-all-start) | async-done | bytes 6291488 | tf_op jit(solution)/shard_map/all_to_all | solution.py:18
  206.6 3.9 convert_reduce_fusion
  210.5 0.1 copy.13
  210.6 0.1 abs_reduce_fusion
  210.7 0.1 divide_convert_fusion
  210.8 152.8 %all_gather.9 = bf16[192,8,256]{2,1,0:T(8,128)(2,1)S(1)} all-gather(bf16[24,8,256]{2,1,0:T(8,128)(2,1)S(1)} %divide_convert_fusion), channel_id=1, replica_groups=mesh['cuts'=8,'fsdp'=64] {'cuts'}, dimensions={0}, use_global_device_ids=true | all-gather | bytes 884736 | tf_op jit(solution)/shard_map/all_gather | solution.py:26
  363.7 0.1 copy.11
  363.7 37.1 %all-gather = bf16[8,24,8]{1,2,0:T(8,128)(2,1)S(1)} all-gather(bf16[1,24,8]{1,2,0:T(8,128)(2,1)S(1)} %copy.11), channel_id=1, replica_groups=mesh['cuts'=8,'fsdp'=64] {'cuts'}, dimensions={0}, use_global_device_ids=true | all-gather | bytes 3456 | tf_op jit(solution)/shard_map/all_gather | solution.py:27
  400.8 0.1 copy.12
  400.9 0.3 fusion.1
  401.2 0.1 copy.15
  401.2 0.0 copy-done.2
  401.2 0.0 copy-done.3
  401.3 0.0 copy-done.5
  401.3 0.9 subtract_convert_fusion
  402.1 0.0 all-gather.3.cloned.1.call-update
  402.1 154.4 %all-gather.3.cloned.1.call-done = bf16[1536,2048]{1,0:T(8,128)(2,1)} async-done(((bf16[24,2048]{1,0:T(8,128)(2,1)}), bf16[1536,2048]{1,0:T(8,128)(2,1)}) %all-gather.3.cloned.1.call-update) | async-done | bytes 6291472 | tf_op jit(solution)/shard_map/all_gather | solution.py:44
  556.6 0.0 copy-done.1
  556.6 4.8 fusion
  (2 shorter events, 0.0 us)
Async XLA Ops:
  7.2 1.1 copy-start
  13.8 22.6 %copy-start.4 = (f32[1,24,2048]{2,1,0:T(8,128)S(1)}, f32[1,24,2048]{2,1,0:T(8,128)}, u32[]{:S(2)}) copy-start(f32[1,24,2048]{2,1,0:T(8,128)} %param.11) | copy-start | bytes 589828
  13.8 192.8 %all-to-all-start = ((bf16[64,24,2048]{2,1,0:T(8,128)(2,1)}), bf16[64,24,2048]{2,1,0:T(8,128)(2,1)}, u32[]{:S(2)}, u32[]{:S(2)}) async-start(bf16[64,24,2048]{2,1,0:T(8,128)(2,1)} %bitcast.20), calls=%async_computation | async-start | bytes 12582912 | tf_op jit(solution)/shard_map/all_to_all | solution.py:18
  36.3 364.9 %copy-start.2 = (f32[24,2048]{1,0:T(8,128)S(1)}, f32[24,2048]{1,0:T(8,128)}, u32[]{:S(2)}) copy-start(f32[24,2048]{1,0:T(8,128)} %param.9) | copy-start | bytes 589828
  36.3 364.9 %copy-start.3 = (f32[24,2048]{1,0:T(8,128)S(1)}, f32[24,2048]{1,0:T(8,128)}, u32[]{:S(2)}) copy-start(f32[24,2048]{1,0:T(8,128)} %param.10) | copy-start | bytes 589828
  36.4 364.9 %copy-start.5 = (bf16[24,2048]{1,0:T(8,128)(2,1)S(1)}, bf16[24,2048]{1,0:T(8,128)(2,1)}, u32[]{:S(2)}) copy-start(bf16[24,2048]{1,0:T(8,128)(2,1)} %param.8) | copy-start | bytes 294916
  36.4 520.2 %copy-start.1 = (bf16[160,1536]{1,0:T(8,128)(2,1)S(1)}, bf16[160,1536]{1,0:T(8,128)(2,1)}, u32[]{:S(2)}) copy-start(bf16[160,1536]{1,0:T(8,128)(2,1)} %param.6) | copy-start | bytes 1474564
  36.4 520.2 %all-gather.3.cloned.1.call-start = ((), (), s32[]{:S(2)}) async-start(), calls=%async_computation.1 | async-start | bytes 6389760 | tf_op jit(solution)/shard_map/all_gather | solution.py:44
Sparse Core Ops, SparseCore 0:
  402.3 154.2 all-gather.2
where the time goes:
time: 569 us; the launch traced here: 568 us
  waiting for transfers between devices  325 us (57%)
  blocking collectives  190 us (33%)
  starting transfers between devices  22.6 us (4%)
  between operations  14.2 us (2%)
  matrix products  10.3 us (2%)
    all_to_all x1, waiting for transfers between devices, relay(): lax.all_to_all(pieces, 'fsdp', split_axis=0, concat_axis=0, tiled=True)  170 us
    all_gather x1, waiting for transfers between devices, relay(): lax.all_gather(new_weights, 'fsdp', axis=0, tiled=True)  154 us
    all_gather x1, blocking collectives, relay(): lax.all_gather(codes, 'cuts', axis=0, tiled=True)  153 us
    all_gather x1, blocking collectives, relay(): lax.all_gather(scale_low, 'cuts', axis=0, tiled=True)  37.1 us
    all_to_all x1, starting transfers between devices, relay(): lax.all_to_all(pieces, 'fsdp', split_axis=0, concat_axis=0, tiled=True)  22.5 us
  transfers between devices with their start and end apart: 2, of which 2 were waited for; matrix products, arithmetic and copies ran while one was open for 0% of the time, Pallas kernels for 0%

commit v1 on v0

v1 whole, which is shorter than its diff:
```python
import jax
import jax.numpy as jnp
from jax import lax
from jax.sharding import Mesh, PartitionSpec as P

HEAD_SIZE = 256
BF16 = jnp.bfloat16
F32 = jnp.float32


def update_of(grad, first, second, weight):
    new_first = 0.9 * first + 0.1 * grad
    new_second = 0.95 * second + 0.05 * grad * grad
    update = new_first / (1.0 - 0.9**10) / (jnp.sqrt(new_second / (1.0 - 0.95**10)) + 1e-08)
    new_weight = weight.astype(F32) * (1.0 - 0.002 * 0.1) - 0.002 * update
    return new_first, new_second, new_weight.astype(BF16)


def relay(act, cot, weight, first, second, residue):
    nx, ny, nz, nzh = (lax.axis_size(a) for a in ("x", "y", "zl", "zh"))
    core, zh, zl = (lax.axis_index(a) for a in ("core", "zh", "zl"))
    tok, width = cot.shape
    own = weight.shape[0]
    heads = width // HEAD_SIZE
    per = heads // nz * HEAD_SIZE
    rows = nzh * own
    swap = [(0, 1), (1, 0)]

    turned = act.T.reshape(nx, nzh, ny, 2, own, tok).transpose(3, 0, 2, 1, 4, 5)
    turned = turned.reshape(2, nx * ny * rows, tok)
    mine = lax.dynamic_index_in_dim(turned, core, 0, keepdims=False)
    other = lax.dynamic_index_in_dim(turned, 1 - core, 0, keepdims=False)
    other_act = lax.ppermute(other, "core", swap)
    other_cot = lax.ppermute(cot, "core", swap)

    def columns(a):
        return lax.dynamic_slice_in_dim(a, zl * per, per, 1)

    states = jnp.stack([columns(first), columns(second), columns(weight).astype(F32)])
    far = lax.ppermute(states, "zh", swap)
    both = jnp.stack([jnp.where(zh == 0, states, far), jnp.where(zh == 0, far, states)], axis=1)
    both = both.reshape(3, rows, per)

    term = jnp.dot(mine, cot, preferred_element_type=F32)
    term = term + jnp.dot(other_act, other_cot, preferred_element_type=F32)
    pieces = term.astype(BF16).reshape(nx * ny, rows, width)
    arrived = lax.all_to_all(pieces, ("x", "y"), split_axis=0, concat_axis=0, tiled=True)
    part = jnp.sum(arrived, axis=0, dtype=F32).reshape(nzh, own, width)
    here = (jnp.arange(nzh) == zh)[:, None, None]
    part = part + jnp.where(here, residue, 0.0)

    part = part.astype(BF16).reshape(rows, nz, per).transpose(1, 0, 2)
    part = jnp.broadcast_to(part[:, None], (nz, nzh, rows, per)).reshape(nz * nzh, rows, per)
    parts = lax.all_to_all(part, ("zl", "zh"), split_axis=0, concat_axis=0, tiled=True)
    combined = jnp.sum(parts.reshape(nz, nzh, rows, per), axis=1, dtype=F32)
    blocks = combined.reshape(nz, rows, per // HEAD_SIZE, HEAD_SIZE)
    scale = (jnp.max(jnp.abs(blocks), axis=-1) + 1e-06).astype(BF16).astype(F32)
    codes = (blocks / scale[..., None]).astype(BF16)
    grad = jnp.sum(codes.astype(F32) * scale[..., None], axis=0).reshape(rows, per)
    _, _, new_part = update_of(grad, both[0], both[1], both[2])

    own_grad = lax.dynamic_slice_in_dim(grad, zh * own, own, 0)
    high = lax.reduce_precision(own_grad, 8, 7)
    low = (own_grad - high).astype(BF16)
    packed = jnp.concatenate([new_part, high.astype(BF16), low], axis=0)
    packed = jnp.broadcast_to(packed[None], (nz,) + packed.shape)
    packed = lax.all_to_all(packed, "zl", split_axis=0, concat_axis=0, tiled=True)
    spread = packed.transpose(1, 0, 2).reshape(rows + 2 * own, width)
    full_grad = spread[rows : rows + own].astype(F32) + spread[rows + own :].astype(F32)
    new_first, new_second, _ = update_of(full_grad, first, second, weight)

    sent = jnp.broadcast_to(spread[None, :rows], (nx * ny, rows, width))
    new_weights = lax.all_to_all(sent, ("x", "y"), split_axis=0, concat_axis=0, tiled=True)
    new_weights = new_weights.reshape(nx * ny * rows, width)

    def project(turned_act):
        return lax.dot_general(
            turned_act, new_weights, (((0,), (0,)), ((), ())), preferred_element_type=F32
        )

    other_out = lax.ppermute(project(other_act).astype(BF16), "core", swap)
    projected = project(mine) + other_out.astype(F32)
    return projected.astype(BF16), new_first, new_second


def solution(mesh):
    names = ("zl", "x", "zh", "y", "core")
    fine = Mesh(mesh.devices.reshape(8, 4, 2, 4, 2), names)
    fsdp = ("x", "zh", "y", "core")
    in_specs = (P(names, None), P(names, None), P(fsdp, None), P(fsdp, None), P(fsdp, None), P("zl", fsdp, None))
    out_specs = (P(names, None), P(fsdp, None), P(fsdp, None))
    return jax.shard_map(relay, mesh=fine, in_specs=in_specs, out_specs=out_specs, check_vma=False)
```

time: 569 us -> 196 us (0.34)
  waiting for transfers between devices: 325 us -> 89.7 us
  blocking collectives: 190 us -> 26.1 us
  starting transfers between devices: 22.6 us -> 58.7 us
  between operations: 14.2 us -> 0.94 us
  local copies, waits for them, and re-layouts: 1.48 us -> 8.88 us
    all_gather x2 -> x0, blocking collectives: 190 us -> none  [the longest x1 153 us: relay(): lax.all_gather(codes, 'cuts', axis=0, tiled=True)]
    all_gather x1 -> x0, waiting for transfers between devices: 154 us -> none  [relay(): lax.all_gather(new_weights, 'fsdp', axis=0, tiled=True)]
    all_to_all x1 -> x3, waiting for transfers between devices: 170 us -> 73.6 us  [the longest x1 40.2 us: relay(): lax.all_to_all(pieces, ('x', 'y'), split_axis=0, concat_axis=0, tiled=True)]
    ppermute x0 -> x4, starting transfers between devices: none -> 31.9 us  [the longest x1 12 us: relay(): far = lax.ppermute(states, 'zh', swap)]
    all_to_all x0 -> x1, blocking collectives: none -> 26.1 us  [relay(): lax.all_to_all(packed, 'zl', split_axis=0, concat_axis=0, tiled=True)]
    ppermute x0 -> x4, waiting for transfers between devices: none -> 16.1 us  [the longest x1 15.2 us: relay(): far = lax.ppermute(states, 'zh', swap)]
    all_to_all x1 -> x3, starting transfers between devices: 22.5 us -> 26.7 us  [the longest x1 11.7 us: relay(): lax.all_to_all(sent, ('x', 'y'), split_axis=0, concat_axis=0, tiled=True)]
  transfers between devices with their start and end apart: 2 -> 7, of which waited for: 2 -> 5; matrix products, arithmetic and copies ran while one was open for 0% -> 5% of each run, Pallas kernels for 0% -> 0%
where the time goes in v1:
time: 196 us; the launch traced here: 194 us
  waiting for transfers between devices  89.7 us (46%)
  starting transfers between devices  58.7 us (30%)
  blocking collectives  26.1 us (13%)
  local copies, waits for them, and re-layouts  8.88 us (5%)
  matrix products  4.99 us (3%)
  other arithmetic  4.63 us (2%)
    all_to_all x1, waiting for transfers between devices, relay(): lax.all_to_all(pieces, ('x', 'y'), split_axis=0, concat_axis=0, tiled=True)  40.2 us
    all_to_all x1, waiting for transfers between devices, relay(): lax.all_to_all(sent, ('x', 'y'), split_axis=0, concat_axis=0, tiled=True)  33.3 us
    all_to_all x1, blocking collectives, relay(): lax.all_to_all(packed, 'zl', split_axis=0, concat_axis=0, tiled=True)  26.1 us
    ppermute x1, waiting for transfers between devices, relay(): far = lax.ppermute(states, 'zh', swap)  15.2 us
    ppermute x1, starting transfers between devices, relay(): far = lax.ppermute(states, 'zh', swap)  12 us
    all_to_all x1, starting transfers between devices, relay(): lax.all_to_all(sent, ('x', 'y'), split_axis=0, concat_axis=0, tiled=True)  11.7 us
    all_to_all x1, starting transfers between devices, relay(): lax.all_to_all(part, ('zl', 'zh'), split_axis=0, concat_axis=0, tiled=True)  11.3 us
    ppermute x1, starting transfers between devices, relay(): other_out = lax.ppermute(project(other_act).astype(BF16), 'core', swap)  9.13 us
  transfers between devices with their start and end apart: 7, of which 5 were waited for; matrix products, arithmetic and copies ran while one was open for 5% of the time, Pallas kernels for 0%

profile of v1, /device:TPU:1, one launch (start us, length us, event | category | flops | bytes accessed | tf_op | source)
XLA Modules:
  0.0 193.9 jit_solution(460144466789419715)
XLA Ops:
  0.6 0.0 copy-start.5
  0.6 8.9 %collective-permute-start.2 = (bf16[160,2048]{1,0:T(8,128)(2,1)}, bf16[160,2048]{1,0:T(8,128)(2,1)S(1)}, u32[]{:S(2)}, u32[]{:S(2)}) collective-permute-start(bf16[160,2048]{1,0:T(8,128)(2,1)} %param.7), channel_id=1, source_target_pairs={{0,1},{1,0},{2,3},{3,2},{4,5},{5,4},{6,7},{7,6},{8,9},{9,8},{10,11... | collective-permute-start | bytes 1966088 | tf_op jit(solution)/shard_map/ppermute | solution.py:34
  9.6 1.3 copy.25
  10.9 0.1 copy.26
  10.9 0.0 copy-start
  11.0 1.9 collective-permute-start.1
  12.9 0.0 copy-done.5
  12.9 1.0 fusion.4
  13.9 0.0 copy-done
  13.9 0.7 collective-permute-done.1
  14.6 0.0 collective-permute-done.2
  14.6 2.6 %add_convert_fusion = bf16[768,2048]{1,0:T(8,128)(2,1)} fusion(f32[768,2048]{1,0:T(8,128)S(1)} %fusion.4, bf16[768,160]{1,0:T(8,128)(2,1)S(1)} %collective-permute-done.1, bf16[160,2048]{1,0:T(8,128)(2,1)S(1)} %collective-permute-done.2), kind=kOutput, calls=%fused_computation.1 | convolution fusion | flops 506462208 | bytes 10338304 | tf_op jit(solution)/shard_map/dot_general | solution.py:45
  17.2 3.7 %all-to-all-start = ((bf16[16,48,2048]{2,1,0:T(8,128)(2,1)}), bf16[16,48,2048]{2,1,0:T(8,128)(2,1)S(1)}, u32[]{:S(2)}, u32[]{:S(2)}) async-start(bf16[16,48,2048]{2,1,0:T(8,128)(2,1)} %bitcast.74), calls=%async_computation | async-start | bytes 6291456 | tf_op jit(solution)/shard_map/all_to_all | solution.py:47
  21.0 0.1 broadcast_in_dim.51
  21.1 0.1 broadcast_in_dim.52
  21.1 1.0 broadcast_in_dim.55
  22.1 0.9 copy.33
  23.0 40.2 %all-to-all-done = bf16[16,48,2048]{2,1,0:T(8,128)(2,1)S(1)} async-done(((bf16[16,48,2048]{2,1,0:T(8,128)(2,1)}), bf16[16,48,2048]{2,1,0:T(8,128)(2,1)S(1)}, u32[]{:S(2)}, u32[]{:S(2)}) %all-to-all-start) | async-done | bytes 3145760 | tf_op jit(solution)/shard_map/all_to_all | solution.py:47
  63.2 0.0 copy-start.2
  63.2 0.6 convert_reduce_fusion
  63.8 0.1 copy.32
  63.9 0.3 copy-done.2
  64.2 0.1 fusion.1
  64.4 0.8 broadcast_in_dim.58
  65.2 11.3 %all-to-all-start.1 = ((bf16[16,48,256]{2,1,0:T(8,128)(2,1)}), bf16[16,48,256]{2,1,0:T(8,128)(2,1)S(1)}, u32[]{:S(2)}, u32[]{:S(2)}) async-start(bf16[16,48,256]{2,1,0:T(8,128)(2,1)} %bitcast.16), calls=%async_computation.1 | async-start | bytes 786432 | tf_op jit(solution)/shard_map/all_to_all | solution.py:54
  76.5 0.7 bitcast_convert_fusion
  77.2 0.8 dynamic-slice_bitcast_fusion.1
  77.9 12.0 %collective-permute-start = (f32[3,24,256]{2,1,0:T(8,128)S(1)}, f32[3,24,256]{2,1,0:T(8,128)S(1)}, u32[]{:S(2)}, u32[]{:S(2)}) collective-permute-start(f32[3,24,256]{2,1,0:T(8,128)S(1)} %pad_maximum_fusion), channel_id=1, source_target_pairs={{0,8},{8,0},{1,9},{9,1},{2,10},{10,2},{3,11},{11,3},{4,12},{12,4},... | collective-permute-start | bytes 221192 | tf_op jit(solution)/shard_map/ppermute | solution.py:40
  89.9 15.2 %collective-permute-done = f32[3,24,256]{2,1,0:T(8,128)S(1)} collective-permute-done((f32[3,24,256]{2,1,0:T(8,128)S(1)}, f32[3,24,256]{2,1,0:T(8,128)S(1)}, u32[]{:S(2)}, u32[]{:S(2)}) %collective-permute-start) | collective-permute-done | bytes 73760 | tf_op jit(solution)/shard_map/ppermute | solution.py:40
  105.2 0.0 all-to-all-done.1
  105.2 0.1 convert_reduce_fusion.1
  105.3 0.1 abs_reduce_fusion
  105.4 0.1 multiply_reduce_fusion
  105.7 26.1 %all_to_all.20 = bf16[8,96,256]{2,1,0:T(8,128)(2,1)S(1)} all-to-all(bf16[8,96,256]{2,1,0:T(8,128)(2,1)S(1)} %broadcast_in_dim.59), channel_id=1, replica_groups=mesh['zl'=8,'x'=4,'zh'=2,'y'=4,'core'=2] {'zl'}, dimensions={0} | all-to-all | bytes 786432 | tf_op jit(solution)/shard_map/all_to_all | solution.py:67
  131.8 0.0 copy-start.3
  131.8 0.7 copy-done.3
  132.5 2.0 %broadcast_in_dim.61 = bf16[16,48,2048]{2,1,0:T(8,128)(2,1)} broadcast(bf16[48,2048]{1,0:T(8,128)(2,1)S(1)} %bitcast.84), dimensions={1,2} | broadcast | bytes 3342336 | tf_op jit(solution)/shard_map/broadcast_in_dim | solution.py:72
  134.6 11.7 %all-to-all-start.3 = ((bf16[16,48,2048]{2,1,0:T(8,128)(2,1)}), bf16[16,48,2048]{2,1,0:T(8,128)(2,1)S(1)}, u32[]{:S(2)}, u32[]{:S(2)}) async-start(bf16[16,48,2048]{2,1,0:T(8,128)(2,1)} %broadcast_in_dim.61), calls=%async_computation.3 | async-start | bytes 6291456 | tf_op jit(solution)/shard_map/all_to_all | solution.py:73
  146.3 1.0 add_bitcast_fusion
  147.3 0.7 copy.31
  148.0 33.3 %all-to-all-done.3 = bf16[16,48,2048]{2,1,0:T(8,128)(2,1)S(1)} async-done(((bf16[16,48,2048]{2,1,0:T(8,128)(2,1)}), bf16[16,48,2048]{2,1,0:T(8,128)(2,1)S(1)}, u32[]{:S(2)}, u32[]{:S(2)}) %all-to-all-start.3) | async-done | bytes 3145760 | tf_op jit(solution)/shard_map/all_to_all | solution.py:73
  181.3 0.0 copy-start.4
  181.3 0.0 copy-start.6
  181.3 0.0 copy-start.7
  181.3 0.0 copy-start.1
  181.3 0.7 convolution_convert_fusion
  182.0 9.1 %collective-permute-start.3 = (bf16[160,2048]{1,0:T(8,128)(2,1)S(1)}, bf16[160,2048]{1,0:T(8,128)(2,1)S(1)}, u32[]{:S(2)}, u32[]{:S(2)}) collective-permute-start(bf16[160,2048]{1,0:T(8,128)(2,1)S(1)} %convolution_convert_fusion), channel_id=1, source_target_pairs={{0,1},{1,0},{2,3},{3,2},{4,5},{5,4},{6,7},{7,6},{8,9},{9,8},{10,11... | collective-permute-start | bytes 1966088 | tf_op jit(solution)/shard_map/ppermute | solution.py:81
  191.2 0.0 copy-done.4
  191.2 0.0 copy-done.6
  191.2 0.0 copy-done.7
  191.2 0.8 fusion.8
  192.0 0.0 copy-done.1
  192.0 0.7 fusion.2
  192.7 0.1 collective-permute-done.3
  192.9 1.0 add_convert_fusion.1
  (13 shorter events, 0.2 us)
Async XLA Ops:
  0.6 12.3 %copy-start.5 = (bf16[160,2048]{1,0:T(8,128)(2,1)S(1)}, bf16[160,2048]{1,0:T(8,128)(2,1)}, u32[]{:S(2)}) copy-start(bf16[160,2048]{1,0:T(8,128)(2,1)} %param.7) | copy-start | bytes 1966084
  0.6 14.0 %collective-permute-start.2 = (bf16[160,2048]{1,0:T(8,128)(2,1)}, bf16[160,2048]{1,0:T(8,128)(2,1)S(1)}, u32[]{:S(2)}, u32[]{:S(2)}) collective-permute-start(bf16[160,2048]{1,0:T(8,128)(2,1)} %param.7), channel_id=1, source_target_pairs={{0,1},{1,0},{2,3},{3,2},{4,5},{5,4},{6,7},{7,6},{8,9},{9,8},{10,11... | collective-permute-start | bytes 1966088 | tf_op jit(solution)/shard_map/ppermute | solution.py:34
  10.9 3.0 %copy-start = (bf16[2,4,4,2,24,160]{5,4,3,2,1,0:T(8,128)(2,1)}, bf16[2,4,4,2,24,160]{5,4,3,2,1,0:T(8,128)(2,1)S(1)}, u32[]{:S(2)}) copy-start(bf16[2,4,4,2,24,160]{5,4,3,2,1,0:T(8,128)(2,1)S(1)} %copy.26) | copy-start | bytes 1474564
  11.0 3.6 %collective-permute-start.1 = (bf16[768,160]{1,0:T(8,128)(2,1)S(1)}, bf16[768,160]{1,0:T(8,128)(2,1)S(1)}, u32[]{:S(2)}, u32[]{:S(2)}) collective-permute-start(bf16[768,160]{1,0:T(8,128)(2,1)S(1)} %dynamic-slice_bitcast_fusion), channel_id=1, source_target_pairs={{0,1},{1,0},{2,3},{3,2},{4,5},{5,4},{6,7},{7,6},{8,9},{9,8},{10,11... | collective-permute-start | bytes 737288 | tf_op jit(solution)/shard_map/ppermute | solution.py:33
  17.2 46.0 %all-to-all-start = ((bf16[16,48,2048]{2,1,0:T(8,128)(2,1)}), bf16[16,48,2048]{2,1,0:T(8,128)(2,1)S(1)}, u32[]{:S(2)}, u32[]{:S(2)}) async-start(bf16[16,48,2048]{2,1,0:T(8,128)(2,1)} %bitcast.74), calls=%async_computation | async-start | bytes 6291456 | tf_op jit(solution)/shard_map/all_to_all | solution.py:47
  63.2 1.0 copy-start.2
  65.2 40.1 %all-to-all-start.1 = ((bf16[16,48,256]{2,1,0:T(8,128)(2,1)}), bf16[16,48,256]{2,1,0:T(8,128)(2,1)S(1)}, u32[]{:S(2)}, u32[]{:S(2)}) async-start(bf16[16,48,256]{2,1,0:T(8,128)(2,1)} %bitcast.16), calls=%async_computation.1 | async-start | bytes 786432 | tf_op jit(solution)/shard_map/all_to_all | solution.py:54
  77.9 27.2 %collective-permute-start = (f32[3,24,256]{2,1,0:T(8,128)S(1)}, f32[3,24,256]{2,1,0:T(8,128)S(1)}, u32[]{:S(2)}, u32[]{:S(2)}) collective-permute-start(f32[3,24,256]{2,1,0:T(8,128)S(1)} %pad_maximum_fusion), channel_id=1, source_target_pairs={{0,8},{8,0},{1,9},{9,1},{2,10},{10,2},{3,11},{11,3},{4,12},{12,4},... | collective-permute-start | bytes 221192 | tf_op jit(solution)/shard_map/ppermute | solution.py:40
  131.8 0.7 copy-start.3
  134.6 46.7 %all-to-all-start.3 = ((bf16[16,48,2048]{2,1,0:T(8,128)(2,1)}), bf16[16,48,2048]{2,1,0:T(8,128)(2,1)S(1)}, u32[]{:S(2)}, u32[]{:S(2)}) async-start(bf16[16,48,2048]{2,1,0:T(8,128)(2,1)} %broadcast_in_dim.61), calls=%async_computation.3 | async-start | bytes 6291456 | tf_op jit(solution)/shard_map/all_to_all | solution.py:73
  181.3 9.9 %copy-start.4 = (f32[8,3,8,256]{3,2,0,1:T(8,128)S(1)}, f32[8,3,8,256]{3,2,0,1:T(8,128)}, u32[]{:S(2)}) copy-start(f32[8,3,8,256]{3,2,0,1:T(8,128)} %copy.31) | copy-start | bytes 589828
  181.3 9.9 %copy-start.6 = (f32[24,2048]{1,0:T(8,128)S(1)}, f32[24,2048]{1,0:T(8,128)}, u32[]{:S(2)}) copy-start(f32[24,2048]{1,0:T(8,128)} %param.10) | copy-start | bytes 589828
  181.3 9.9 %copy-start.7 = (f32[24,2048]{1,0:T(8,128)S(1)}, f32[24,2048]{1,0:T(8,128)}, u32[]{:S(2)}) copy-start(f32[24,2048]{1,0:T(8,128)} %param.9) | copy-start | bytes 589828
  181.3 10.7 %copy-start.1 = (bf16[2,4,4,2,24,160]{5,4,3,2,1,0:T(8,128)(2,1)S(1)}, bf16[2,4,4,2,24,160]{5,4,3,2,1,0:T(8,128)(2,1)}, u32[]{:S(2)}) copy-start(bf16[2,4,4,2,24,160]{5,4,3,2,1,0:T(8,128)(2,1)} %copy-done) | copy-start | bytes 1474564
  182.0 10.8 %collective-permute-start.3 = (bf16[160,2048]{1,0:T(8,128)(2,1)S(1)}, bf16[160,2048]{1,0:T(8,128)(2,1)S(1)}, u32[]{:S(2)}, u32[]{:S(2)}) collective-permute-start(bf16[160,2048]{1,0:T(8,128)(2,1)S(1)} %convolution_convert_fusion), channel_id=1, source_target_pairs={{0,1},{1,0},{2,3},{3,2},{4,5},{5,4},{6,7},{7,6},{8,9},{9,8},{10,11... | collective-permute-start | bytes 1966088 | tf_op jit(solution)/shard_map/ppermute | solution.py:81

commit v2 on v1

v2 whole, which is shorter than its diff:
```python
import jax
import jax.numpy as jnp
from jax import lax
from jax.sharding import Mesh, PartitionSpec as P

HEAD_SIZE = 256
BF16 = jnp.bfloat16
F32 = jnp.float32


def update_of(grad, first, second, weight):
    new_first = 0.9 * first + 0.1 * grad
    new_second = 0.95 * second + 0.05 * grad * grad
    update = new_first / (1.0 - 0.9**10) / (jnp.sqrt(new_second / (1.0 - 0.95**10)) + 1e-08)
    new_weight = weight.astype(F32) * (1.0 - 0.002 * 0.1) - 0.002 * update
    return new_first, new_second, new_weight.astype(BF16)


def exchange(pieces, axes):
    return lax.all_to_all(pieces, axes, split_axis=0, concat_axis=0, tiled=True)


def relay(act, cot, weight, first, second, residue):
    nx, ny, nz, nzh = (lax.axis_size(a) for a in ("x", "y", "zl", "zh"))
    core, zh, zl = (lax.axis_index(a) for a in ("core", "zh", "zl"))
    tok, width = cot.shape
    depth = act.shape[1]
    own = weight.shape[0]
    per = width // nz
    rows = nzh * own
    swap = [(0, 1), (1, 0)]

    all_act = lax.all_gather(act, ("y", "core"), axis=0, tiled=True)

    turned = act.T.reshape(nx, nzh, ny, 2, own, tok).transpose(3, 0, 2, 1, 4, 5)
    turned = turned.reshape(2, nx * ny * rows, tok)
    mine = lax.dynamic_index_in_dim(turned, core, 0, keepdims=False)
    other = lax.dynamic_index_in_dim(turned, 1 - core, 0, keepdims=False)
    other_act = lax.ppermute(other, "core", swap)
    other_cot = lax.ppermute(cot, "core", swap)

    def columns(a):
        return lax.dynamic_slice_in_dim(a, zl * per, per, 1)

    states = jnp.stack([columns(first), columns(second), columns(weight).astype(F32)])
    far = lax.ppermute(states, "zh", swap)

    term = jnp.dot(mine, cot, preferred_element_type=F32)
    term = term + jnp.dot(other_act, other_cot, preferred_element_type=F32)
    pieces = term.astype(BF16).reshape(nx, ny * rows, width)
    arrived = exchange(pieces, "x")
    arrived, far = lax.optimization_barrier((arrived, far))
    part = jnp.sum(arrived, axis=0, dtype=F32).astype(BF16).reshape(ny, rows, width)
    arrived = exchange(part, "y")
    part = jnp.sum(arrived, axis=0, dtype=F32).reshape(nzh, own, width)
    here = (jnp.arange(nzh) == zh)[:, None, None]
    part = part + jnp.where(here, residue, 0.0)

    part = part.astype(BF16).reshape(rows, nz, per).transpose(1, 0, 2)
    part = jnp.broadcast_to(part[:, None], (nz, nzh, rows, per)).reshape(nz * nzh, rows, per)
    parts = exchange(part, ("zl", "zh"))
    combined = jnp.sum(parts.reshape(nz, nzh, rows, per), axis=1, dtype=F32)
    blocks = combined.reshape(nz, rows, per // HEAD_SIZE, HEAD_SIZE)
    scale = (jnp.max(jnp.abs(blocks), axis=-1) + 1e-06).astype(BF16).astype(F32)
    codes = (blocks / scale[..., None]).astype(BF16)
    grad = jnp.sum(codes.astype(F32) * scale[..., None], axis=0).reshape(rows, per)
    both = jnp.stack([jnp.where(zh == 0, states, far), jnp.where(zh == 0, far, states)], axis=1)
    both = both.reshape(3, rows, per)
    _, _, new_part = update_of(grad, both[0], both[1], both[2])

    own_grad = lax.dynamic_slice_in_dim(grad, zh * own, own, 0)
    high = lax.reduce_precision(own_grad, 8, 7)
    low = (own_grad - high).astype(BF16)
    packed = jnp.concatenate([new_part, high.astype(BF16), low], axis=0)
    packed = exchange(jnp.broadcast_to(packed[None], (nz,) + packed.shape), "zl")
    full_grad = packed[:, rows : rows + own].astype(F32) + packed[:, rows + own :].astype(F32)
    full_grad = full_grad.transpose(1, 0, 2).reshape(own, width)
    new_first, new_second, _ = update_of(full_grad, first, second, weight)

    sent = jnp.broadcast_to(packed[None, :, :rows], (nx, nz, rows, per))
    got = exchange(sent.reshape(nx * nz, rows, per), ("x", "y", "core"))
    head = got.reshape(nx, nz, nzh, own, per).transpose(0, 2, 1, 3, 4).reshape(depth, per)
    out = jnp.dot(all_act, head, preferred_element_type=F32).astype(BF16)
    back = exchange(out.reshape(nz, tok, per), ("y", "core"))
    projected = back.transpose(1, 0, 2).reshape(tok, width)
    return projected, new_first, new_second


def solution(mesh):
    names = ("zl", "x", "zh", "y", "core")
    fine = Mesh(mesh.devices.reshape(8, 4, 2, 4, 2), names)
    fsdp = ("x", "zh", "y", "core")
    by_token, by_row = P(names, None), P(fsdp, None)
    in_specs = (by_token, by_token, by_row, by_row, by_row, P("zl", fsdp, None))
    out_specs = (by_token, by_row, by_row)
    return jax.shard_map(relay, mesh=fine, in_specs=in_specs, out_specs=out_specs, check_vma=False)
```

time: 196 us -> 191 us (0.974)
  blocking collectives: 26.1 us -> 50.7 us
  waiting for transfers between devices: 89.7 us -> 65.5 us
  starting transfers between devices: 58.7 us -> 41.8 us
  between operations: 0.94 us -> 14.4 us
  local copies, waits for them, and re-layouts: 8.88 us -> 5.78 us
  matrix products: 4.99 us -> 6.97 us
    all_to_all x1 -> x2, blocking collectives: 26.1 us -> 50.7 us  [exchange(): return lax.all_to_all(pieces, axes, split_axis=0, concat_axis=0, tiled=True)]
    all_to_all x3 -> x4, waiting for transfers between devices: 73.6 us -> 60.1 us  [exchange(): return lax.all_to_all(pieces, axes, split_axis=0, concat_axis=0, tiled=True)]
    ppermute x1, waiting for transfers between devices: 15.2 us -> 4.05 us  [relay(): far = lax.ppermute(states, 'zh', swap)]
    ppermute x1 -> x0, starting transfers between devices: 9.13 us -> none  [relay(): other_out = lax.ppermute(project(other_act).astype(BF16), 'core', swap)]
    all_to_all x3 -> x4, starting transfers between devices: 26.7 us -> 20.6 us  [exchange(): return lax.all_to_all(pieces, axes, split_axis=0, concat_axis=0, tiled=True)]
    broadcast_in_dim x3 -> x2, local copies, waits for them, and re-layouts: 2.06 us -> 0.08 us  [the longest x1 0.05 us: relay(): sent = jnp.broadcast_to(packed[None, :, :rows], (nx, nz, rows, per))]
  transfers between devices with their start and end apart: 7 -> 8, of which waited for: 5 -> 6; matrix products, arithmetic and copies ran while one was open for 5% -> 5% of each run, Pallas kernels for 0% -> 0%
where the time goes in v2:
time: 191 us; the launch traced here: 190 us
  waiting for transfers between devices  65.5 us (34%)
  blocking collectives  50.7 us (27%)
  starting transfers between devices  41.8 us (22%)
  between operations  14.4 us (8%)
  matrix products  6.97 us (4%)
  local copies, waits for them, and re-layouts  5.78 us (3%)
  other arithmetic  4.78 us (3%)
    all_to_all x4, waiting for transfers between devices, exchange(): return lax.all_to_all(pieces, axes, split_axis=0, concat_axis=0, tiled=True)  60.1 us
    all_to_all x2, blocking collectives, exchange(): return lax.all_to_all(pieces, axes, split_axis=0, concat_axis=0, tiled=True)  50.7 us
    all_to_all x4, starting transfers between devices, exchange(): return lax.all_to_all(pieces, axes, split_axis=0, concat_axis=0, tiled=True)  20.6 us
    ppermute x1, starting transfers between devices, relay(): far = lax.ppermute(states, 'zh', swap)  10.4 us
    ppermute x1, starting transfers between devices, relay(): other_cot = lax.ppermute(cot, 'core', swap)  8.92 us
    ppermute x1, waiting for transfers between devices, relay(): far = lax.ppermute(states, 'zh', swap)  4.05 us
  transfers between devices with their start and end apart: 8, of which 6 were waited for; matrix products, arithmetic and copies ran while one was open for 5% of the time, Pallas kernels for 0%

profile of v2, /device:TPU:1, one launch (start us, length us, event | category | flops | bytes accessed | tf_op | source)
XLA Modules:
  0.0 190.0 jit_solution(18128804856720256505)
XLA Ops:
  7.2 0.0 copy-start
  7.2 8.9 %collective-permute-start.1 = (bf16[160,2048]{1,0:T(8,128)(2,1)}, bf16[160,2048]{1,0:T(8,128)(2,1)S(1)}, u32[]{:S(2)}, u32[]{:S(2)}) collective-permute-start(bf16[160,2048]{1,0:T(8,128)(2,1)} %param.7), channel_id=1, source_target_pairs={{0,1},{1,0},{2,3},{3,2},{4,5},{5,4},{6,7},{7,6},{8,9},{9,8},{10,11... | collective-permute-start | bytes 1966088 | tf_op jit(solution)/shard_map/ppermute | solution.py:40
  16.1 1.3 copy.37
  17.4 0.1 copy.38
  17.5 1.9 %collective-permute-start = (bf16[768,160]{1,0:T(8,128)(2,1)S(1)}, bf16[768,160]{1,0:T(8,128)(2,1)S(1)}, u32[]{:S(2)}, u32[]{:S(2)}) collective-permute-start(bf16[768,160]{1,0:T(8,128)(2,1)S(1)} %dynamic-slice_bitcast_fusion), channel_id=1, source_target_pairs={{0,1},{1,0},{2,3},{3,2},{4,5},{5,4},{6,7},{7,6},{8,9},{9,8},{10,11... | collective-permute-start | bytes 737288 | tf_op jit(solution)/shard_map/ppermute | solution.py:39
  19.5 0.0 copy-done
  19.5 1.0 fusion.3
  20.4 0.7 collective-permute-done
  21.1 0.0 collective-permute-done.1
  21.1 2.6 %add_convert_fusion = bf16[768,2048]{1,0:T(8,128)(2,1)} fusion(f32[768,2048]{1,0:T(8,128)S(1)} %fusion.3, bf16[768,160]{1,0:T(8,128)(2,1)S(1)} %collective-permute-done, bf16[160,2048]{1,0:T(8,128)(2,1)S(1)} %collective-permute-done.1), kind=kOutput, calls=%fused_computation | convolution fusion | flops 506462208 | bytes 10338304 | tf_op jit(solution)/shard_map/dot_general | solution.py:49
  23.8 0.0 copy-start.1
  23.8 0.0 copy-start.2
  23.8 3.8 %all-to-all-start = ((bf16[4,192,2048]{2,1,0:T(8,128)(2,1)}), bf16[4,192,2048]{2,1,0:T(8,128)(2,1)S(1)}, u32[]{:S(2)}, u32[]{:S(2)}) async-start(bf16[4,192,2048]{2,1,0:T(8,128)(2,1)} %bitcast.77), calls=%async_computation | async-start | bytes 6291456 | tf_op jit(solution)/shard_map/all_to_all | solution.py:20
  27.6 0.0 all-gather.2.cloned.1.call-start
  27.7 0.7 all-gather.2.cloned.1.call-update
  28.4 0.7 bitcast_convert_fusion
  29.1 0.0 copy-done.1
  29.1 0.0 copy-done.2
  29.1 0.0 copy-start.3
  29.1 0.0 copy-start.5
  29.1 0.0 copy-start.7
  29.2 10.4 %collective-permute-start.2 = (f32[3,24,256]{2,1,0:T(8,128)S(1)}, f32[3,24,256]{2,1,0:T(8,128)}, u32[]{:S(2)}, u32[]{:S(2)}) collective-permute-start(f32[3,24,256]{2,1,0:T(8,128)S(1)} %pad_maximum_fusion), channel_id=1, source_target_pairs={{0,8},{8,0},{1,9},{9,1},{2,10},{10,2},{3,11},{11,3},{4,12},{12,4},... | collective-permute-start | bytes 221192 | tf_op jit(solution)/shard_map/ppermute | solution.py:46
  39.5 0.0 copy-done.3
  39.5 0.0 copy-done.5
  39.6 0.0 copy-done.7
  39.6 4.1 %collective-permute-done.2 = f32[3,24,256]{2,1,0:T(8,128)} collective-permute-done((f32[3,24,256]{2,1,0:T(8,128)S(1)}, f32[3,24,256]{2,1,0:T(8,128)}, u32[]{:S(2)}, u32[]{:S(2)}) %collective-permute-start.2) | collective-permute-done | bytes 73760 | tf_op jit(solution)/shard_map/ppermute | solution.py:46
  43.6 21.6 %all-to-all-done = bf16[4,192,2048]{2,1,0:T(8,128)(2,1)S(1)} async-done(((bf16[4,192,2048]{2,1,0:T(8,128)(2,1)}), bf16[4,192,2048]{2,1,0:T(8,128)(2,1)S(1)}, u32[]{:S(2)}, u32[]{:S(2)}) %all-to-all-start) | async-done | bytes 3145760 | tf_op jit(solution)/shard_map/all_to_all | solution.py:20
  65.2 1.7 reduce_sum.39
  66.8 0.0 copy-start.4
  66.8 0.0 copy-start.6
  66.8 0.0 copy-start.8
  66.9 3.6 %all-to-all-start.1 = ((bf16[4,48,2048]{2,1,0:T(8,128)(2,1)}), bf16[4,48,2048]{2,1,0:T(8,128)(2,1)S(1)}, u32[]{:S(2)}, u32[]{:S(2)}) async-start(bf16[4,48,2048]{2,1,0:T(8,128)(2,1)} %bitcast.82), calls=%async_computation.1 | async-start | bytes 1572864 | tf_op jit(solution)/shard_map/all_to_all | solution.py:20
  70.5 0.1 broadcast_in_dim.49
  70.6 0.1 broadcast_in_dim.50
  70.7 1.0 broadcast_in_dim.53
  71.6 0.1 copy.47
  71.8 10.1 %all-to-all-done.1 = bf16[4,48,2048]{2,1,0:T(8,128)(2,1)S(1)} async-done(((bf16[4,48,2048]{2,1,0:T(8,128)(2,1)}), bf16[4,48,2048]{2,1,0:T(8,128)(2,1)S(1)}, u32[]{:S(2)}, u32[]{:S(2)}) %all-to-all-start.1) | async-done | bytes 786464 | tf_op jit(solution)/shard_map/all_to_all | solution.py:20
  81.8 0.1 convert_reduce_fusion
  82.0 0.1 copy.46
  82.1 0.1 fusion.2
  82.3 0.8 broadcast_in_dim.56
  83.0 9.7 %all-to-all-start.2 = ((bf16[16,48,256]{2,1,0:T(8,128)(2,1)}), bf16[16,48,256]{2,1,0:T(8,128)(2,1)S(1)}, u32[]{:S(2)}, u32[]{:S(2)}) async-start(bf16[16,48,256]{2,1,0:T(8,128)(2,1)} %bitcast.17), calls=%async_computation.2 | async-start | bytes 786432 | tf_op jit(solution)/shard_map/all_to_all | solution.py:20
  92.7 0.0 copy-done.4
  92.7 0.0 copy-done.6
  92.7 0.0 copy-done.8
  92.7 0.9 select_bitcast_fusion.1
  93.7 18.6 %all-to-all-done.2 = bf16[16,48,256]{2,1,0:T(8,128)(2,1)S(1)} async-done(((bf16[16,48,256]{2,1,0:T(8,128)(2,1)}), bf16[16,48,256]{2,1,0:T(8,128)(2,1)S(1)}, u32[]{:S(2)}, u32[]{:S(2)}) %all-to-all-start.2) | async-done | bytes 393248 | tf_op jit(solution)/shard_map/all_to_all | solution.py:20
  112.3 0.1 convert_reduce_fusion.1
  112.3 0.1 abs_reduce_fusion
  112.5 0.1 multiply_reduce_fusion
  112.7 28.6 %all_to_all.30 = bf16[8,96,256]{2,1,0:T(8,128)(2,1)S(1)} all-to-all(bf16[8,96,256]{2,1,0:T(8,128)(2,1)S(1)} %broadcast_in_dim.57), channel_id=1, replica_groups=mesh['zl'=8,'x'=4,'zh'=2,'y'=4,'core'=2] {'zl'}, dimensions={0} | all-to-all | bytes 786432 | tf_op jit(solution)/shard_map/all_to_all | solution.py:20
  141.4 0.1 broadcast_in_dim.58
  141.4 22.1 %all_to_all.31 = bf16[32,48,256]{2,1,0:T(8,128)(2,1)S(1)} all-to-all(bf16[32,48,256]{2,1,0:T(8,128)(2,1)S(1)} %bitcast.83), channel_id=1, replica_groups=mesh['zl'=8,'x'=4,'zh'=2,'y'=4,'core'=2] {'x','y','core'}, dimensions={0} | all-to-all | bytes 1572864 | tf_op jit(solution)/shard_map/all_to_all | solution.py:20
  163.5 0.1 copy.40
  163.5 0.0 all-gather.2.cloned.1.call-done
  163.6 3.3 %fusion = bf16[1280,256]{0,1:T(8,128)(2,1)S(1)} fusion(bf16[1536,256]{1,0:T(8,128)(2,1)S(1)} %bitcast.88, bf16[1280,1536]{1,0:T(8,128)(2,1)} %all-gather.2.cloned.1.call-done), kind=kOutput, calls=%fused_computation.2 | convolution fusion | flops 1006960640 | bytes 5373952 | tf_op jit(solution)/shard_map/dot_general | solution.py:83
  166.9 1.1 copy.41
  168.0 3.5 %all-to-all-start.5 = ((bf16[8,160,256]{2,1,0:T(8,128)(2,1)}), bf16[8,160,256]{2,1,0:T(8,128)(2,1)S(1)}, u32[]{:S(2)}, u32[]{:S(2)}) async-start(bf16[8,160,256]{2,1,0:T(8,128)(2,1)} %bitcast.25), calls=%async_computation.5 | async-start | bytes 1310720 | tf_op jit(solution)/shard_map/all_to_all | solution.py:20
  171.6 0.8 fusion.6
  172.4 9.8 %all-to-all-done.5 = bf16[8,160,256]{2,1,0:T(8,128)(2,1)S(1)} async-done(((bf16[8,160,256]{2,1,0:T(8,128)(2,1)}), bf16[8,160,256]{2,1,0:T(8,128)(2,1)S(1)}, u32[]{:S(2)}, u32[]{:S(2)}) %all-to-all-start.5) | async-done | bytes 655392 | tf_op jit(solution)/shard_map/all_to_all | solution.py:20
  182.2 0.9 copy.44
  (14 shorter events, 0.3 us)
Async XLA Ops:
  7.2 12.3 %copy-start = (bf16[160,2048]{1,0:T(8,128)(2,1)S(1)}, bf16[160,2048]{1,0:T(8,128)(2,1)}, u32[]{:S(2)}) copy-start(bf16[160,2048]{1,0:T(8,128)(2,1)} %param.7) | copy-start | bytes 1966084
  7.2 14.0 %collective-permute-start.1 = (bf16[160,2048]{1,0:T(8,128)(2,1)}, bf16[160,2048]{1,0:T(8,128)(2,1)S(1)}, u32[]{:S(2)}, u32[]{:S(2)}) collective-permute-start(bf16[160,2048]{1,0:T(8,128)(2,1)} %param.7), channel_id=1, source_target_pairs={{0,1},{1,0},{2,3},{3,2},{4,5},{5,4},{6,7},{7,6},{8,9},{9,8},{10,11... | collective-permute-start | bytes 1966088 | tf_op jit(solution)/shard_map/ppermute | solution.py:40
  17.5 3.6 %collective-permute-start = (bf16[768,160]{1,0:T(8,128)(2,1)S(1)}, bf16[768,160]{1,0:T(8,128)(2,1)S(1)}, u32[]{:S(2)}, u32[]{:S(2)}) collective-permute-start(bf16[768,160]{1,0:T(8,128)(2,1)S(1)} %dynamic-slice_bitcast_fusion), channel_id=1, source_target_pairs={{0,1},{1,0},{2,3},{3,2},{4,5},{5,4},{6,7},{7,6},{8,9},{9,8},{10,11... | collective-permute-start | bytes 737288 | tf_op jit(solution)/shard_map/ppermute | solution.py:39
  23.8 5.3 %copy-start.1 = (f32[24,2048]{1,0:T(8,128)S(1)}, f32[24,2048]{1,0:T(8,128)}, u32[]{:S(2)}) copy-start(f32[24,2048]{1,0:T(8,128)} %param.10) | copy-start | bytes 589828
  23.8 5.3 %copy-start.2 = (f32[24,2048]{1,0:T(8,128)S(1)}, f32[24,2048]{1,0:T(8,128)}, u32[]{:S(2)}) copy-start(f32[24,2048]{1,0:T(8,128)} %param.9) | copy-start | bytes 589828
  23.8 41.4 %all-to-all-start = ((bf16[4,192,2048]{2,1,0:T(8,128)(2,1)}), bf16[4,192,2048]{2,1,0:T(8,128)(2,1)S(1)}, u32[]{:S(2)}, u32[]{:S(2)}) async-start(bf16[4,192,2048]{2,1,0:T(8,128)(2,1)} %bitcast.77), calls=%async_computation | async-start | bytes 6291456 | tf_op jit(solution)/shard_map/all_to_all | solution.py:20
  27.6 135.9 %all-gather.2.cloned.1.call-start = ((), (), s32[]{:S(2)}) async-start(), calls=%async_computation.6 | async-start | bytes 4423680 | tf_op jit(solution)/shard_map/all_gather | solution.py:33
  29.1 10.4 %copy-start.3 = (f32[1,24,256]{2,1,0:T(8,128)}, f32[1,24,256]{2,1,0:T(8,128)S(1)}, u32[]{:S(2)}) copy-start(f32[1,24,256]{2,1,0:T(8,128)S(1)} %bitcast_convert_fusion) | copy-start | bytes 73732
  29.1 10.4 %copy-start.5 = (f32[1,24,256]{2,1,0:T(8,128)}, f32[1,24,256]{2,1,0:T(8,128)S(1)}, u32[]{:S(2)}) copy-start(f32[1,24,256]{2,1,0:T(8,128)S(1)} %get-tuple-element.16) | copy-start | bytes 73732
  29.1 10.4 %copy-start.7 = (f32[1,24,256]{2,1,0:T(8,128)}, f32[1,24,256]{2,1,0:T(8,128)S(1)}, u32[]{:S(2)}) copy-start(f32[1,24,256]{2,1,0:T(8,128)S(1)} %get-tuple-element.17) | copy-start | bytes 73732
  29.2 14.4 %collective-permute-start.2 = (f32[3,24,256]{2,1,0:T(8,128)S(1)}, f32[3,24,256]{2,1,0:T(8,128)}, u32[]{:S(2)}, u32[]{:S(2)}) collective-permute-start(f32[3,24,256]{2,1,0:T(8,128)S(1)} %pad_maximum_fusion), channel_id=1, source_target_pairs={{0,8},{8,0},{1,9},{9,1},{2,10},{10,2},{3,11},{11,3},{4,12},{12,4},... | collective-permute-start | bytes 221192 | tf_op jit(solution)/shard_map/ppermute | solution.py:46
  66.8 25.9 %copy-start.4 = (f32[1,24,256]{2,1,0:T(8,128)S(1)}, f32[1,24,256]{2,1,0:T(8,128)}, u32[]{:S(2)}) copy-start(f32[1,24,256]{2,1,0:T(8,128)} %copy-done.3) | copy-start | bytes 73732
  66.8 25.9 %copy-start.6 = (f32[1,24,256]{2,1,0:T(8,128)S(1)}, f32[1,24,256]{2,1,0:T(8,128)}, u32[]{:S(2)}) copy-start(f32[1,24,256]{2,1,0:T(8,128)} %copy-done.5) | copy-start | bytes 73732
  66.8 25.9 %copy-start.8 = (f32[1,24,256]{2,1,0:T(8,128)S(1)}, f32[1,24,256]{2,1,0:T(8,128)}, u32[]{:S(2)}) copy-start(f32[1,24,256]{2,1,0:T(8,128)} %copy-done.7) | copy-start | bytes 73732
  66.9 15.0 %all-to-all-start.1 = ((bf16[4,48,2048]{2,1,0:T(8,128)(2,1)}), bf16[4,48,2048]{2,1,0:T(8,128)(2,1)S(1)}, u32[]{:S(2)}, u32[]{:S(2)}) async-start(bf16[4,48,2048]{2,1,0:T(8,128)(2,1)} %bitcast.82), calls=%async_computation.1 | async-start | bytes 1572864 | tf_op jit(solution)/shard_map/all_to_all | solution.py:20
  83.0 29.2 %all-to-all-start.2 = ((bf16[16,48,256]{2,1,0:T(8,128)(2,1)}), bf16[16,48,256]{2,1,0:T(8,128)(2,1)S(1)}, u32[]{:S(2)}, u32[]{:S(2)}) async-start(bf16[16,48,256]{2,1,0:T(8,128)(2,1)} %bitcast.17), calls=%async_computation.2 | async-start | bytes 786432 | tf_op jit(solution)/shard_map/all_to_all | solution.py:20
  168.0 14.2 %all-to-all-start.5 = ((bf16[8,160,256]{2,1,0:T(8,128)(2,1)}), bf16[8,160,256]{2,1,0:T(8,128)(2,1)S(1)}, u32[]{:S(2)}, u32[]{:S(2)}) async-start(bf16[8,160,256]{2,1,0:T(8,128)(2,1)} %bitcast.25), calls=%async_computation.5 | async-start | bytes 1310720 | tf_op jit(solution)/shard_map/all_to_all | solution.py:20
Sparse Core Ops, SparseCore 0:
  30.6 38.7 all-gather.1

commit v3 on v2

v3 whole, which is shorter than its diff:
```python
import jax
import jax.numpy as jnp
from jax import lax
from jax.sharding import Mesh, PartitionSpec as P

HEAD_SIZE = 256
BF16 = jnp.bfloat16
F32 = jnp.float32


def update_of(grad, first, second, weight):
    new_first = 0.9 * first + 0.1 * grad
    new_second = 0.95 * second + 0.05 * grad * grad
    update = new_first / (1.0 - 0.9**10) / (jnp.sqrt(new_second / (1.0 - 0.95**10)) + 1e-08)
    new_weight = weight.astype(F32) * (1.0 - 0.002 * 0.1) - 0.002 * update
    return new_first, new_second, new_weight.astype(BF16)


def exchange(pieces, axes):
    return lax.all_to_all(pieces, axes, split_axis=0, concat_axis=0, tiled=True)


def relay(act, cot, weight, first, second, residue):
    nx, ny, nz, nzh = (lax.axis_size(a) for a in ("x", "y", "zl", "zh"))
    core, y, zh, zl = (lax.axis_index(a) for a in ("core", "y", "zh", "zl"))
    tok, width = cot.shape
    depth = act.shape[1]
    own = weight.shape[0]
    per = width // nz
    rows = nzh * own
    swap = [(0, 1), (1, 0)]

    turned = act.T.reshape(nx, nzh, ny, 2, own, tok).transpose(3, 0, 2, 1, 4, 5)
    turned = turned.reshape(2, nx * ny * rows, tok)
    mine = lax.dynamic_index_in_dim(turned, core, 0, keepdims=False)
    other = lax.dynamic_index_in_dim(turned, 1 - core, 0, keepdims=False)
    other_act = lax.ppermute(other, "core", swap)
    other_cot = lax.ppermute(cot, "core", swap)

    term = jnp.dot(mine, cot, preferred_element_type=F32)
    term = term + jnp.dot(other_act, other_cot, preferred_element_type=F32)
    pieces = term.astype(BF16).reshape(nx, ny * rows, width)

    pieces, act = lax.optimization_barrier((pieces, act))
    arrived = exchange(pieces, "x")
    steps = range(1, ny)
    others = [lax.ppermute(act, "y", [(i, (i + k) % ny) for i in range(ny)]) for k in steps]
    arrived, *others = lax.optimization_barrier((arrived, *others))
    part = jnp.sum(arrived, axis=0, dtype=F32).astype(BF16).reshape(ny, rows, width)

    arrived = exchange(part, "y")
    part = jnp.sum(arrived, axis=0, dtype=F32).reshape(nzh, own, width)
    here = (jnp.arange(nzh) == zh)[:, None, None]
    part = part + jnp.where(here, residue, 0.0)

    part = part.astype(BF16).reshape(nzh, own, nz, per).transpose(2, 0, 1, 3)
    part, act, *others = lax.optimization_barrier((part, act, *others))
    parts = exchange(part.reshape(nz * nzh, own, per), ("zl", "zh"))

    row_act = jnp.zeros((ny, 1, tok, depth), BF16)
    for k, a in enumerate([act, *others]):
        row_act = lax.dynamic_update_slice(row_act, a[None, None], ((y + ny - k) % ny, 0, 0, 0))
    other_row = lax.ppermute(row_act, "core", swap)

    combined = jnp.sum(parts.reshape(nz, nzh, own, per), axis=1, dtype=F32)
    blocks = combined.reshape(nz, own, per // HEAD_SIZE, HEAD_SIZE)
    scale = (jnp.max(jnp.abs(blocks), axis=-1) + 1e-06).astype(BF16).astype(F32)
    codes = (blocks / scale[..., None]).astype(BF16)
    grad = jnp.sum(codes.astype(F32) * scale[..., None], axis=0).reshape(own, per)

    def columns(a):
        return lax.dynamic_slice_in_dim(a, zl * per, per, 1)

    _, _, new_part = update_of(grad, columns(first), columns(second), columns(weight))

    packed = jnp.concatenate([new_part, grad.astype(BF16)], axis=0)
    packed = exchange(jnp.broadcast_to(packed[None], (nz * nzh, 2 * own, per)), ("zl", "zh"))
    packed = packed.reshape(nz, nzh, 2, own, per)
    full_grad = lax.dynamic_index_in_dim(packed[:, :, 1], zh, 1, keepdims=False)
    full_grad = full_grad.astype(F32).transpose(1, 0, 2).reshape(own, width)
    new_first, new_second, _ = update_of(full_grad, first, second, weight)

    sent = packed[:, :, 0].reshape(nz, rows, per)
    sent = jnp.broadcast_to(sent[None], (nx, nz, rows, per)).reshape(nx * nz, rows, per)
    sent, row_act, other_row = lax.optimization_barrier((sent, row_act, other_row))
    got = exchange(sent, ("x", "y", "core"))
    all_act = jnp.zeros((ny, 2, tok, depth), BF16)
    all_act = lax.dynamic_update_slice(all_act, row_act, (0, core, 0, 0))
    all_act = lax.dynamic_update_slice(all_act, other_row, (0, 1 - core, 0, 0))
    all_act = all_act.reshape(ny * 2 * tok, depth)
    head = got.reshape(nx, nz, nzh, own, per).transpose(0, 2, 1, 3, 4).reshape(depth, per)
    out = jnp.dot(all_act, head, preferred_element_type=F32).astype(BF16)
    back = exchange(out.reshape(nz, tok, per), ("y", "core"))
    projected = back.transpose(1, 0, 2).reshape(tok, width)
    return projected, new_first, new_second


def solution(mesh):
    names = ("zl", "x", "zh", "y", "core")
    fine = Mesh(mesh.devices.reshape(8, 4, 2, 4, 2), names)
    fsdp = ("x", "zh", "y", "core")
    by_token, by_row = P(names, None), P(fsdp, None)
    in_specs = (by_token, by_token, by_row, by_row, by_row, P("zl", fsdp, None))
    out_specs = (by_token, by_row, by_row)
    return jax.shard_map(relay, mesh=fine, in_specs=in_specs, out_specs=out_specs, check_vma=False)
```

time: 191 us -> 173 us (0.906)
  blocking collectives: 50.7 us -> 25.5 us
  between operations: 14.4 us -> 1.08 us
  starting transfers between devices: 41.8 us -> 53.9 us
  local copies, waits for them, and re-layouts: 5.78 us -> 14.8 us
    all_to_all x2 -> x1, blocking collectives: 50.7 us -> 25.5 us  [exchange(): return lax.all_to_all(pieces, axes, split_axis=0, concat_axis=0, tiled=True)]
    all_to_all x4 -> x5, waiting for transfers between devices: 60.1 us -> 44.2 us  [exchange(): return lax.all_to_all(pieces, axes, split_axis=0, concat_axis=0, tiled=True)]
    ppermute x1 -> x4, waiting for transfers between devices: 4.05 us -> 18.9 us  [the longest x3 18.9 us: relay(): lax.ppermute(act, 'y', [(i, (i + k) % ny) for i in range(ny)])]
    all_to_all x4 -> x5, starting transfers between devices: 20.6 us -> 29.8 us  [exchange(): return lax.all_to_all(pieces, axes, split_axis=0, concat_axis=0, tiled=True)]
    dynamic_update_slice x0 -> x6, local copies, waits for them, and re-layouts: none -> 6.57 us  [the longest x1 2.97 us: relay(): all_act = lax.dynamic_update_slice(all_act, other_row, (0, 1 - core, 0, 0))]
    ppermute x1 -> x4, starting transfers between devices: 10.4 us -> 13.2 us  [the longest x3 8.55 us: relay(): lax.ppermute(act, 'y', [(i, (i + k) % ny) for i in range(ny)])]
  transfers between devices with their start and end apart: 8 -> 11, of which waited for: 6 -> 8; matrix products, arithmetic and copies ran while one was open for 5% -> 8% of each run, Pallas kernels for 0% -> 0%
where the time goes in v3:
time: 173 us; the launch traced here: 171 us
  waiting for transfers between devices  63.8 us (37%)
  starting transfers between devices  53.9 us (31%)
  blocking collectives  25.5 us (15%)
  local copies, waits for them, and re-layouts  14.8 us (9%)
  matrix products  7.75 us (4%)
  other arithmetic  3.78 us (2%)
    all_to_all x5, waiting for transfers between devices, exchange(): return lax.all_to_all(pieces, axes, split_axis=0, concat_axis=0, tiled=True)  44.2 us
    all_to_all x5, starting transfers between devices, exchange(): return lax.all_to_all(pieces, axes, split_axis=0, concat_axis=0, tiled=True)  29.8 us
    all_to_all x1, blocking collectives, exchange(): return lax.all_to_all(pieces, axes, split_axis=0, concat_axis=0, tiled=True)  25.5 us
    ppermute x3, waiting for transfers between devices, relay(): lax.ppermute(act, 'y', [(i, (i + k) % ny) for i in range(ny)])  18.9 us
    ppermute x1, starting transfers between devices, relay(): other_cot = lax.ppermute(cot, 'core', swap)  8.92 us
    ppermute x3, starting transfers between devices, relay(): lax.ppermute(act, 'y', [(i, (i + k) % ny) for i in range(ny)])  8.55 us
    ppermute x1, starting transfers between devices, relay(): other_row = lax.ppermute(row_act, 'core', swap)  4.66 us
    dot_general x1, matrix products, relay(): out = jnp.dot(all_act, head, preferred_element_type=F32).astype(BF16)  4.19 us
  transfers between devices with their start and end apart: 11, of which 8 were waited for; matrix products, arithmetic and copies ran while one was open for 8% of the time, Pallas kernels for 0%

profile of v3, /device:TPU:1, one launch (start us, length us, event | category | flops | bytes accessed | tf_op | source)
XLA Modules:
  0.0 170.6 jit_solution(6163786231771049754)
XLA Ops:
  0.6 0.0 copy-start.1
  0.6 8.9 %collective-permute-start.1 = (bf16[160,2048]{1,0:T(8,128)(2,1)}, bf16[160,2048]{1,0:T(8,128)(2,1)S(1)}, u32[]{:S(2)}, u32[]{:S(2)}) collective-permute-start(bf16[160,2048]{1,0:T(8,128)(2,1)} %param.7), channel_id=1, source_target_pairs={{0,1},{1,0},{2,3},{3,2},{4,5},{5,4},{6,7},{7,6},{8,9},{9,8},{10,11... | collective-permute-start | bytes 1966088 | tf_op jit(solution)/shard_map/ppermute | solution.py:38
  9.6 1.3 copy.21
  10.9 0.1 copy.22
  11.0 1.9 %collective-permute-start = (bf16[768,160]{1,0:T(8,128)(2,1)S(1)}, bf16[768,160]{1,0:T(8,128)(2,1)S(1)}, u32[]{:S(2)}, u32[]{:S(2)}) collective-permute-start(bf16[768,160]{1,0:T(8,128)(2,1)S(1)} %dynamic-slice_bitcast_fusion), channel_id=1, source_target_pairs={{0,1},{1,0},{2,3},{3,2},{4,5},{5,4},{6,7},{7,6},{8,9},{9,8},{10,11... | collective-permute-start | bytes 737288 | tf_op jit(solution)/shard_map/ppermute | solution.py:37
  12.9 0.0 copy-done.1
  12.9 1.0 fusion.1
  13.9 0.7 collective-permute-done
  14.6 0.0 collective-permute-done.1
  14.6 2.6 %add_convert_fusion = bf16[768,2048]{1,0:T(8,128)(2,1)} fusion(f32[768,2048]{1,0:T(8,128)S(1)} %fusion.1, bf16[768,160]{1,0:T(8,128)(2,1)S(1)} %collective-permute-done, bf16[160,2048]{1,0:T(8,128)(2,1)S(1)} %collective-permute-done.1), kind=kOutput, calls=%fused_computation | convolution fusion | flops 506462208 | bytes 10338304 | tf_op jit(solution)/shard_map/dot_general | solution.py:41
  17.2 3.7 %all-to-all-start = ((bf16[4,192,2048]{2,1,0:T(8,128)(2,1)}), bf16[4,192,2048]{2,1,0:T(8,128)(2,1)S(1)}, u32[]{:S(2)}, u32[]{:S(2)}) async-start(bf16[4,192,2048]{2,1,0:T(8,128)(2,1)} %bitcast.63), calls=%async_computation | async-start | bytes 6291456 | tf_op jit(solution)/shard_map/all_to_all | solution.py:20
  20.9 0.0 copy-start.7
  20.9 2.1 %collective-permute-start.2 = (bf16[160,1536]{1,0:T(8,128)(2,1)}, bf16[160,1536]{1,0:T(8,128)(2,1)S(1)}, u32[]{:S(2)}, u32[]{:S(2)}) collective-permute-start(bf16[160,1536]{1,0:T(8,128)(2,1)} %param.6), channel_id=1, source_target_pairs={{0,2},{2,4},{4,6},{6,0},{1,3},{3,5},{5,7},{7,1},{8,10},{10,12},{12... | collective-permute-start | bytes 1474568 | tf_op jit(solution)/shard_map/ppermute | solution.py:47
  23.0 1.9 %collective-permute-start.3 = (bf16[160,1536]{1,0:T(8,128)(2,1)}, bf16[160,1536]{1,0:T(8,128)(2,1)S(1)}, u32[]{:S(2)}, u32[]{:S(2)}) collective-permute-start(bf16[160,1536]{1,0:T(8,128)(2,1)} %param.6), channel_id=1, source_target_pairs={{0,4},{2,6},{4,0},{6,2},{1,5},{3,7},{5,1},{7,3},{8,12},{10,14},{12... | collective-permute-start | bytes 1474568 | tf_op jit(solution)/shard_map/ppermute | solution.py:47
  24.9 4.6 %collective-permute-start.4 = (bf16[160,1536]{1,0:T(8,128)(2,1)}, bf16[160,1536]{1,0:T(8,128)(2,1)}, u32[]{:S(2)}, u32[]{:S(2)}) collective-permute-start(bf16[160,1536]{1,0:T(8,128)(2,1)} %param.6), channel_id=1, source_target_pairs={{0,6},{2,0},{4,2},{6,4},{1,7},{3,1},{5,3},{7,5},{8,14},{10,8},{12,... | collective-permute-start | bytes 1474568 | tf_op jit(solution)/shard_map/ppermute | solution.py:47
  29.5 18.1 %collective-permute-done.2 = bf16[160,1536]{1,0:T(8,128)(2,1)S(1)} collective-permute-done((bf16[160,1536]{1,0:T(8,128)(2,1)}, bf16[160,1536]{1,0:T(8,128)(2,1)S(1)}, u32[]{:S(2)}, u32[]{:S(2)}) %collective-permute-start.2) | collective-permute-done | bytes 491552 | tf_op jit(solution)/shard_map/ppermute | solution.py:47
  47.6 0.0 copy-start.2
  47.6 0.0 collective-permute-done.3
  47.6 0.8 copy-done.2
  48.4 0.0 copy-start.4
  48.4 0.8 copy-done.4
  49.2 0.8 collective-permute-done.4
  49.9 8.5 %all-to-all-done = bf16[4,192,2048]{2,1,0:T(8,128)(2,1)S(1)} async-done(((bf16[4,192,2048]{2,1,0:T(8,128)(2,1)}), bf16[4,192,2048]{2,1,0:T(8,128)(2,1)S(1)}, u32[]{:S(2)}, u32[]{:S(2)}) %all-to-all-start) | async-done | bytes 3145760 | tf_op jit(solution)/shard_map/all_to_all | solution.py:20
  58.4 1.7 reduce_sum.39
  60.1 3.5 %all-to-all-start.1 = ((bf16[4,48,2048]{2,1,0:T(8,128)(2,1)}), bf16[4,48,2048]{2,1,0:T(8,128)(2,1)S(1)}, u32[]{:S(2)}, u32[]{:S(2)}) async-start(bf16[4,48,2048]{2,1,0:T(8,128)(2,1)} %bitcast.68), calls=%async_computation.1 | async-start | bytes 1572864 | tf_op jit(solution)/shard_map/all_to_all | solution.py:20
  63.6 0.0 copy-start
  63.7 0.0 copy-done.7
  63.7 0.1 copy.30
  63.8 0.0 copy-start.3
  63.8 11.1 %all-to-all-done.1 = bf16[4,48,2048]{2,1,0:T(8,128)(2,1)S(1)} async-done(((bf16[4,48,2048]{2,1,0:T(8,128)(2,1)}), bf16[4,48,2048]{2,1,0:T(8,128)(2,1)S(1)}, u32[]{:S(2)}, u32[]{:S(2)}) %all-to-all-start.1) | async-done | bytes 786464 | tf_op jit(solution)/shard_map/all_to_all | solution.py:20
  75.0 0.1 convert_reduce_fusion
  75.1 0.1 copy.29
  75.2 0.1 fusion.5
  75.3 0.7 copy.23
  76.1 9.7 %all-to-all-start.2 = ((bf16[16,24,256]{2,1,0:T(8,128)(2,1)}), bf16[16,24,256]{2,1,0:T(8,128)(2,1)S(1)}, u32[]{:S(2)}, u32[]{:S(2)}) async-start(bf16[16,24,256]{2,1,0:T(8,128)(2,1)} %bitcast.9), calls=%async_computation.2 | async-start | bytes 393216 | tf_op jit(solution)/shard_map/all_to_all | solution.py:20
  85.7 0.1 broadcast_in_dim.64
  85.9 0.0 copy-done
  86.0 0.0 copy-done.3
  86.0 1.1 bitcast_dynamic-update-slice_fusion.1
  87.1 1.1 bitcast_dynamic-update-slice_fusion
  88.2 4.7 %collective-permute-start.5 = (bf16[4,1,160,1536]{3,2,1,0:T(8,128)(2,1)S(1)}, bf16[4,1,160,1536]{3,2,1,0:T(8,128)(2,1)}, u32[]{:S(2)}, u32[]{:S(2)}) collective-permute-start(bf16[4,1,160,1536]{3,2,1,0:T(8,128)(2,1)S(1)} %bitcast_dynamic-update-slice_fusion), channel_id=1, source_target_pairs={{0,1},{1,0},{2,3},{3,2},{4,5},{5,4},{6,7},{7,6},{8,9},{9,8},{10,11... | collective-permute-start | bytes 5898248 | tf_op jit(solution)/shard_map/ppermute | solution.py:63
  92.8 6.9 %all-to-all-done.2 = bf16[16,24,256]{2,1,0:T(8,128)(2,1)S(1)} async-done(((bf16[16,24,256]{2,1,0:T(8,128)(2,1)}), bf16[16,24,256]{2,1,0:T(8,128)(2,1)S(1)}, u32[]{:S(2)}, u32[]{:S(2)}) %all-to-all-start.2) | async-done | bytes 196640 | tf_op jit(solution)/shard_map/all_to_all | solution.py:20
  99.8 0.1 abs_reduce_fusion
  99.9 0.1 multiply_reduce_fusion
  100.0 0.8 fusion.13
  100.9 25.5 %all_to_all.30 = bf16[16,48,256]{2,1,0:T(8,128)(2,1)S(1)} all-to-all(bf16[16,48,256]{2,1,0:T(8,128)(2,1)S(1)} %broadcast_in_dim.61), channel_id=1, replica_groups=mesh['zl'=8,'x'=4,'zh'=2,'y'=4,'core'=2] {'zl','zh'}, dimensions={0} | all-to-all | bytes 786432 | tf_op jit(solution)/shard_map/all_to_all | solution.py:20
  126.4 0.0 collective-permute-done.5
  126.5 1.0 broadcast_in_dim.63
  127.4 9.5 %all-to-all-start.4 = ((bf16[32,48,256]{2,1,0:T(8,128)(2,1)}), bf16[32,48,256]{2,1,0:T(8,128)(2,1)S(1)}, u32[]{:S(2)}, u32[]{:S(2)}) async-start(bf16[32,48,256]{2,1,0:T(8,128)(2,1)} %bitcast.13), calls=%async_computation.4 | async-start | bytes 1572864 | tf_op jit(solution)/shard_map/all_to_all | solution.py:20
  136.9 2.2 %broadcast_in_dim.56 = bf16[4,2,160,1536]{3,2,1,0:T(8,128)(2,1)} broadcast(bf16[]{:T(256)} %constant.79.clone.1), dimensions={} | broadcast | bytes 3932162 | tf_op jit(solution)/shard_map/broadcast_in_dim | solution.py:87
  139.1 1.4 constant_dynamic-update-slice_fusion.1
  140.5 3.0 %constant_dynamic-update-slice_fusion = bf16[4,2,160,1536]{3,2,1,0:T(8,128)(2,1)} fusion(bf16[4,2,160,1536]{3,2,1,0:T(8,128)(2,1)} %constant_dynamic-update-slice_fusion.1, bf16[4,1,160,1536]{3,2,1,0:T(8,128)(2,1)} %collective-permute-done.5, s32[]{:T(128)S(6)} %select_n.56), kind=kLoop, calls=%fused_computation.33 | loop fusion | bytes 3932164 | tf_op jit(solution)/shard_map/dynamic_update_slice | solution.py:89
  143.4 7.8 %all-to-all-done.4 = bf16[32,48,256]{2,1,0:T(8,128)(2,1)S(1)} async-done(((bf16[32,48,256]{2,1,0:T(8,128)(2,1)}), bf16[32,48,256]{2,1,0:T(8,128)(2,1)S(1)}, u32[]{:S(2)}, u32[]{:S(2)}) %all-to-all-start.4) | async-done | bytes 786464 | tf_op jit(solution)/shard_map/all_to_all | solution.py:20
  151.2 0.1 copy.24
  151.3 0.0 copy-start.5
  151.3 0.0 copy-start.6
  151.3 4.2 %convolution_convert_fusion = bf16[1280,256]{1,0:T(8,128)(2,1)} fusion(bf16[1280,1536]{1,0:T(8,128)(2,1)} %bitcast.18, bf16[1536,256]{1,0:T(8,128)(2,1)S(1)} %bitcast.73), kind=kOutput, calls=%fused_computation.1 | convolution fusion | flops 1006960640 | bytes 5373952 | tf_op jit(solution)/shard_map/dot_general | solution.py:92
  155.5 3.5 %all-to-all-start.5 = ((bf16[8,160,256]{2,1,0:T(8,128)(2,1)}), bf16[8,160,256]{2,1,0:T(8,128)(2,1)S(1)}, u32[]{:S(2)}, u32[]{:S(2)}) async-start(bf16[8,160,256]{2,1,0:T(8,128)(2,1)} %bitcast.22), calls=%async_computation.5 | async-start | bytes 1310720 | tf_op jit(solution)/shard_map/all_to_all | solution.py:20
  159.1 0.0 copy-done.5
  159.1 0.0 copy-done.6
  159.1 0.8 fusion.4
  159.9 9.8 %all-to-all-done.5 = bf16[8,160,256]{2,1,0:T(8,128)(2,1)S(1)} async-done(((bf16[8,160,256]{2,1,0:T(8,128)(2,1)}), bf16[8,160,256]{2,1,0:T(8,128)(2,1)S(1)}, u32[]{:S(2)}, u32[]{:S(2)}) %all-to-all-start.5) | async-done | bytes 655392 | tf_op jit(solution)/shard_map/all_to_all | solution.py:20
  169.7 0.9 copy.27
  (11 shorter events, 0.2 us)
Async XLA Ops:
  0.6 12.3 %copy-start.1 = (bf16[160,2048]{1,0:T(8,128)(2,1)S(1)}, bf16[160,2048]{1,0:T(8,128)(2,1)}, u32[]{:S(2)}) copy-start(bf16[160,2048]{1,0:T(8,128)(2,1)} %param.7) | copy-start | bytes 1966084
  0.6 14.0 %collective-permute-start.1 = (bf16[160,2048]{1,0:T(8,128)(2,1)}, bf16[160,2048]{1,0:T(8,128)(2,1)S(1)}, u32[]{:S(2)}, u32[]{:S(2)}) collective-permute-start(bf16[160,2048]{1,0:T(8,128)(2,1)} %param.7), channel_id=1, source_target_pairs={{0,1},{1,0},{2,3},{3,2},{4,5},{5,4},{6,7},{7,6},{8,9},{9,8},{10,11... | collective-permute-start | bytes 1966088 | tf_op jit(solution)/shard_map/ppermute | solution.py:38
  11.0 3.6 %collective-permute-start = (bf16[768,160]{1,0:T(8,128)(2,1)S(1)}, bf16[768,160]{1,0:T(8,128)(2,1)S(1)}, u32[]{:S(2)}, u32[]{:S(2)}) collective-permute-start(bf16[768,160]{1,0:T(8,128)(2,1)S(1)} %dynamic-slice_bitcast_fusion), channel_id=1, source_target_pairs={{0,1},{1,0},{2,3},{3,2},{4,5},{5,4},{6,7},{7,6},{8,9},{9,8},{10,11... | collective-permute-start | bytes 737288 | tf_op jit(solution)/shard_map/ppermute | solution.py:37
  17.2 41.2 %all-to-all-start = ((bf16[4,192,2048]{2,1,0:T(8,128)(2,1)}), bf16[4,192,2048]{2,1,0:T(8,128)(2,1)S(1)}, u32[]{:S(2)}, u32[]{:S(2)}) async-start(bf16[4,192,2048]{2,1,0:T(8,128)(2,1)} %bitcast.63), calls=%async_computation | async-start | bytes 6291456 | tf_op jit(solution)/shard_map/all_to_all | solution.py:20
  20.9 42.8 %copy-start.7 = (f32[1,24,2048]{2,1,0:T(8,128)S(1)}, f32[1,24,2048]{2,1,0:T(8,128)}, u32[]{:S(2)}) copy-start(f32[1,24,2048]{2,1,0:T(8,128)} %param.11) | copy-start | bytes 589828
  20.9 26.7 %collective-permute-start.2 = (bf16[160,1536]{1,0:T(8,128)(2,1)}, bf16[160,1536]{1,0:T(8,128)(2,1)S(1)}, u32[]{:S(2)}, u32[]{:S(2)}) collective-permute-start(bf16[160,1536]{1,0:T(8,128)(2,1)} %param.6), channel_id=1, source_target_pairs={{0,2},{2,4},{4,6},{6,0},{1,3},{3,5},{5,7},{7,1},{8,10},{10,12},{12... | collective-permute-start | bytes 1474568 | tf_op jit(solution)/shard_map/ppermute | solution.py:47
  23.0 24.6 %collective-permute-start.3 = (bf16[160,1536]{1,0:T(8,128)(2,1)}, bf16[160,1536]{1,0:T(8,128)(2,1)S(1)}, u32[]{:S(2)}, u32[]{:S(2)}) collective-permute-start(bf16[160,1536]{1,0:T(8,128)(2,1)} %param.6), channel_id=1, source_target_pairs={{0,4},{2,6},{4,0},{6,2},{1,5},{3,7},{5,1},{7,3},{8,12},{10,14},{12... | collective-permute-start | bytes 1474568 | tf_op jit(solution)/shard_map/ppermute | solution.py:47
  24.9 25.0 %collective-permute-start.4 = (bf16[160,1536]{1,0:T(8,128)(2,1)}, bf16[160,1536]{1,0:T(8,128)(2,1)}, u32[]{:S(2)}, u32[]{:S(2)}) collective-permute-start(bf16[160,1536]{1,0:T(8,128)(2,1)} %param.6), channel_id=1, source_target_pairs={{0,6},{2,0},{4,2},{6,4},{1,7},{3,1},{5,3},{7,5},{8,14},{10,8},{12,... | collective-permute-start | bytes 1474568 | tf_op jit(solution)/shard_map/ppermute | solution.py:47
  47.6 0.8 copy-start.2
  48.4 0.8 copy-start.4
  60.1 14.8 %all-to-all-start.1 = ((bf16[4,48,2048]{2,1,0:T(8,128)(2,1)}), bf16[4,48,2048]{2,1,0:T(8,128)(2,1)S(1)}, u32[]{:S(2)}, u32[]{:S(2)}) async-start(bf16[4,48,2048]{2,1,0:T(8,128)(2,1)} %bitcast.68), calls=%async_computation.1 | async-start | bytes 1572864 | tf_op jit(solution)/shard_map/all_to_all | solution.py:20
  63.6 22.3 %copy-start = (bf16[160,1536]{1,0:T(8,128)(2,1)S(1)}, bf16[160,1536]{1,0:T(8,128)(2,1)}, u32[]{:S(2)}) copy-start(bf16[160,1536]{1,0:T(8,128)(2,1)} %param.6) | copy-start | bytes 1474564
  63.8 22.1 %copy-start.3 = (bf16[160,1536]{1,0:T(8,128)(2,1)S(1)}, bf16[160,1536]{1,0:T(8,128)(2,1)}, u32[]{:S(2)}) copy-start(bf16[160,1536]{1,0:T(8,128)(2,1)} %copy-done.2) | copy-start | bytes 1474564
  76.1 23.7 %all-to-all-start.2 = ((bf16[16,24,256]{2,1,0:T(8,128)(2,1)}), bf16[16,24,256]{2,1,0:T(8,128)(2,1)S(1)}, u32[]{:S(2)}, u32[]{:S(2)}) async-start(bf16[16,24,256]{2,1,0:T(8,128)(2,1)} %bitcast.9), calls=%async_computation.2 | async-start | bytes 393216 | tf_op jit(solution)/shard_map/all_to_all | solution.py:20
  88.2 38.3 %collective-permute-start.5 = (bf16[4,1,160,1536]{3,2,1,0:T(8,128)(2,1)S(1)}, bf16[4,1,160,1536]{3,2,1,0:T(8,128)(2,1)}, u32[]{:S(2)}, u32[]{:S(2)}) collective-permute-start(bf16[4,1,160,1536]{3,2,1,0:T(8,128)(2,1)S(1)} %bitcast_dynamic-update-slice_fusion), channel_id=1, source_target_pairs={{0,1},{1,0},{2,3},{3,2},{4,5},{5,4},{6,7},{7,6},{8,9},{9,8},{10,11... | collective-permute-start | bytes 5898248 | tf_op jit(solution)/shard_map/ppermute | solution.py:63
  127.4 23.8 %all-to-all-start.4 = ((bf16[32,48,256]{2,1,0:T(8,128)(2,1)}), bf16[32,48,256]{2,1,0:T(8,128)(2,1)S(1)}, u32[]{:S(2)}, u32[]{:S(2)}) async-start(bf16[32,48,256]{2,1,0:T(8,128)(2,1)} %bitcast.13), calls=%async_computation.4 | async-start | bytes 1572864 | tf_op jit(solution)/shard_map/all_to_all | solution.py:20
  151.3 7.8 %copy-start.5 = (f32[24,2048]{1,0:T(8,128)S(1)}, f32[24,2048]{1,0:T(8,128)}, u32[]{:S(2)}) copy-start(f32[24,2048]{1,0:T(8,128)} %param.10) | copy-start | bytes 589828
  151.3 7.8 %copy-start.6 = (f32[24,2048]{1,0:T(8,128)S(1)}, f32[24,2048]{1,0:T(8,128)}, u32[]{:S(2)}) copy-start(f32[24,2048]{1,0:T(8,128)} %param.9) | copy-start | bytes 589828
  155.5 14.2 %all-to-all-start.5 = ((bf16[8,160,256]{2,1,0:T(8,128)(2,1)}), bf16[8,160,256]{2,1,0:T(8,128)(2,1)S(1)}, u32[]{:S(2)}, u32[]{:S(2)}) async-start(bf16[8,160,256]{2,1,0:T(8,128)(2,1)} %bitcast.22), calls=%async_computation.5 | async-start | bytes 1310720 | tf_op jit(solution)/shard_map/all_to_all | solution.py:20

commit v4 on v2

v4 whole, which is shorter than its diff:
```python
import jax
import jax.numpy as jnp
from jax import lax
from jax.sharding import Mesh, PartitionSpec as P

HEAD_SIZE = 256
BF16 = jnp.bfloat16
F32 = jnp.float32


def update_of(grad, first, second, weight):
    new_first = 0.9 * first + 0.1 * grad
    new_second = 0.95 * second + 0.05 * grad * grad
    update = new_first / (1.0 - 0.9**10) / (jnp.sqrt(new_second / (1.0 - 0.95**10)) + 1e-08)
    new_weight = weight.astype(F32) * (1.0 - 0.002 * 0.1) - 0.002 * update
    return new_first, new_second, new_weight.astype(BF16)


def exchange(pieces, axes):
    return lax.all_to_all(pieces, axes, split_axis=0, concat_axis=0, tiled=True)


def shift(a, axis, k):
    n = lax.axis_size(axis)
    return lax.ppermute(a, axis, [(i, (i + k) % n) for i in range(n)])


def by_head(a):
    rows, width = a.shape
    return a.reshape(rows, width // HEAD_SIZE, HEAD_SIZE).transpose(1, 0, 2)


def flat(a):
    heads, rows, size = a.shape
    return a.transpose(1, 0, 2).reshape(rows, heads * size)


def pick(a, i):
    return lax.dynamic_slice_in_dim(a, i, 1, 0)


def relay(act, cot, weight, first, second, residue):
    nx, ny, nz, nzh = (lax.axis_size(a) for a in ("x", "y", "zl", "zh"))
    core, y, zh, zl = (lax.axis_index(a) for a in ("core", "y", "zh", "zl"))
    tok, depth = act.shape
    own = weight.shape[0]
    group = ("y", "core")
    swap = [(0, 1), (1, 0)]

    near = [act] + [shift(act, "y", k) for k in range(1, ny)]
    acts = near + [lax.ppermute(a, "core", swap) for a in near]

    pieces = jnp.concatenate([by_head(cot), by_head(residue[0].astype(BF16))], axis=1)
    got = exchange(pieces, group)

    member = [2 * lax.rem(y + ny - j % ny, ny) + (core if j < ny else 1 - core) for j in range(2 * ny)]
    place = [lax.rem(y + ny - m // 2, ny) + ny * jnp.abs(core - m % 2) for m in range(2 * ny)]

    all_act = jnp.concatenate(acts, axis=0)
    head_cot = jnp.concatenate([pick(got, m)[0, :tok] for m in member], axis=0)
    term = lax.dot_general(all_act, head_cot, (((0,), (0,)), ((), ())), preferred_element_type=F32)
    term = term.astype(BF16).reshape(nx, depth // nx, HEAD_SIZE)

    def columns(a):
        return lax.dynamic_slice_in_dim(a, zl * HEAD_SIZE, HEAD_SIZE, 1)

    states = jnp.stack([columns(first), columns(second), columns(weight).astype(F32)])
    turn = [(a * nz + b, b * nz + a) for a in range(nz) for b in range(nz)]
    states = lax.ppermute(states, ("zl", "y", "core"), turn)

    arrived = exchange(term, "x")
    arrived, states = lax.optimization_barrier((arrived, states))
    part = jnp.sum(arrived, axis=0, dtype=F32).reshape(nzh, nz, own, HEAD_SIZE)
    here = (jnp.arange(nzh) == zh)[:, None, None, None]
    part = part + jnp.where(here, got[:, tok:].astype(F32), 0.0)

    part = part.astype(BF16).transpose(1, 0, 2, 3).reshape(nz * nzh, own, HEAD_SIZE)
    parts = exchange(part, ("zl", "zh"))
    combined = jnp.sum(parts.reshape(nz, nzh, own, HEAD_SIZE), axis=1, dtype=F32)
    scale = (jnp.max(jnp.abs(combined), axis=-1) + 1e-06).astype(BF16).astype(F32)
    codes = (combined / scale[..., None]).astype(BF16)
    grad = jnp.sum(codes.astype(F32) * scale[..., None], axis=0)
    _, _, new_part = update_of(grad, states[0], states[1], states[2])

    packed = jnp.concatenate([new_part, grad.astype(BF16)], axis=0)
    packed = exchange(jnp.broadcast_to(packed[None], (nz * nzh, 2 * own, HEAD_SIZE)), ("zl", "zh"))
    packed = packed.reshape(nz, nzh, 2, own, HEAD_SIZE)
    sent = packed[:, :, 0].transpose(1, 0, 2, 3).reshape(depth // nx, HEAD_SIZE)
    sent = jnp.broadcast_to(sent[None], (nx, depth // nx, HEAD_SIZE))
    head_weight = exchange(sent, "x").reshape(depth, HEAD_SIZE)

    out = jnp.dot(all_act, head_weight, preferred_element_type=F32).astype(BF16)
    out = out.reshape(2 * ny, tok, HEAD_SIZE)
    out = jnp.concatenate([pick(out, p) for p in place], axis=0)
    row_grad = lax.dynamic_index_in_dim(packed[:, :, 1], zh, 1, keepdims=False)
    back = exchange(jnp.concatenate([out, row_grad], axis=1), group)
    new_first, new_second, _ = update_of(flat(back[:, tok:]).astype(F32), first, second, weight)
    return flat(back[:, :tok]), new_first, new_second


def solution(mesh):
    names = ("zl", "x", "zh", "y", "core")
    fine = Mesh(mesh.devices.reshape(8, 4, 2, 4, 2), names)
    fsdp = ("x", "zh", "y", "core")
    by_token, by_row = P(names, None), P(fsdp, None)
    in_specs = (by_token, by_token, by_row, by_row, by_row, P("zl", fsdp, None))
    out_specs = (by_token, by_row, by_row)
    return jax.shard_map(relay, mesh=fine, in_specs=in_specs, out_specs=out_specs, check_vma=False)
```

time: 191 us -> 168 us (0.88)
  waiting for transfers between devices: 65.5 us -> 14.7 us
  blocking collectives: 50.7 us -> 83.4 us
  between operations: 14.4 us -> 1.02 us
  local copies, waits for them, and re-layouts: 5.78 us -> 13.1 us
    all_to_all x4 -> x3, waiting for transfers between devices: 60.1 us -> 12.4 us  [exchange(): return lax.all_to_all(pieces, axes, split_axis=0, concat_axis=0, tiled=True)]
    all_to_all x2 -> x3, blocking collectives: 50.7 us -> 83.4 us  [exchange(): return lax.all_to_all(pieces, axes, split_axis=0, concat_axis=0, tiled=True)]
    ppermute x3 -> x8, starting transfers between devices: 21.2 us -> 30.2 us  [the longest x4 14.2 us: relay(): acts = near + [lax.ppermute(a, 'core', swap) for a in near]]
    all_to_all x4 -> x3, starting transfers between devices: 20.6 us -> 12.6 us  [exchange(): return lax.all_to_all(pieces, axes, split_axis=0, concat_axis=0, tiled=True)]
    unnamed x21 -> x30, local copies, waits for them, and re-layouts: 1.59 us -> 8.29 us
    concatenate x0 -> x4, local copies, waits for them, and re-layouts: none -> 2.89 us  [the longest x1 1.84 us: relay(): all_act = jnp.concatenate(acts, axis=0)]
    ppermute x3 -> x8, waiting for transfers between devices: 4.76 us -> 2.29 us  [the longest x1 2.28 us: relay(): states = lax.ppermute(states, ('zl', 'y', 'core'), turn)]
    dot_general x3 -> x2, matrix products: 6.97 us -> 7.59 us  [the longest x1 4.29 us: relay(): lax.dot_general(all_act, head_cot, (((0,), (0,)), ((), ())), preferred_el...]
  transfers between devices with their start and end apart: 8 -> 11, of which waited for: 6 -> 3; matrix products, arithmetic and copies ran while one was open for 5% -> 7% of each run, Pallas kernels for 0% -> 0%
where the time goes in v4:
time: 168 us; the launch traced here: 166 us
  blocking collectives  83.4 us (50%)
  starting transfers between devices  42.8 us (25%)
  waiting for transfers between devices  14.7 us (9%)
  local copies, waits for them, and re-layouts  13.1 us (8%)
  matrix products  7.59 us (5%)
  other arithmetic  3.09 us (2%)
    all_to_all x3, blocking collectives, exchange(): return lax.all_to_all(pieces, axes, split_axis=0, concat_axis=0, tiled=True)  83.4 us
    ppermute x4, starting transfers between devices, relay(): acts = near + [lax.ppermute(a, 'core', swap) for a in near]  14.2 us
    all_to_all x3, starting transfers between devices, exchange(): return lax.all_to_all(pieces, axes, split_axis=0, concat_axis=0, tiled=True)  12.6 us
    all_to_all x3, waiting for transfers between devices, exchange(): return lax.all_to_all(pieces, axes, split_axis=0, concat_axis=0, tiled=True)  12.4 us
    ppermute x3, starting transfers between devices, shift(): return lax.ppermute(a, axis, [(i, (i + k) % n) for i in range(n)])  11.7 us
    unnamed x30, local copies, waits for them, and re-layouts  8.29 us
    ppermute x1, starting transfers between devices, relay(): states = lax.ppermute(states, ('zl', 'y', 'core'), turn)  4.3 us
    dot_general x1, matrix products, relay(): lax.dot_general(all_act, head_cot, (((0,), (0,)), ((), ())), preferred_el...  4.29 us
  transfers between devices with their start and end apart: 11, of which 3 were waited for; matrix products, arithmetic and copies ran while one was open for 7% of the time, Pallas kernels for 0%

profile of v4, /device:TPU:1, one launch (start us, length us, event | category | flops | bytes accessed | tf_op | source)
XLA Modules:
  0.0 165.7 jit_solution(14654563944800262335)
XLA Ops:
  0.6 0.0 copy-start
  0.6 4.2 %collective-permute-start = (bf16[160,1536]{1,0:T(8,128)(2,1)}, bf16[160,1536]{1,0:T(8,128)(2,1)S(1)}, u32[]{:S(2)}, u32[]{:S(2)}) collective-permute-start(bf16[160,1536]{1,0:T(8,128)(2,1)} %param.6), channel_id=1, source_target_pairs={{0,2},{2,4},{4,6},{6,0},{1,3},{3,5},{5,7},{7,1},{8,10},{10,12},{12... | collective-permute-start | bytes 1474568 | tf_op jit(solution)/shard_map/ppermute | solution.py:25
  4.8 4.5 %collective-permute-start.1 = (bf16[160,1536]{1,0:T(8,128)(2,1)}, bf16[160,1536]{1,0:T(8,128)(2,1)S(1)}, u32[]{:S(2)}, u32[]{:S(2)}) collective-permute-start(bf16[160,1536]{1,0:T(8,128)(2,1)} %param.6), channel_id=1, source_target_pairs={{0,4},{2,6},{4,0},{6,2},{1,5},{3,7},{5,1},{7,3},{8,12},{10,14},{12... | collective-permute-start | bytes 1474568 | tf_op jit(solution)/shard_map/ppermute | solution.py:25
  9.3 3.0 %collective-permute-start.2 = (bf16[160,1536]{1,0:T(8,128)(2,1)}, bf16[160,1536]{1,0:T(8,128)(2,1)S(1)}, u32[]{:S(2)}, u32[]{:S(2)}) collective-permute-start(bf16[160,1536]{1,0:T(8,128)(2,1)} %param.6), channel_id=1, source_target_pairs={{0,6},{2,0},{4,2},{6,4},{1,7},{3,1},{5,3},{7,5},{8,14},{10,8},{12,... | collective-permute-start | bytes 1474568 | tf_op jit(solution)/shard_map/ppermute | solution.py:25
  12.3 6.2 %collective-permute-start.3 = (bf16[160,1536]{1,0:T(8,128)(2,1)}, bf16[160,1536]{1,0:T(8,128)(2,1)S(1)}, u32[]{:S(2)}, u32[]{:S(2)}) collective-permute-start(bf16[160,1536]{1,0:T(8,128)(2,1)} %param.6), channel_id=1, source_target_pairs={{0,1},{1,0},{2,3},{3,2},{4,5},{5,4},{6,7},{7,6},{8,9},{9,8},{10,11... | collective-permute-start | bytes 1474568 | tf_op jit(solution)/shard_map/ppermute | solution.py:51
  18.6 0.9 convert_element_type.64
  19.5 1.2 copy.94
  20.8 0.1 pad_maximum_fusion
  20.9 1.0 copy.87
  21.9 4.3 %all-to-all-start = ((bf16[8,184,256]{2,1,0:T(8,128)(2,1)}), bf16[8,184,256]{2,1,0:T(8,128)(2,1)S(1)}, u32[]{:S(2)}, u32[]{:S(2)}) async-start(bf16[8,184,256]{2,1,0:T(8,128)(2,1)} %copy.87), calls=%async_computation | async-start | bytes 1507328 | tf_op jit(solution)/shard_map/all_to_all | solution.py:20
  26.2 0.0 copy-done
  26.2 0.8 constant_dynamic-update-slice_fusion.7
  27.0 0.0 collective-permute-done
  27.0 1.9 %collective-permute-start.4 = (bf16[160,1536]{1,0:T(8,128)(2,1)S(1)}, bf16[160,1536]{1,0:T(8,128)(2,1)S(1)}, u32[]{:S(2)}, u32[]{:S(2)}) collective-permute-start(bf16[160,1536]{1,0:T(8,128)(2,1)S(1)} %collective-permute-done), channel_id=1, source_target_pairs={{0,1},{1,0},{2,3},{3,2},{4,5},{5,4},{6,7},{7,6},{8,9},{9,8},{10,11... | collective-permute-start | bytes 1474568 | tf_op jit(solution)/shard_map/ppermute | solution.py:51
  28.9 0.8 constant_dynamic-update-slice_fusion.6
  29.7 0.0 collective-permute-done.1
  29.7 2.5 %collective-permute-start.5 = (bf16[160,1536]{1,0:T(8,128)(2,1)S(1)}, bf16[160,1536]{1,0:T(8,128)(2,1)}, u32[]{:S(2)}, u32[]{:S(2)}) collective-permute-start(bf16[160,1536]{1,0:T(8,128)(2,1)S(1)} %collective-permute-done.1), channel_id=1, source_target_pairs={{0,1},{1,0},{2,3},{3,2},{4,5},{5,4},{6,7},{7,6},{8,9},{9,8},{10,11... | collective-permute-start | bytes 1474568 | tf_op jit(solution)/shard_map/ppermute | solution.py:51
  32.2 0.0 collective-permute-done.2
  32.2 3.6 %collective-permute-start.6 = (bf16[160,1536]{1,0:T(8,128)(2,1)S(1)}, bf16[160,1536]{1,0:T(8,128)(2,1)}, u32[]{:S(2)}, u32[]{:S(2)}) collective-permute-start(bf16[160,1536]{1,0:T(8,128)(2,1)S(1)} %collective-permute-done.2), channel_id=1, source_target_pairs={{0,1},{1,0},{2,3},{3,2},{4,5},{5,4},{6,7},{7,6},{8,9},{9,8},{10,11... | collective-permute-start | bytes 1474568 | tf_op jit(solution)/shard_map/ppermute | solution.py:51
  35.8 0.8 constant_dynamic-update-slice_fusion.5
  36.6 0.8 constant_dynamic-update-slice_fusion.4
  37.5 0.0 collective-permute-done.3
  37.5 0.8 constant_dynamic-update-slice_fusion.3
  38.3 0.0 all-to-all-done
  38.5 0.0 collective-permute-done.4
  38.5 0.8 constant_dynamic-update-slice_fusion.2
  39.3 0.0 collective-permute-done.5
  39.3 1.8 %constant_dynamic-update-slice_fusion.1 = bf16[1280,1536]{1,0:T(8,128)(2,1)} fusion(bf16[1280,1536]{1,0:T(8,128)(2,1)} %constant_dynamic-update-slice_fusion.2, bf16[160,1536]{1,0:T(8,128)(2,1)} %collective-permute-done.5), kind=kLoop, calls=%fused_computation.45 | loop fusion | bytes 983040
  41.1 0.0 collective-permute-done.6
  41.1 1.8 %constant_dynamic-update-slice_fusion = bf16[1280,1536]{1,0:T(8,128)(2,1)} fusion(bf16[1280,1536]{1,0:T(8,128)(2,1)} %constant_dynamic-update-slice_fusion.1, bf16[160,1536]{1,0:T(8,128)(2,1)} %collective-permute-done.6), kind=kLoop, calls=%fused_computation.44 | loop fusion | bytes 983040 | tf_op jit(solution)/shard_map/concatenate | solution.py:59
  43.0 0.0 copy-start.1
  43.0 0.0 copy-start.2
  43.0 4.3 %convolution_convert_fusion.1 = bf16[1536,256]{1,0:T(8,128)(2,1)} fusion(bf16[1280,1536]{1,0:T(8,128)(2,1)} %constant_dynamic-update-slice_fusion, bf16[1280,256]{1,0:T(8,128)(2,1)S(1)} %fusion.2), kind=kOutput, calls=%fused_computation.1 | convolution fusion | flops 1007026176 | bytes 5373952 | tf_op jit(solution)/shard_map/dot_general | solution.py:61
  47.3 3.6 %all-to-all-start.1 = ((bf16[4,384,256]{2,1,0:T(8,128)(2,1)}), bf16[4,384,256]{2,1,0:T(8,128)(2,1)S(1)}, u32[]{:S(2)}, u32[]{:S(2)}) async-start(bf16[4,384,256]{2,1,0:T(8,128)(2,1)} %bitcast.10), calls=%async_computation.1 | async-start | bytes 1572864 | tf_op jit(solution)/shard_map/all_to_all | solution.py:20
  50.8 0.7 bitcast_convert_fusion
  51.6 0.0 copy-done.1
  51.6 0.0 copy-done.2
  51.6 4.3 %collective-permute-start.7 = (f32[3,24,256]{2,1,0:T(8,128)S(1)}, f32[3,24,256]{2,1,0:T(8,128)S(1)}, u32[]{:S(2)}, u32[]{:S(2)}) collective-permute-start(f32[3,24,256]{2,1,0:T(8,128)S(1)} %pad_maximum_fusion.2), channel_id=1, source_target_pairs={{0,0},{1,64},{2,128},{3,192},{4,256},{5,320},{6,384},{7,448},{64,1... | collective-permute-start | bytes 221192 | tf_op jit(solution)/shard_map/ppermute | solution.py:69
  55.9 2.3 %collective-permute-done.7 = f32[3,24,256]{2,1,0:T(8,128)S(1)} collective-permute-done((f32[3,24,256]{2,1,0:T(8,128)S(1)}, f32[3,24,256]{2,1,0:T(8,128)S(1)}, u32[]{:S(2)}, u32[]{:S(2)}) %collective-permute-start.7) | collective-permute-done | bytes 73760 | tf_op jit(solution)/shard_map/ppermute | solution.py:69
  58.2 4.1 %all-to-all-done.1 = bf16[4,384,256]{2,1,0:T(8,128)(2,1)S(1)} async-done(((bf16[4,384,256]{2,1,0:T(8,128)(2,1)}), bf16[4,384,256]{2,1,0:T(8,128)(2,1)S(1)}, u32[]{:S(2)}, u32[]{:S(2)}) %all-to-all-start.1) | async-done | bytes 786464 | tf_op jit(solution)/shard_map/all_to_all | solution.py:20
  62.3 0.1 convert_reduce_fusion
  62.4 0.1 fusion.1
  62.5 28.7 %all_to_all.30 = bf16[16,24,256]{2,1,0:T(8,128)(2,1)S(1)} all-to-all(bf16[16,24,256]{2,1,0:T(8,128)(2,1)S(1)} %bitcast.98), channel_id=1, replica_groups=mesh['zl'=8,'x'=4,'zh'=2,'y'=4,'core'=2] {'zl','zh'}, dimensions={0} | all-to-all | bytes 393216 | tf_op jit(solution)/shard_map/all_to_all | solution.py:20
  91.3 0.1 abs_reduce_fusion
  91.4 0.1 multiply_reduce_fusion
  91.6 25.4 %all_to_all.31 = bf16[16,48,256]{2,1,0:T(8,128)(2,1)S(1)} all-to-all(bf16[16,48,256]{2,1,0:T(8,128)(2,1)S(1)} %broadcast_in_dim.35), channel_id=1, replica_groups=mesh['zl'=8,'x'=4,'zh'=2,'y'=4,'core'=2] {'zl','zh'}, dimensions={0} | all-to-all | bytes 786432 | tf_op jit(solution)/shard_map/all_to_all | solution.py:20
  117.1 0.9 broadcast_in_dim.37
  118.0 4.8 %all-to-all-start.4 = ((bf16[4,384,256]{2,1,0:T(8,128)(2,1)}), bf16[4,384,256]{2,1,0:T(8,128)(2,1)S(1)}, u32[]{:S(2)}, u32[]{:S(2)}) async-start(bf16[4,384,256]{2,1,0:T(8,128)(2,1)} %broadcast_in_dim.37), calls=%async_computation.4 | async-start | bytes 1572864 | tf_op jit(solution)/shard_map/all_to_all | solution.py:20
  122.8 8.3 %all-to-all-done.4 = bf16[4,384,256]{2,1,0:T(8,128)(2,1)S(1)} async-done(((bf16[4,384,256]{2,1,0:T(8,128)(2,1)}), bf16[4,384,256]{2,1,0:T(8,128)(2,1)S(1)}, u32[]{:S(2)}, u32[]{:S(2)}) %all-to-all-start.4) | async-done | bytes 786464 | tf_op jit(solution)/shard_map/all_to_all | solution.py:20
  131.2 3.3 %convolution_convert_fusion = bf16[1280,256]{1,0:T(8,128)(2,1)S(1)} fusion(bf16[1280,1536]{1,0:T(8,128)(2,1)} %constant_dynamic-update-slice_fusion, bf16[1536,256]{1,0:T(8,128)(2,1)S(1)} %bitcast.97), kind=kOutput, calls=%fused_computation | convolution fusion | flops 1006960640 | bytes 5373952 | tf_op jit(solution)/shard_map/dot_general | solution.py:92
  134.7 0.1 pad_maximum_fusion.1
  134.7 29.2 %all_to_all.32 = bf16[8,184,256]{2,1,0:T(8,128)(2,1)S(1)} all-to-all(bf16[8,184,256]{2,1,0:T(8,128)(2,1)S(1)} %pad_maximum_fusion.1), channel_id=1, replica_groups=mesh['zl'=8,'x'=4,'zh'=2,'y'=4,'core'=2] {'y','core'}, dimensions={0} | all-to-all | bytes 1507328 | tf_op jit(solution)/shard_map/all_to_all | solution.py:20
  164.0 0.9 copy.92
  164.9 0.8 fusion
  (33 shorter events, 0.5 us)
Async XLA Ops:
  0.6 25.6 %copy-start = (bf16[160,1536]{1,0:T(8,128)(2,1)S(1)}, bf16[160,1536]{1,0:T(8,128)(2,1)}, u32[]{:S(2)}) copy-start(bf16[160,1536]{1,0:T(8,128)(2,1)} %param.6) | copy-start | bytes 1474564
  0.6 26.4 %collective-permute-start = (bf16[160,1536]{1,0:T(8,128)(2,1)}, bf16[160,1536]{1,0:T(8,128)(2,1)S(1)}, u32[]{:S(2)}, u32[]{:S(2)}) collective-permute-start(bf16[160,1536]{1,0:T(8,128)(2,1)} %param.6), channel_id=1, source_target_pairs={{0,2},{2,4},{4,6},{6,0},{1,3},{3,5},{5,7},{7,1},{8,10},{10,12},{12... | collective-permute-start | bytes 1474568 | tf_op jit(solution)/shard_map/ppermute | solution.py:25
  4.8 24.9 %collective-permute-start.1 = (bf16[160,1536]{1,0:T(8,128)(2,1)}, bf16[160,1536]{1,0:T(8,128)(2,1)S(1)}, u32[]{:S(2)}, u32[]{:S(2)}) collective-permute-start(bf16[160,1536]{1,0:T(8,128)(2,1)} %param.6), channel_id=1, source_target_pairs={{0,4},{2,6},{4,0},{6,2},{1,5},{3,7},{5,1},{7,3},{8,12},{10,14},{12... | collective-permute-start | bytes 1474568 | tf_op jit(solution)/shard_map/ppermute | solution.py:25
  9.3 22.9 %collective-permute-start.2 = (bf16[160,1536]{1,0:T(8,128)(2,1)}, bf16[160,1536]{1,0:T(8,128)(2,1)S(1)}, u32[]{:S(2)}, u32[]{:S(2)}) collective-permute-start(bf16[160,1536]{1,0:T(8,128)(2,1)} %param.6), channel_id=1, source_target_pairs={{0,6},{2,0},{4,2},{6,4},{1,7},{3,1},{5,3},{7,5},{8,14},{10,8},{12,... | collective-permute-start | bytes 1474568 | tf_op jit(solution)/shard_map/ppermute | solution.py:25
  12.3 25.1 %collective-permute-start.3 = (bf16[160,1536]{1,0:T(8,128)(2,1)}, bf16[160,1536]{1,0:T(8,128)(2,1)S(1)}, u32[]{:S(2)}, u32[]{:S(2)}) collective-permute-start(bf16[160,1536]{1,0:T(8,128)(2,1)} %param.6), channel_id=1, source_target_pairs={{0,1},{1,0},{2,3},{3,2},{4,5},{5,4},{6,7},{7,6},{8,9},{9,8},{10,11... | collective-permute-start | bytes 1474568 | tf_op jit(solution)/shard_map/ppermute | solution.py:51
  21.9 16.4 %all-to-all-start = ((bf16[8,184,256]{2,1,0:T(8,128)(2,1)}), bf16[8,184,256]{2,1,0:T(8,128)(2,1)S(1)}, u32[]{:S(2)}, u32[]{:S(2)}) async-start(bf16[8,184,256]{2,1,0:T(8,128)(2,1)} %copy.87), calls=%async_computation | async-start | bytes 1507328 | tf_op jit(solution)/shard_map/all_to_all | solution.py:20
  27.0 11.5 %collective-permute-start.4 = (bf16[160,1536]{1,0:T(8,128)(2,1)S(1)}, bf16[160,1536]{1,0:T(8,128)(2,1)S(1)}, u32[]{:S(2)}, u32[]{:S(2)}) collective-permute-start(bf16[160,1536]{1,0:T(8,128)(2,1)S(1)} %collective-permute-done), channel_id=1, source_target_pairs={{0,1},{1,0},{2,3},{3,2},{4,5},{5,4},{6,7},{7,6},{8,9},{9,8},{10,11... | collective-permute-start | bytes 1474568 | tf_op jit(solution)/shard_map/ppermute | solution.py:51
  29.7 9.6 %collective-permute-start.5 = (bf16[160,1536]{1,0:T(8,128)(2,1)S(1)}, bf16[160,1536]{1,0:T(8,128)(2,1)}, u32[]{:S(2)}, u32[]{:S(2)}) collective-permute-start(bf16[160,1536]{1,0:T(8,128)(2,1)S(1)} %collective-permute-done.1), channel_id=1, source_target_pairs={{0,1},{1,0},{2,3},{3,2},{4,5},{5,4},{6,7},{7,6},{8,9},{9,8},{10,11... | collective-permute-start | bytes 1474568 | tf_op jit(solution)/shard_map/ppermute | solution.py:51
  32.2 8.9 %collective-permute-start.6 = (bf16[160,1536]{1,0:T(8,128)(2,1)S(1)}, bf16[160,1536]{1,0:T(8,128)(2,1)}, u32[]{:S(2)}, u32[]{:S(2)}) collective-permute-start(bf16[160,1536]{1,0:T(8,128)(2,1)S(1)} %collective-permute-done.2), channel_id=1, source_target_pairs={{0,1},{1,0},{2,3},{3,2},{4,5},{5,4},{6,7},{7,6},{8,9},{9,8},{10,11... | collective-permute-start | bytes 1474568 | tf_op jit(solution)/shard_map/ppermute | solution.py:51
  43.0 8.6 %copy-start.1 = (f32[24,2048]{1,0:T(8,128)S(1)}, f32[24,2048]{1,0:T(8,128)}, u32[]{:S(2)}) copy-start(f32[24,2048]{1,0:T(8,128)} %param.10) | copy-start | bytes 589828
  43.0 8.6 %copy-start.2 = (f32[24,2048]{1,0:T(8,128)S(1)}, f32[24,2048]{1,0:T(8,128)}, u32[]{:S(2)}) copy-start(f32[24,2048]{1,0:T(8,128)} %param.9) | copy-start | bytes 589828
  47.3 15.0 %all-to-all-start.1 = ((bf16[4,384,256]{2,1,0:T(8,128)(2,1)}), bf16[4,384,256]{2,1,0:T(8,128)(2,1)S(1)}, u32[]{:S(2)}, u32[]{:S(2)}) async-start(bf16[4,384,256]{2,1,0:T(8,128)(2,1)} %bitcast.10), calls=%async_computation.1 | async-start | bytes 1572864 | tf_op jit(solution)/shard_map/all_to_all | solution.py:20
  51.6 6.6 %collective-permute-start.7 = (f32[3,24,256]{2,1,0:T(8,128)S(1)}, f32[3,24,256]{2,1,0:T(8,128)S(1)}, u32[]{:S(2)}, u32[]{:S(2)}) collective-permute-start(f32[3,24,256]{2,1,0:T(8,128)S(1)} %pad_maximum_fusion.2), channel_id=1, source_target_pairs={{0,0},{1,64},{2,128},{3,192},{4,256},{5,320},{6,384},{7,448},{64,1... | collective-permute-start | bytes 221192 | tf_op jit(solution)/shard_map/ppermute | solution.py:69
  118.0 13.1 %all-to-all-start.4 = ((bf16[4,384,256]{2,1,0:T(8,128)(2,1)}), bf16[4,384,256]{2,1,0:T(8,128)(2,1)S(1)}, u32[]{:S(2)}, u32[]{:S(2)}) async-start(bf16[4,384,256]{2,1,0:T(8,128)(2,1)} %broadcast_in_dim.37), calls=%async_computation.4 | async-start | bytes 1572864 | tf_op jit(solution)/shard_map/all_to_all | solution.py:20

commit v5 on v4

--- a/solution.py
+++ b/solution.py
@@ -1,6 +1,8 @@
 import jax
 import jax.numpy as jnp
 from jax import lax
+from jax.experimental import pallas as pl
+from jax.experimental.pallas import tpu as pltpu
 from jax.sharding import Mesh, PartitionSpec as P
 
 HEAD_SIZE = 256
@@ -25,18 +27,50 @@
     return lax.ppermute(a, axis, [(i, (i + k) % n) for i in range(n)])
 
 
-def by_head(a):
-    rows, width = a.shape
-    return a.reshape(rows, width // HEAD_SIZE, HEAD_SIZE).transpose(1, 0, 2)
+def call(body, shape, *args):
+    spaces = [pltpu.SMEM if a.dtype == jnp.int32 else pltpu.VMEM for a in args]
+    return pl.pallas_call(
+        body,
+        out_shape=jax.ShapeDtypeStruct(shape, BF16),
+        in_specs=[pl.BlockSpec(memory_space=m) for m in spaces],
+        out_specs=pl.BlockSpec(memory_space=pltpu.VMEM),
+        compiler_params=pltpu.CompilerParams(vmem_limit_bytes=32 << 20),
+    )(*args)
+
+
+def split_heads(cot, residue, out):
+    heads, rows, size = out.shape
+    tok, own = cot.shape[0], residue.shape[0]
+    zeros = jnp.zeros((rows - tok - own, size), F32)
+    for h in range(heads):
+        at = pl.ds(h * size, size)
+        out[h, :tok, :] = cot[:, at]
+        out[h, tok:, :] = jnp.concatenate([residue[:, at], zeros], axis=0).astype(BF16)
+
+
+def head_term(member, *refs):
+    *acts, cot, out = refs
+    tok = acts[0].shape[0]
+    blocks, rows, _ = out.shape
+    head_cot = jnp.concatenate([cot[member[j], :tok, :] for j in range(len(acts))], axis=0)
+    for i in range(blocks):
+        act = jnp.concatenate([a[:, i * rows : (i + 1) * rows] for a in acts], axis=0)
+        term = lax.dot_general(act, head_cot, (((0,), (0,)), ((), ())), preferred_element_type=F32)
+        out[i] = term.astype(BF16)
+
+
+def project(member, *refs):
+    *acts, weight, grad, out = refs
+    tok = acts[0].shape[0]
+    for j, a in enumerate(acts):
+        block = jnp.dot(a[...], weight[...], preferred_element_type=F32)
+        out[member[j], :tok, :] = block.astype(BF16)
+    out[:, tok:, :] = grad[...]
 
 
 def flat(a):
     heads, rows, size = a.shape
     return a.transpose(1, 0, 2).reshape(rows, heads * size)
-
-
-def pick(a, i):
-    return lax.dynamic_slice_in_dim(a, i, 1, 0)
 
 
 def relay(act, cot, weight, first, second, residue):
@@ -50,16 +84,12 @@
     near = [act] + [shift(act, "y", k) for k in range(1, ny)]
     acts = near + [lax.ppermute(a, "core", swap) for a in near]
 
-    pieces = jnp.concatenate([by_head(cot), by_head(residue[0].astype(BF16))], axis=1)
-    got = exchange(pieces, group)
+    block = -(-(tok + own) // 16) * 16
+    got = exchange(call(split_heads, (nz, block, HEAD_SIZE), cot, residue[0]), group)
 
     member = [2 * lax.rem(y + ny - j % ny, ny) + (core if j < ny else 1 - core) for j in range(2 * ny)]
-    place = [lax.rem(y + ny - m // 2, ny) + ny * jnp.abs(core - m % 2) for m in range(2 * ny)]
-
-    all_act = jnp.concatenate(acts, axis=0)
-    head_cot = jnp.concatenate([pick(got, m)[0, :tok] for m in member], axis=0)
-    term = lax.dot_general(all_act, head_cot, (((0,), (0,)), ((), ())), preferred_element_type=F32)
-    term = term.astype(BF16).reshape(nx, depth // nx, HEAD_SIZE)
+    member = jnp.stack(member).astype(jnp.int32)
+    term = call(head_term, (nx, depth // nx, HEAD_SIZE), member, *acts, got)
 
     def columns(a):
         return lax.dynamic_slice_in_dim(a, zl * HEAD_SIZE, HEAD_SIZE, 1)
@@ -72,7 +102,7 @@
     arrived, states = lax.optimization_barrier((arrived, states))
     part = jnp.sum(arrived, axis=0, dtype=F32).reshape(nzh, nz, own, HEAD_SIZE)
     here = (jnp.arange(nzh) == zh)[:, None, None, None]
-    part = part + jnp.where(here, got[:, tok:].astype(F32), 0.0)
+    part = part + jnp.where(here, got[:, tok : tok + own].astype(F32), 0.0)
 
     part = part.astype(BF16).transpose(1, 0, 2, 3).reshape(nz * nzh, own, HEAD_SIZE)
     parts = exchange(part, ("zl", "zh"))
@@ -89,12 +119,13 @@
     sent = jnp.broadcast_to(sent[None], (nx, depth // nx, HEAD_SIZE))
     head_weight = exchange(sent, "x").reshape(depth, HEAD_SIZE)
 
-    out = jnp.dot(all_act, head_weight, preferred_element_type=F32).astype(BF16)
-    out = out.reshape(2 * ny, tok, HEAD_SIZE)
-    out = jnp.concatenate([pick(out, p) for p in place], axis=0)
     row_grad = lax.dynamic_index_in_dim(packed[:, :, 1], zh, 1, keepdims=False)
-    back = exchange(jnp.concatenate([out, row_grad], axis=1), group)
-    new_first, new_second, _ = update_of(flat(back[:, tok:]).astype(F32), first, second, weight)
+    row_grad = jnp.pad(row_grad, ((0, 0), (0, block - tok - own), (0, 0)))
+    out = call(project, (nz, block, HEAD_SIZE), member, *acts, head_weight, row_grad)
+    back = exchange(out, group)
+    new_first, new_second, _ = update_of(
+        flat(back[:, tok : tok + own]).astype(F32), first, second, weight
+    )
     return flat(back[:, :tok]), new_first, new_second
 
 

time: 168 us -> 164 us (0.976)
  local copies, waits for them, and re-layouts: 13.1 us -> 5.12 us
  matrix products: 7.59 us -> 0 us
  Pallas kernels: 0 us -> 6.96 us
  starting transfers between devices: 42.8 us -> 46.4 us
    dot_general x2 -> x0, matrix products: 7.59 us -> none  [the longest x1 4.29 us: relay(): lax.dot_general(all_act, head_cot, (((0,), (0,)), ((), ())), preferred_el...]
    pallas_call x0 -> x3, Pallas kernels: none -> 6.96 us  [call(): pl.pallas_call(body, out_shape=jax.ShapeDtypeStruct(shape, BF16), in_spec...]
    unnamed x30 -> x11, local copies, waits for them, and re-layouts: 8.29 us -> 2.3 us
    all_to_all x3, starting transfers between devices: 12.6 us -> 17.5 us  [exchange(): return lax.all_to_all(pieces, axes, split_axis=0, concat_axis=0, tiled=True)]
    concatenate x4 -> x0, local copies, waits for them, and re-layouts: 2.89 us -> none  [the longest x1 1.84 us: relay(): all_act = jnp.concatenate(acts, axis=0)]
  transfers between devices with their start and end apart: 11 -> 11, of which waited for: 3 -> 4; matrix products, arithmetic and copies ran while one was open for 7% -> 1% of each run, Pallas kernels for 0% -> 1%
where the time goes in v5:
time: 164 us; the launch traced here: 161 us
  blocking collectives  82.8 us (50%)
  starting transfers between devices  46.4 us (28%)
  waiting for transfers between devices  15 us (9%)
  Pallas kernels  6.96 us (4%)
  local copies, waits for them, and re-layouts  5.12 us (3%)
  other arithmetic  3.99 us (2%)
    all_to_all x3, blocking collectives, exchange(): return lax.all_to_all(pieces, axes, split_axis=0, concat_axis=0, tiled=True)  82.8 us
    all_to_all x3, starting transfers between devices, exchange(): return lax.all_to_all(pieces, axes, split_axis=0, concat_axis=0, tiled=True)  17.5 us
    ppermute x4, starting transfers between devices, relay(): acts = near + [lax.ppermute(a, 'core', swap) for a in near]  13.3 us
    all_to_all x3, waiting for transfers between devices, exchange(): return lax.all_to_all(pieces, axes, split_axis=0, concat_axis=0, tiled=True)  12.6 us
    ppermute x3, starting transfers between devices, shift(): return lax.ppermute(a, axis, [(i, (i + k) % n) for i in range(n)])  10.3 us
    pallas_call x3, Pallas kernels, call(): pl.pallas_call(body, out_shape=jax.ShapeDtypeStruct(shape, BF16), in_spec...  6.96 us
    ppermute x1, starting transfers between devices, relay(): states = lax.ppermute(states, ('zl', 'y', 'core'), turn)  5.25 us
  transfers between devices with their start and end apart: 11, of which 4 were waited for; matrix products, arithmetic and copies ran while one was open for 1% of the time, Pallas kernels for 1%

profile of v5, /device:TPU:1, one launch (start us, length us, event | category | flops | bytes accessed | tf_op | source)
XLA Modules:
  0.0 161.2 jit_solution(7411647426309229840)
XLA Ops:
  0.6 5.5 %collective-permute-start.2 = (bf16[160,1536]{1,0:T(8,128)(2,1)}, bf16[160,1536]{1,0:T(8,128)(2,1)S(1)}, u32[]{:S(2)}, u32[]{:S(2)}) collective-permute-start(bf16[160,1536]{1,0:T(8,128)(2,1)} %refs_0_.3), channel_id=1, source_target_pairs={{0,6},{2,0},{4,2},{6,4},{1,7},{3,1},{5,3},{7,5},{8,14},{10,8},{12,... | collective-permute-start | bytes 1474568 | tf_op jit(solution)/shard_map/ppermute | solution.py:27
  6.1 2.3 %collective-permute-start.1 = (bf16[160,1536]{1,0:T(8,128)(2,1)}, bf16[160,1536]{1,0:T(8,128)(2,1)S(1)}, u32[]{:S(2)}, u32[]{:S(2)}) collective-permute-start(bf16[160,1536]{1,0:T(8,128)(2,1)} %refs_0_.3), channel_id=1, source_target_pairs={{0,4},{2,6},{4,0},{6,2},{1,5},{3,7},{5,1},{7,3},{8,12},{10,14},{12... | collective-permute-start | bytes 1474568 | tf_op jit(solution)/shard_map/ppermute | solution.py:27
  8.4 2.6 %collective-permute-start = (bf16[160,1536]{1,0:T(8,128)(2,1)}, bf16[160,1536]{1,0:T(8,128)(2,1)S(1)}, u32[]{:S(2)}, u32[]{:S(2)}) collective-permute-start(bf16[160,1536]{1,0:T(8,128)(2,1)} %refs_0_.3), channel_id=1, source_target_pairs={{0,2},{2,4},{4,6},{6,0},{1,3},{3,5},{5,7},{7,1},{8,10},{10,12},{12... | collective-permute-start | bytes 1474568 | tf_op jit(solution)/shard_map/ppermute | solution.py:27
  11.0 0.0 copy-start.1
  11.0 1.1 copy-done.1
  12.1 0.0 copy-start.2
  12.1 0.9 copy-done.2
  13.0 0.9 shard_map.85
  14.0 0.0 copy-start
  14.0 9.8 %all-to-all-start = ((bf16[8,192,256]{2,1,0:T(8,128)(2,1)}), bf16[8,192,256]{2,1,0:T(8,128)(2,1)S(1)}, u32[]{:S(2)}, u32[]{:S(2)}) async-start(bf16[8,192,256]{2,1,0:T(8,128)(2,1)} %shard_map.85), calls=%async_computation | async-start | bytes 1572864 | tf_op jit(solution)/shard_map/all_to_all | solution.py:22
  23.8 0.0 copy-done
  23.8 1.9 %collective-permute-start.3 = (bf16[160,1536]{1,0:T(8,128)(2,1)S(1)}, bf16[160,1536]{1,0:T(8,128)(2,1)S(1)}, u32[]{:S(2)}, u32[]{:S(2)}) collective-permute-start(bf16[160,1536]{1,0:T(8,128)(2,1)S(1)} %copy-done), channel_id=1, source_target_pairs={{0,1},{1,0},{2,3},{3,2},{4,5},{5,4},{6,7},{7,6},{8,9},{9,8},{10,11... | collective-permute-start | bytes 1474568 | tf_op jit(solution)/shard_map/ppermute | solution.py:85
  25.7 0.0 collective-permute-done.2.refs_3_
  25.7 7.1 %collective-permute-start.6 = (bf16[160,1536]{1,0:T(8,128)(2,1)S(1)}, bf16[160,1536]{1,0:T(8,128)(2,1)}, u32[]{:S(2)}, u32[]{:S(2)}) collective-permute-start(bf16[160,1536]{1,0:T(8,128)(2,1)S(1)} %collective-permute-done.2.refs_3_), channel_id=1, source_target_pairs={{0,1},{1,0},{2,3},{3,2},{4,5},{5,4},{6,7},{7,6},{8,9},{9,8},{10,11... | collective-permute-start | bytes 1474568 | tf_op jit(solution)/shard_map/ppermute | solution.py:85
  32.8 0.0 collective-permute-done.1.refs_2_
  32.8 1.9 %collective-permute-start.5 = (bf16[160,1536]{1,0:T(8,128)(2,1)S(1)}, bf16[160,1536]{1,0:T(8,128)(2,1)}, u32[]{:S(2)}, u32[]{:S(2)}) collective-permute-start(bf16[160,1536]{1,0:T(8,128)(2,1)S(1)} %collective-permute-done.1.refs_2_), channel_id=1, source_target_pairs={{0,1},{1,0},{2,3},{3,2},{4,5},{5,4},{6,7},{7,6},{8,9},{9,8},{10,11... | collective-permute-start | bytes 1474568 | tf_op jit(solution)/shard_map/ppermute | solution.py:85
  34.8 0.0 collective-permute-done.refs_1_
  34.8 2.4 %collective-permute-start.4 = (bf16[160,1536]{1,0:T(8,128)(2,1)S(1)}, bf16[160,1536]{1,0:T(8,128)(2,1)}, u32[]{:S(2)}, u32[]{:S(2)}) collective-permute-start(bf16[160,1536]{1,0:T(8,128)(2,1)S(1)} %collective-permute-done.refs_1_), channel_id=1, source_target_pairs={{0,1},{1,0},{2,3},{3,2},{4,5},{5,4},{6,7},{7,6},{8,9},{9,8},{10,11... | collective-permute-start | bytes 1474568 | tf_op jit(solution)/shard_map/ppermute | solution.py:85
  37.2 0.1 stack.50.member
  37.3 0.0 collective-permute-done.3.refs_4_
  37.3 3.3 %all-to-all-done.refs_8_ = bf16[8,192,256]{2,1,0:T(8,128)(2,1)S(1)} async-done(((bf16[8,192,256]{2,1,0:T(8,128)(2,1)}), bf16[8,192,256]{2,1,0:T(8,128)(2,1)S(1)}, u32[]{:S(2)}, u32[]{:S(2)}) %all-to-all-start) | async-done | bytes 786464 | tf_op jit(solution)/shard_map/all_to_all | solution.py:22
  40.6 0.0 collective-permute-done.6.refs_7_
  40.6 0.0 collective-permute-done.5.refs_6_
  40.6 0.0 collective-permute-done.4.refs_5_
  40.6 3.5 %shard_map.86 = bf16[4,384,256]{2,1,0:T(8,128)(2,1)} custom-call(s32[8]{0:T(128)S(1)} %stack.50.member, bf16[160,1536]{1,0:T(8,128)(2,1)S(1)} %copy-done, bf16[160,1536]{1,0:T(8,128)(2,1)S(1)} %collective-permute-done.refs_1_, bf16[160,1536]{1,0:T(8,128)(2,1)S(1)} %collective-permute-done.1.refs_2_, bf16[160,1536]{1,0:T(8,128)(2,1)S(1)} %collective-permute-done.2.refs_3_, ...), custom_call_target="tpu_custom_call" | custom-call | tf_op jit(solution)/shard_map/pallas_call | solution.py:32
  44.1 4.2 %all-to-all-start.1 = ((bf16[4,384,256]{2,1,0:T(8,128)(2,1)}), bf16[4,384,256]{2,1,0:T(8,128)(2,1)}, u32[]{:S(2)}, u32[]{:S(2)}) async-start(bf16[4,384,256]{2,1,0:T(8,128)(2,1)} %shard_map.86), calls=%async_computation.1 | async-start | bytes 1572864 | tf_op jit(solution)/shard_map/all_to_all | solution.py:22
  48.3 0.7 bitcast_convert_fusion
  49.0 0.8 dynamic-slice_bitcast_fusion.1
  49.8 5.3 %collective-permute-start.7 = (f32[3,24,256]{2,1,0:T(8,128)S(1)}, f32[3,24,256]{2,1,0:T(8,128)}, u32[]{:S(2)}, u32[]{:S(2)}) collective-permute-start(f32[3,24,256]{2,1,0:T(8,128)S(1)} %pad_maximum_fusion), channel_id=1, source_target_pairs={{0,0},{1,64},{2,128},{3,192},{4,256},{5,320},{6,384},{7,448},{64,1... | collective-permute-start | bytes 221192 | tf_op jit(solution)/shard_map/ppermute | solution.py:99
  55.1 2.4 %collective-permute-done.7 = f32[3,24,256]{2,1,0:T(8,128)} collective-permute-done((f32[3,24,256]{2,1,0:T(8,128)S(1)}, f32[3,24,256]{2,1,0:T(8,128)}, u32[]{:S(2)}, u32[]{:S(2)}) %collective-permute-start.7) | collective-permute-done | bytes 73760 | tf_op jit(solution)/shard_map/ppermute | solution.py:99
  57.5 1.0 all-to-all-done.1
  58.5 1.3 convert_reduce_fusion
  59.8 0.1 fusion.1
  59.9 30.5 %all_to_all.30 = bf16[16,24,256]{2,1,0:T(8,128)(2,1)S(1)} all-to-all(bf16[16,24,256]{2,1,0:T(8,128)(2,1)S(1)} %bitcast.60), channel_id=1, replica_groups=mesh['zl'=8,'x'=4,'zh'=2,'y'=4,'core'=2] {'zl','zh'}, dimensions={0} | all-to-all | bytes 393216 | tf_op jit(solution)/shard_map/all_to_all | solution.py:22
  90.4 0.1 abs_reduce_fusion
  90.6 0.1 multiply_reduce_fusion
  90.7 0.8 fusion.10
  91.5 25.0 %all_to_all.31 = bf16[16,48,256]{2,1,0:T(8,128)(2,1)S(1)} all-to-all(bf16[16,48,256]{2,1,0:T(8,128)(2,1)S(1)} %broadcast_in_dim.35), channel_id=1, replica_groups=mesh['zl'=8,'x'=4,'zh'=2,'y'=4,'core'=2] {'zl','zh'}, dimensions={0} | all-to-all | bytes 786432 | tf_op jit(solution)/shard_map/all_to_all | solution.py:22
  116.5 0.9 broadcast_in_dim.37
  117.5 3.5 %all-to-all-start.4 = ((bf16[4,384,256]{2,1,0:T(8,128)(2,1)}), bf16[4,384,256]{2,1,0:T(8,128)(2,1)S(1)}, u32[]{:S(2)}, u32[]{:S(2)}) async-start(bf16[4,384,256]{2,1,0:T(8,128)(2,1)} %broadcast_in_dim.37), calls=%async_computation.4 | async-start | bytes 1572864 | tf_op jit(solution)/shard_map/all_to_all | solution.py:22
  121.0 8.3 %all-to-all-done.4 = bf16[4,384,256]{2,1,0:T(8,128)(2,1)S(1)} async-done(((bf16[4,384,256]{2,1,0:T(8,128)(2,1)}), bf16[4,384,256]{2,1,0:T(8,128)(2,1)S(1)}, u32[]{:S(2)}, u32[]{:S(2)}) %all-to-all-start.4) | async-done | bytes 786464 | tf_op jit(solution)/shard_map/all_to_all | solution.py:22
  129.3 2.5 %shard_map.87 = bf16[8,192,256]{2,1,0:T(8,128)(2,1)S(1)} custom-call(s32[8]{0:T(128)S(1)} %stack.50.member, bf16[160,1536]{1,0:T(8,128)(2,1)S(1)} %copy-done, bf16[160,1536]{1,0:T(8,128)(2,1)S(1)} %collective-permute-done.refs_1_, bf16[160,1536]{1,0:T(8,128)(2,1)S(1)} %collective-permute-done.1.refs_2_, ...), custom_call_target="tpu_custom_call" | custom-call | tf_op jit(solution)/shard_map/pallas_call | solution.py:32
  131.8 27.3 %all_to_all.32 = bf16[8,192,256]{2,1,0:T(8,128)(2,1)S(1)} all-to-all(bf16[8,192,256]{2,1,0:T(8,128)(2,1)S(1)} %shard_map.87), channel_id=1, replica_groups=mesh['zl'=8,'x'=4,'zh'=2,'y'=4,'core'=2] {'y','core'}, dimensions={0} | all-to-all | bytes 1572864 | tf_op jit(solution)/shard_map/all_to_all | solution.py:22
  159.2 0.0 copy-start.3
  159.2 0.0 copy-start.4
  159.2 0.9 copy.19
  160.2 0.0 copy-done.3
  160.2 0.2 copy-done.4
  160.4 0.8 fusion
  (15 shorter events, 0.2 us)
Async XLA Ops:
  0.6 25.1 %collective-permute-start.2 = (bf16[160,1536]{1,0:T(8,128)(2,1)}, bf16[160,1536]{1,0:T(8,128)(2,1)S(1)}, u32[]{:S(2)}, u32[]{:S(2)}) collective-permute-start(bf16[160,1536]{1,0:T(8,128)(2,1)} %refs_0_.3), channel_id=1, source_target_pairs={{0,6},{2,0},{4,2},{6,4},{1,7},{3,1},{5,3},{7,5},{8,14},{10,8},{12,... | collective-permute-start | bytes 1474568 | tf_op jit(solution)/shard_map/ppermute | solution.py:27
  6.1 26.7 %collective-permute-start.1 = (bf16[160,1536]{1,0:T(8,128)(2,1)}, bf16[160,1536]{1,0:T(8,128)(2,1)S(1)}, u32[]{:S(2)}, u32[]{:S(2)}) collective-permute-start(bf16[160,1536]{1,0:T(8,128)(2,1)} %refs_0_.3), channel_id=1, source_target_pairs={{0,4},{2,6},{4,0},{6,2},{1,5},{3,7},{5,1},{7,3},{8,12},{10,14},{12... | collective-permute-start | bytes 1474568 | tf_op jit(solution)/shard_map/ppermute | solution.py:27
  8.4 26.4 %collective-permute-start = (bf16[160,1536]{1,0:T(8,128)(2,1)}, bf16[160,1536]{1,0:T(8,128)(2,1)S(1)}, u32[]{:S(2)}, u32[]{:S(2)}) collective-permute-start(bf16[160,1536]{1,0:T(8,128)(2,1)} %refs_0_.3), channel_id=1, source_target_pairs={{0,2},{2,4},{4,6},{6,0},{1,3},{3,5},{5,7},{7,1},{8,10},{10,12},{12... | collective-permute-start | bytes 1474568 | tf_op jit(solution)/shard_map/ppermute | solution.py:27
  11.0 1.1 copy-start.1
  12.1 0.9 copy-start.2
  14.0 9.8 %copy-start = (bf16[160,1536]{1,0:T(8,128)(2,1)S(1)}, bf16[160,1536]{1,0:T(8,128)(2,1)}, u32[]{:S(2)}) copy-start(bf16[160,1536]{1,0:T(8,128)(2,1)} %refs_0_.3) | copy-start | bytes 1474564
  14.0 26.7 %all-to-all-start = ((bf16[8,192,256]{2,1,0:T(8,128)(2,1)}), bf16[8,192,256]{2,1,0:T(8,128)(2,1)S(1)}, u32[]{:S(2)}, u32[]{:S(2)}) async-start(bf16[8,192,256]{2,1,0:T(8,128)(2,1)} %shard_map.85), calls=%async_computation | async-start | bytes 1572864 | tf_op jit(solution)/shard_map/all_to_all | solution.py:22
  23.8 13.5 %collective-permute-start.3 = (bf16[160,1536]{1,0:T(8,128)(2,1)S(1)}, bf16[160,1536]{1,0:T(8,128)(2,1)S(1)}, u32[]{:S(2)}, u32[]{:S(2)}) collective-permute-start(bf16[160,1536]{1,0:T(8,128)(2,1)S(1)} %copy-done), channel_id=1, source_target_pairs={{0,1},{1,0},{2,3},{3,2},{4,5},{5,4},{6,7},{7,6},{8,9},{9,8},{10,11... | collective-permute-start | bytes 1474568 | tf_op jit(solution)/shard_map/ppermute | solution.py:85
  25.7 14.9 %collective-permute-start.6 = (bf16[160,1536]{1,0:T(8,128)(2,1)S(1)}, bf16[160,1536]{1,0:T(8,128)(2,1)}, u32[]{:S(2)}, u32[]{:S(2)}) collective-permute-start(bf16[160,1536]{1,0:T(8,128)(2,1)S(1)} %collective-permute-done.2.refs_3_), channel_id=1, source_target_pairs={{0,1},{1,0},{2,3},{3,2},{4,5},{5,4},{6,7},{7,6},{8,9},{9,8},{10,11... | collective-permute-start | bytes 1474568 | tf_op jit(solution)/shard_map/ppermute | solution.py:85
  32.8 7.8 %collective-permute-start.5 = (bf16[160,1536]{1,0:T(8,128)(2,1)S(1)}, bf16[160,1536]{1,0:T(8,128)(2,1)}, u32[]{:S(2)}, u32[]{:S(2)}) collective-permute-start(bf16[160,1536]{1,0:T(8,128)(2,1)S(1)} %collective-permute-done.1.refs_2_), channel_id=1, source_target_pairs={{0,1},{1,0},{2,3},{3,2},{4,5},{5,4},{6,7},{7,6},{8,9},{9,8},{10,11... | collective-permute-start | bytes 1474568 | tf_op jit(solution)/shard_map/ppermute | solution.py:85
  34.8 5.8 %collective-permute-start.4 = (bf16[160,1536]{1,0:T(8,128)(2,1)S(1)}, bf16[160,1536]{1,0:T(8,128)(2,1)}, u32[]{:S(2)}, u32[]{:S(2)}) collective-permute-start(bf16[160,1536]{1,0:T(8,128)(2,1)S(1)} %collective-permute-done.refs_1_), channel_id=1, source_target_pairs={{0,1},{1,0},{2,3},{3,2},{4,5},{5,4},{6,7},{7,6},{8,9},{9,8},{10,11... | collective-permute-start | bytes 1474568 | tf_op jit(solution)/shard_map/ppermute | solution.py:85
  44.1 14.4 %all-to-all-start.1 = ((bf16[4,384,256]{2,1,0:T(8,128)(2,1)}), bf16[4,384,256]{2,1,0:T(8,128)(2,1)}, u32[]{:S(2)}, u32[]{:S(2)}) async-start(bf16[4,384,256]{2,1,0:T(8,128)(2,1)} %shard_map.86), calls=%async_computation.1 | async-start | bytes 1572864 | tf_op jit(solution)/shard_map/all_to_all | solution.py:22
  49.8 7.7 %collective-permute-start.7 = (f32[3,24,256]{2,1,0:T(8,128)S(1)}, f32[3,24,256]{2,1,0:T(8,128)}, u32[]{:S(2)}, u32[]{:S(2)}) collective-permute-start(f32[3,24,256]{2,1,0:T(8,128)S(1)} %pad_maximum_fusion), channel_id=1, source_target_pairs={{0,0},{1,64},{2,128},{3,192},{4,256},{5,320},{6,384},{7,448},{64,1... | collective-permute-start | bytes 221192 | tf_op jit(solution)/shard_map/ppermute | solution.py:99
  117.5 11.8 %all-to-all-start.4 = ((bf16[4,384,256]{2,1,0:T(8,128)(2,1)}), bf16[4,384,256]{2,1,0:T(8,128)(2,1)S(1)}, u32[]{:S(2)}, u32[]{:S(2)}) async-start(bf16[4,384,256]{2,1,0:T(8,128)(2,1)} %broadcast_in_dim.37), calls=%async_computation.4 | async-start | bytes 1572864 | tf_op jit(solution)/shard_map/all_to_all | solution.py:22
  159.2 1.0 copy-start.3
  159.2 1.2 copy-start.4

commit v6 on v5

v6 whole, which is shorter than its diff:
```python
import functools

import jax
import jax.numpy as jnp
from jax import lax
from jax.experimental import pallas as pl
from jax.experimental.pallas import tpu as pltpu
from jax.sharding import Mesh, PartitionSpec as P

HEAD_SIZE = 256
BF16 = jnp.bfloat16
F32 = jnp.float32


def moments(grad, first, second):
    return 0.9 * first + 0.1 * grad, 0.95 * second + 0.05 * grad * grad


def updated(grad, first, second, weight):
    new_first, new_second = moments(grad, first, second)
    update = new_first / (1.0 - 0.9**10) / (jnp.sqrt(new_second / (1.0 - 0.95**10)) + 1e-08)
    new_weight = weight * (1.0 - 0.002 * 0.1) - 0.002 * update
    return new_weight


def exchange(pieces, axes):
    return lax.all_to_all(pieces, axes, split_axis=0, concat_axis=0, tiled=True)


def shift(a, axis, k):
    n = lax.axis_size(axis)
    return lax.ppermute(a, axis, [(i, (i + k) % n) for i in range(n)])


def call(body, shapes, *args, scratch=(), hbm=False):
    spaces = [pltpu.SMEM if a.dtype == jnp.int32 else pltpu.HBM if hbm else pltpu.VMEM for a in args]
    out = pl.BlockSpec(memory_space=pltpu.HBM if hbm else pltpu.VMEM)
    return pl.pallas_call(
        body,
        out_shape=shapes,
        in_specs=[pl.BlockSpec(memory_space=m) for m in spaces],
        out_specs=jax.tree.map(lambda _: out, shapes),
        scratch_shapes=scratch,
        compiler_params=pltpu.CompilerParams(vmem_limit_bytes=32 << 20),
    )(*args)


def split_heads(cot, residue, out, residue_here, rounded, copy_sem, residue_sem, out_sem):
    heads, rows, size = out.shape
    tok, own = cot.shape[0], residue.shape[0]
    load = pltpu.make_async_copy(residue, residue_here, residue_sem)
    load.start()
    copies = []
    for h in range(heads):
        source, target = cot.at[:, pl.ds(h * size, size)], out.at[h, pl.ds(0, tok)]
        copies.append(pltpu.make_async_copy(source, target, copy_sem.at[h]))
        copies[-1].start()
    load.wait()
    zeros = jnp.zeros((rows - tok - own, size), F32)
    for h in range(heads):
        block = residue_here[:, h * size : (h + 1) * size]
        rounded[h] = jnp.concatenate([block, zeros], axis=0).astype(BF16)
    copies.append(pltpu.make_async_copy(rounded, out.at[:, pl.ds(tok, rows - tok)], out_sem))
    copies[-1].start()
    for copy in copies:
        copy.wait()


def head_term(own, places, *refs):
    *acts, cot, out = refs
    tok = acts[0].shape[0]
    blocks, rows, _ = out.shape
    heads = cot.shape[0]
    head_cot = jnp.concatenate([cot[places[j], :tok, :] for j in range(len(acts))], axis=0)
    residue = [cot[h, tok:, :].astype(F32)[:own] for h in range(heads)]
    residue = jnp.concatenate(residue, axis=0)
    part = heads * own
    for i in range(blocks):
        act = jnp.concatenate([a[:, i * rows : (i + 1) * rows] for a in acts], axis=0)
        term = lax.dot_general(act, head_cot, (((0,), (0,)), ((), ())), preferred_element_type=F32)
        for k in range(rows // part):
            mine = jnp.logical_and(places[len(acts)] == i, places[len(acts) + 1] == k)
            at = slice(k * part, (k + 1) * part)
            out[i, at, :] = (term[at] + jnp.where(mine, 1.0, 0.0) * residue).astype(BF16)


def sum_blocks(arrived, out):
    total = arrived[0].astype(F32)
    for i in range(1, arrived.shape[0]):
        total = total + arrived[i].astype(F32)
    members, rows, _ = out.shape
    part = total.shape[0] // 2
    own = rows // 2
    for m in range(members):
        low, high = m * own, part + m * own
        block = jnp.concatenate([total[low : low + own], total[high : high + own]], axis=0)
        out[m] = block.astype(BF16)


def update_rows(parts, states, out):
    own = states.shape[1]
    grad = None
    for c in range(parts.shape[0]):
        both = parts[c].astype(F32)
        combined = both[:own] + both[own:]
        scale = jnp.max(jnp.abs(combined), axis=-1, keepdims=True) + 1e-06
        scale = scale.astype(BF16).astype(F32)
        decoded = (combined / scale).astype(BF16).astype(F32) * scale
        grad = decoded if grad is None else grad + decoded
    weight = updated(grad, states[0], states[1], states[2])
    block = jnp.concatenate([weight, grad], axis=0).astype(BF16)
    for i in range(out.shape[0]):
        out[i] = block


def project(places, *refs):
    *acts, weight, grad, out = refs
    tok = acts[0].shape[0]
    for j, a in enumerate(acts):
        block = jnp.dot(a[...], weight[...], preferred_element_type=F32)
        out[places[j], :tok, :] = block.astype(BF16)
    out[:, tok:, :] = grad[...]


def finish(back, first, second, projected, new_first, new_second):
    heads, _, size = back.shape
    tok, own = projected.shape[0], first.shape[0]
    for h in range(heads):
        at = slice(h * size, (h + 1) * size)
        projected[:, at] = back[h, :tok, :]
        grad = back[h, tok:, :].astype(F32)[:own]
        new_first[:, at], new_second[:, at] = moments(grad, first[:, at], second[:, at])


def relay(act, cot, weight, first, second, residue):
    nx, ny, nz, nzh = (lax.axis_size(a) for a in ("x", "y", "zl", "zh"))
    core, x, y, zh, zl = (lax.axis_index(a) for a in ("core", "x", "y", "zh", "zl"))
    tok, depth = act.shape
    own = weight.shape[0]
    group = ("y", "core")
    swap = [(0, 1), (1, 0)]

    near = [act] + [shift(act, "y", k) for k in range(1, ny)]
    acts = near + [lax.ppermute(a, "core", swap) for a in near]

    block = -(-(tok + own) // 16) * 16
    dma = pltpu.SemaphoreType.DMA
    pieces = call(
        split_heads,
        jax.ShapeDtypeStruct((nz, block, HEAD_SIZE), BF16),
        cot,
        residue[0],
        scratch=(
            pltpu.VMEM(residue.shape[1:], F32),
            pltpu.VMEM((nz, block - tok, HEAD_SIZE), BF16),
            dma((nz,)),
            dma,
            dma,
        ),
        hbm=True,
    )
    got = exchange(pieces, group)

    def columns(a):
        return lax.dynamic_slice_in_dim(a, zl * HEAD_SIZE, HEAD_SIZE, 1)

    states = jnp.stack([columns(first), columns(second), columns(weight).astype(F32)])
    turn = [(a * nz + b, b * nz + a) for a in range(nz) for b in range(nz)]
    states = lax.ppermute(states, ("zl", "y", "core"), turn)

    steps = [(k, m) for m in (core, 1 - core) for k in range(ny)]
    places = jnp.stack([2 * lax.rem(y + ny - k, ny) + m for k, m in steps] + [x, zh])
    places = places.astype(jnp.int32)
    rows = depth // nx
    term = jax.ShapeDtypeStruct((nx, rows, HEAD_SIZE), BF16)
    term = call(functools.partial(head_term, own), term, places, *acts, got)

    arrived = exchange(term, "x")
    arrived, states = lax.optimization_barrier((arrived, states))
    part = call(sum_blocks, jax.ShapeDtypeStruct((nz, nzh * own, HEAD_SIZE), BF16), arrived)

    parts = exchange(part.reshape(nz * nzh, own, HEAD_SIZE), ("zl", "zh"))
    packed = jax.ShapeDtypeStruct((nz * nzh, 2 * own, HEAD_SIZE), BF16)
    packed = call(update_rows, packed, parts.reshape(nz, nzh * own, HEAD_SIZE), states)

    packed, upper = lax.optimization_barrier((packed, zh > 0))
    packed = exchange(packed, ("zl", "zh")).reshape(nz, nzh, 2, own, HEAD_SIZE)
    row_grad = jnp.where(upper, packed[:, 1, 1], packed[:, 0, 1])
    row_grad = jnp.pad(row_grad, ((0, 0), (0, block - tok - own), (0, 0)))
    sent = packed[:, :, 0].transpose(1, 0, 2, 3).reshape(rows, HEAD_SIZE)
    sent = jnp.broadcast_to(sent[None], (nx, rows, HEAD_SIZE))
    sent, row_grad = lax.optimization_barrier((sent, row_grad))
    head_weight = exchange(sent, "x").reshape(depth, HEAD_SIZE)

    out = jax.ShapeDtypeStruct((nz, block, HEAD_SIZE), BF16)
    out = call(project, out, places, *acts, head_weight, row_grad)
    back = exchange(out, group)
    state = jax.ShapeDtypeStruct(first.shape, F32)
    shapes = (jax.ShapeDtypeStruct(cot.shape, BF16), state, state)
    return tuple(call(finish, shapes, back, first, second))


def solution(mesh):
    names = ("zl", "x", "zh", "y", "core")
    fine = Mesh(mesh.devices.reshape(8, 4, 2, 4, 2), names)
    fsdp = ("x", "zh", "y", "core")
    by_token, by_row = P(names, None), P(fsdp, None)
    in_specs = (by_token, by_token, by_row, by_row, by_row, P("zl", fsdp, None))
    out_specs = (by_token, by_row, by_row)
    return jax.shard_map(relay, mesh=fine, in_specs=in_specs, out_specs=out_specs, check_vma=False)
```

time: 164 us -> 160 us (0.976)
  blocking collectives: 82.8 us -> 63.9 us
  starting transfers between devices: 46.4 us -> 59.6 us
  waiting for transfers between devices: 15 us -> 20.4 us
  other arithmetic: 3.99 us -> 0.73 us
  Pallas kernels: 6.96 us -> 9.21 us
  local copies, waits for them, and re-layouts: 5.12 us -> 2.94 us
    all_to_all x3, blocking collectives: 82.8 us -> 63.9 us  [exchange(): return lax.all_to_all(pieces, axes, split_axis=0, concat_axis=0, tiled=True)]
    all_to_all x3, starting transfers between devices: 17.5 us -> 30.7 us  [exchange(): return lax.all_to_all(pieces, axes, split_axis=0, concat_axis=0, tiled=True)]
    all_to_all x3, waiting for transfers between devices: 12.6 us -> 18.1 us  [exchange(): return lax.all_to_all(pieces, axes, split_axis=0, concat_axis=0, tiled=True)]
    pallas_call x3 -> x6, Pallas kernels: 6.96 us -> 9.21 us  [call(): pl.pallas_call(body, out_shape=shapes, in_specs=[pl.BlockSpec(memory_spac...]
where the time goes in v6:
time: 160 us; the launch traced here: 158 us
  blocking collectives  63.9 us (40%)
  starting transfers between devices  59.6 us (37%)
  waiting for transfers between devices  20.4 us (13%)
  Pallas kernels  9.21 us (6%)
  local copies, waits for them, and re-layouts  2.94 us (2%)
    all_to_all x3, blocking collectives, exchange(): return lax.all_to_all(pieces, axes, split_axis=0, concat_axis=0, tiled=True)  63.9 us
    all_to_all x3, starting transfers between devices, exchange(): return lax.all_to_all(pieces, axes, split_axis=0, concat_axis=0, tiled=True)  30.7 us
    all_to_all x3, waiting for transfers between devices, exchange(): return lax.all_to_all(pieces, axes, split_axis=0, concat_axis=0, tiled=True)  18.1 us
    ppermute x4, starting transfers between devices, relay(): acts = near + [lax.ppermute(a, 'core', swap) for a in near]  13 us
    ppermute x3, starting transfers between devices, shift(): return lax.ppermute(a, axis, [(i, (i + k) % n) for i in range(n)])  10.3 us
    pallas_call x6, Pallas kernels, call(): pl.pallas_call(body, out_shape=shapes, in_specs=[pl.BlockSpec(memory_spac...  9.21 us
    ppermute x1, starting transfers between devices, relay(): states = lax.ppermute(states, ('zl', 'y', 'core'), turn)  5.45 us
  transfers between devices with their start and end apart: 11, of which 4 were waited for; matrix products, arithmetic and copies ran while one was open for 1% of the time, Pallas kernels for 1%

profile of v6, /device:TPU:1, one launch (start us, length us, event | category | flops | bytes accessed | tf_op | source)
XLA Modules:
  0.0 157.6 jit_solution(91543444850787517)
XLA Ops:
  0.6 5.5 %collective-permute-start.2 = (bf16[160,1536]{1,0:T(8,128)(2,1)}, bf16[160,1536]{1,0:T(8,128)(2,1)S(1)}, u32[]{:S(2)}, u32[]{:S(2)}) collective-permute-start(bf16[160,1536]{1,0:T(8,128)(2,1)} %refs_0_.3), channel_id=1, source_target_pairs={{0,6},{2,0},{4,2},{6,4},{1,7},{3,1},{5,3},{7,5},{8,14},{10,8},{12,... | collective-permute-start | bytes 1474568 | tf_op jit(solution)/shard_map/ppermute | solution.py:32
  6.1 2.3 %collective-permute-start.1 = (bf16[160,1536]{1,0:T(8,128)(2,1)}, bf16[160,1536]{1,0:T(8,128)(2,1)S(1)}, u32[]{:S(2)}, u32[]{:S(2)}) collective-permute-start(bf16[160,1536]{1,0:T(8,128)(2,1)} %refs_0_.3), channel_id=1, source_target_pairs={{0,4},{2,6},{4,0},{6,2},{1,5},{3,7},{5,1},{7,3},{8,12},{10,14},{12... | collective-permute-start | bytes 1474568 | tf_op jit(solution)/shard_map/ppermute | solution.py:32
  8.4 2.6 %collective-permute-start = (bf16[160,1536]{1,0:T(8,128)(2,1)}, bf16[160,1536]{1,0:T(8,128)(2,1)S(1)}, u32[]{:S(2)}, u32[]{:S(2)}) collective-permute-start(bf16[160,1536]{1,0:T(8,128)(2,1)} %refs_0_.3), channel_id=1, source_target_pairs={{0,2},{2,4},{4,6},{6,0},{1,3},{3,5},{5,7},{7,1},{8,10},{10,12},{12... | collective-permute-start | bytes 1474568 | tf_op jit(solution)/shard_map/ppermute | solution.py:32
  11.0 0.0 copy-start.1
  11.0 1.1 copy-done.1
  12.1 0.0 copy-start.4
  12.1 0.9 copy-done.4
  13.0 1.2 shard_map.85
  14.2 0.0 copy-start
  14.2 9.9 %all-to-all-start = ((bf16[8,192,256]{2,1,0:T(8,128)(2,1)}), bf16[8,192,256]{2,1,0:T(8,128)(2,1)S(1)}, u32[]{:S(2)}, u32[]{:S(2)}) async-start(bf16[8,192,256]{2,1,0:T(8,128)(2,1)} %shard_map.85), calls=%async_computation | async-start | bytes 1572864 | tf_op jit(solution)/shard_map/all_to_all | solution.py:27
  24.1 0.0 copy-done
  24.1 1.9 %collective-permute-start.3 = (bf16[160,1536]{1,0:T(8,128)(2,1)S(1)}, bf16[160,1536]{1,0:T(8,128)(2,1)S(1)}, u32[]{:S(2)}, u32[]{:S(2)}) collective-permute-start(bf16[160,1536]{1,0:T(8,128)(2,1)S(1)} %copy-done), channel_id=1, source_target_pairs={{0,1},{1,0},{2,3},{3,2},{4,5},{5,4},{6,7},{7,6},{8,9},{9,8},{10,11... | collective-permute-start | bytes 1474568 | tf_op jit(solution)/shard_map/ppermute | solution.py:144
  26.0 0.0 collective-permute-done.2.refs_3_
  26.0 6.8 %collective-permute-start.6 = (bf16[160,1536]{1,0:T(8,128)(2,1)S(1)}, bf16[160,1536]{1,0:T(8,128)(2,1)}, u32[]{:S(2)}, u32[]{:S(2)}) collective-permute-start(bf16[160,1536]{1,0:T(8,128)(2,1)S(1)} %collective-permute-done.2.refs_3_), channel_id=1, source_target_pairs={{0,1},{1,0},{2,3},{3,2},{4,5},{5,4},{6,7},{7,6},{8,9},{9,8},{10,11... | collective-permute-start | bytes 1474568 | tf_op jit(solution)/shard_map/ppermute | solution.py:144
  32.8 0.0 collective-permute-done.1.refs_2_
  32.8 1.9 %collective-permute-start.5 = (bf16[160,1536]{1,0:T(8,128)(2,1)S(1)}, bf16[160,1536]{1,0:T(8,128)(2,1)}, u32[]{:S(2)}, u32[]{:S(2)}) collective-permute-start(bf16[160,1536]{1,0:T(8,128)(2,1)S(1)} %collective-permute-done.1.refs_2_), channel_id=1, source_target_pairs={{0,1},{1,0},{2,3},{3,2},{4,5},{5,4},{6,7},{7,6},{8,9},{9,8},{10,11... | collective-permute-start | bytes 1474568 | tf_op jit(solution)/shard_map/ppermute | solution.py:144
  34.8 0.0 collective-permute-done.refs_1_
  34.8 2.4 %collective-permute-start.4 = (bf16[160,1536]{1,0:T(8,128)(2,1)S(1)}, bf16[160,1536]{1,0:T(8,128)(2,1)}, u32[]{:S(2)}, u32[]{:S(2)}) collective-permute-start(bf16[160,1536]{1,0:T(8,128)(2,1)S(1)} %collective-permute-done.refs_1_), channel_id=1, source_target_pairs={{0,1},{1,0},{2,3},{3,2},{4,5},{5,4},{6,7},{7,6},{8,9},{9,8},{10,11... | collective-permute-start | bytes 1474568 | tf_op jit(solution)/shard_map/ppermute | solution.py:144
  37.2 0.1 stack.58.places
  37.3 0.0 collective-permute-done.3.refs_4_
  37.3 3.3 %all-to-all-done.refs_8_ = bf16[8,192,256]{2,1,0:T(8,128)(2,1)S(1)} async-done(((bf16[8,192,256]{2,1,0:T(8,128)(2,1)}), bf16[8,192,256]{2,1,0:T(8,128)(2,1)S(1)}, u32[]{:S(2)}, u32[]{:S(2)}) %all-to-all-start) | async-done | bytes 786464 | tf_op jit(solution)/shard_map/all_to_all | solution.py:27
  40.6 0.0 collective-permute-done.6.refs_7_
  40.6 0.0 collective-permute-done.5.refs_6_
  40.6 0.0 collective-permute-done.4.refs_5_
  40.6 3.5 %shard_map.86 = bf16[4,384,256]{2,1,0:T(8,128)(2,1)} custom-call(s32[10]{0:T(128)S(1)} %stack.58.places, bf16[160,1536]{1,0:T(8,128)(2,1)S(1)} %copy-done, bf16[160,1536]{1,0:T(8,128)(2,1)S(1)} %collective-permute-done.refs_1_, bf16[160,1536]{1,0:T(8,128)(2,1)S(1)} %collective-permute-done.1.refs_2_, bf16[160,1536]{1,0:T(8,128)(2,1)S(1)} %collective-permute-done.2.refs_3_, ...), custom_call_target="tpu_custom_call" | custom-call | tf_op jit(solution)/shard_map/pallas_call | solution.py:38
  44.1 0.0 copy-start.2
  44.1 4.1 %all-to-all-start.1 = ((bf16[4,384,256]{2,1,0:T(8,128)(2,1)}), bf16[4,384,256]{2,1,0:T(8,128)(2,1)S(1)}, u32[]{:S(2)}, u32[]{:S(2)}) async-start(bf16[4,384,256]{2,1,0:T(8,128)(2,1)} %shard_map.86), calls=%async_computation.1 | async-start | bytes 1572864 | tf_op jit(solution)/shard_map/all_to_all | solution.py:27
  48.2 0.7 bitcast_convert_fusion
  48.9 0.0 copy-done.2
  48.9 0.7 dynamic-slice_bitcast_fusion
  49.7 5.5 %collective-permute-start.7 = (f32[3,24,256]{2,1,0:T(8,128)S(1)}, f32[3,24,256]{2,1,0:T(8,128)S(1)}, u32[]{:S(2)}, u32[]{:S(2)}) collective-permute-start(f32[3,24,256]{2,1,0:T(8,128)S(1)} %pad_maximum_fusion), channel_id=1, source_target_pairs={{0,0},{1,64},{2,128},{3,192},{4,256},{5,320},{6,384},{7,448},{64,1... | collective-permute-start | bytes 221192 | tf_op jit(solution)/shard_map/ppermute | solution.py:169
  55.2 2.3 %collective-permute-done.7.states = f32[3,24,256]{2,1,0:T(8,128)S(1)} collective-permute-done((f32[3,24,256]{2,1,0:T(8,128)S(1)}, f32[3,24,256]{2,1,0:T(8,128)S(1)}, u32[]{:S(2)}, u32[]{:S(2)}) %collective-permute-start.7) | collective-permute-done | bytes 73760 | tf_op jit(solution)/shard_map/ppermute | solution.py:169
  57.5 0.8 all-to-all-done.1.arrived
  58.2 0.8 shard_map.87
  59.0 16.7 %all-to-all-start.2 = ((bf16[16,24,256]{2,1,0:T(8,128)(2,1)}), bf16[16,24,256]{2,1,0:T(8,128)(2,1)S(1)}, u32[]{:S(2)}, u32[]{:S(2)}) async-start(bf16[16,24,256]{2,1,0:T(8,128)(2,1)} %bitcast.14), calls=%async_computation.2 | async-start | bytes 393216 | tf_op jit(solution)/shard_map/all_to_all | solution.py:27
  75.8 14.0 %all-to-all-done.2 = bf16[16,24,256]{2,1,0:T(8,128)(2,1)S(1)} async-done(((bf16[16,24,256]{2,1,0:T(8,128)(2,1)}), bf16[16,24,256]{2,1,0:T(8,128)(2,1)S(1)}, u32[]{:S(2)}, u32[]{:S(2)}) %all-to-all-start.2) | async-done | bytes 196640 | tf_op jit(solution)/shard_map/all_to_all | solution.py:27
  89.8 0.2 shard_map.88
  89.9 21.6 %all_to_all.30 = bf16[16,48,256]{2,1,0:T(8,128)(2,1)S(1)} all-to-all(bf16[16,48,256]{2,1,0:T(8,128)(2,1)S(1)} %shard_map.88), channel_id=1, replica_groups=mesh['zl'=8,'x'=4,'zh'=2,'y'=4,'core'=2] {'zl','zh'}, dimensions={0} | all-to-all | bytes 786432 | tf_op jit(solution)/shard_map/all_to_all | solution.py:27
  111.6 0.1 broadcast_in_dim.8
  111.6 10.7 %all_to_all.31 = bf16[4,384,256]{2,1,0:T(8,128)(2,1)S(1)} all-to-all(bf16[4,384,256]{2,1,0:T(8,128)(2,1)S(1)} %broadcast_in_dim.8), channel_id=1, replica_groups=mesh['zl'=8,'x'=4,'zh'=2,'y'=4,'core'=2] {'x'}, dimensions={0} | all-to-all | bytes 1572864 | tf_op jit(solution)/shard_map/all_to_all | solution.py:27
  122.4 2.5 %shard_map.89 = bf16[8,192,256]{2,1,0:T(8,128)(2,1)S(1)} custom-call(s32[10]{0:T(128)S(1)} %stack.58.places, bf16[160,1536]{1,0:T(8,128)(2,1)S(1)} %copy-done, bf16[160,1536]{1,0:T(8,128)(2,1)S(1)} %collective-permute-done.refs_1_, bf16[160,1536]{1,0:T(8,128)(2,1)S(1)} %collective-permute-done.1.refs_2_, ...), custom_call_target="tpu_custom_call" | custom-call | tf_op jit(solution)/shard_map/pallas_call | solution.py:38
  124.9 0.0 copy-start.3
  124.9 31.6 %all_to_all.32.back = bf16[8,192,256]{2,1,0:T(8,128)(2,1)S(1)} all-to-all(bf16[8,192,256]{2,1,0:T(8,128)(2,1)S(1)} %shard_map.89), channel_id=1, replica_groups=mesh['zl'=8,'x'=4,'zh'=2,'y'=4,'core'=2] {'y','core'}, dimensions={0} | all-to-all | bytes 1572864 | tf_op jit(solution)/shard_map/all_to_all | solution.py:27
  156.5 0.0 copy-done.3
  156.5 1.1 shard_map.90
  (5 shorter events, 0.1 us)
Async XLA Ops:
  0.6 25.4 %collective-permute-start.2 = (bf16[160,1536]{1,0:T(8,128)(2,1)}, bf16[160,1536]{1,0:T(8,128)(2,1)S(1)}, u32[]{:S(2)}, u32[]{:S(2)}) collective-permute-start(bf16[160,1536]{1,0:T(8,128)(2,1)} %refs_0_.3), channel_id=1, source_target_pairs={{0,6},{2,0},{4,2},{6,4},{1,7},{3,1},{5,3},{7,5},{8,14},{10,8},{12,... | collective-permute-start | bytes 1474568 | tf_op jit(solution)/shard_map/ppermute | solution.py:32
  6.1 26.7 %collective-permute-start.1 = (bf16[160,1536]{1,0:T(8,128)(2,1)}, bf16[160,1536]{1,0:T(8,128)(2,1)S(1)}, u32[]{:S(2)}, u32[]{:S(2)}) collective-permute-start(bf16[160,1536]{1,0:T(8,128)(2,1)} %refs_0_.3), channel_id=1, source_target_pairs={{0,4},{2,6},{4,0},{6,2},{1,5},{3,7},{5,1},{7,3},{8,12},{10,14},{12... | collective-permute-start | bytes 1474568 | tf_op jit(solution)/shard_map/ppermute | solution.py:32
  8.4 26.4 %collective-permute-start = (bf16[160,1536]{1,0:T(8,128)(2,1)}, bf16[160,1536]{1,0:T(8,128)(2,1)S(1)}, u32[]{:S(2)}, u32[]{:S(2)}) collective-permute-start(bf16[160,1536]{1,0:T(8,128)(2,1)} %refs_0_.3), channel_id=1, source_target_pairs={{0,2},{2,4},{4,6},{6,0},{1,3},{3,5},{5,7},{7,1},{8,10},{10,12},{12... | collective-permute-start | bytes 1474568 | tf_op jit(solution)/shard_map/ppermute | solution.py:32
  11.0 1.1 copy-start.1
  12.1 0.9 copy-start.4
  14.2 9.9 %copy-start = (bf16[160,1536]{1,0:T(8,128)(2,1)S(1)}, bf16[160,1536]{1,0:T(8,128)(2,1)}, u32[]{:S(2)}) copy-start(bf16[160,1536]{1,0:T(8,128)(2,1)} %refs_0_.3) | copy-start | bytes 1474564
  14.2 26.4 %all-to-all-start = ((bf16[8,192,256]{2,1,0:T(8,128)(2,1)}), bf16[8,192,256]{2,1,0:T(8,128)(2,1)S(1)}, u32[]{:S(2)}, u32[]{:S(2)}) async-start(bf16[8,192,256]{2,1,0:T(8,128)(2,1)} %shard_map.85), calls=%async_computation | async-start | bytes 1572864 | tf_op jit(solution)/shard_map/all_to_all | solution.py:27
  24.1 13.2 %collective-permute-start.3 = (bf16[160,1536]{1,0:T(8,128)(2,1)S(1)}, bf16[160,1536]{1,0:T(8,128)(2,1)S(1)}, u32[]{:S(2)}, u32[]{:S(2)}) collective-permute-start(bf16[160,1536]{1,0:T(8,128)(2,1)S(1)} %copy-done), channel_id=1, source_target_pairs={{0,1},{1,0},{2,3},{3,2},{4,5},{5,4},{6,7},{7,6},{8,9},{9,8},{10,11... | collective-permute-start | bytes 1474568 | tf_op jit(solution)/shard_map/ppermute | solution.py:144
  26.0 14.6 %collective-permute-start.6 = (bf16[160,1536]{1,0:T(8,128)(2,1)S(1)}, bf16[160,1536]{1,0:T(8,128)(2,1)}, u32[]{:S(2)}, u32[]{:S(2)}) collective-permute-start(bf16[160,1536]{1,0:T(8,128)(2,1)S(1)} %collective-permute-done.2.refs_3_), channel_id=1, source_target_pairs={{0,1},{1,0},{2,3},{3,2},{4,5},{5,4},{6,7},{7,6},{8,9},{9,8},{10,11... | collective-permute-start | bytes 1474568 | tf_op jit(solution)/shard_map/ppermute | solution.py:144
  32.8 7.8 %collective-permute-start.5 = (bf16[160,1536]{1,0:T(8,128)(2,1)S(1)}, bf16[160,1536]{1,0:T(8,128)(2,1)}, u32[]{:S(2)}, u32[]{:S(2)}) collective-permute-start(bf16[160,1536]{1,0:T(8,128)(2,1)S(1)} %collective-permute-done.1.refs_2_), channel_id=1, source_target_pairs={{0,1},{1,0},{2,3},{3,2},{4,5},{5,4},{6,7},{7,6},{8,9},{9,8},{10,11... | collective-permute-start | bytes 1474568 | tf_op jit(solution)/shard_map/ppermute | solution.py:144
  34.8 5.8 %collective-permute-start.4 = (bf16[160,1536]{1,0:T(8,128)(2,1)S(1)}, bf16[160,1536]{1,0:T(8,128)(2,1)}, u32[]{:S(2)}, u32[]{:S(2)}) collective-permute-start(bf16[160,1536]{1,0:T(8,128)(2,1)S(1)} %collective-permute-done.refs_1_), channel_id=1, source_target_pairs={{0,1},{1,0},{2,3},{3,2},{4,5},{5,4},{6,7},{7,6},{8,9},{9,8},{10,11... | collective-permute-start | bytes 1474568 | tf_op jit(solution)/shard_map/ppermute | solution.py:144
  44.1 4.9 %copy-start.2 = (f32[24,2048]{1,0:T(8,128)S(1)}, f32[24,2048]{1,0:T(8,128)}, u32[]{:S(2)}) copy-start(f32[24,2048]{1,0:T(8,128)} %second.1) | copy-start | bytes 589828
  44.1 14.1 %all-to-all-start.1 = ((bf16[4,384,256]{2,1,0:T(8,128)(2,1)}), bf16[4,384,256]{2,1,0:T(8,128)(2,1)S(1)}, u32[]{:S(2)}, u32[]{:S(2)}) async-start(bf16[4,384,256]{2,1,0:T(8,128)(2,1)} %shard_map.86), calls=%async_computation.1 | async-start | bytes 1572864 | tf_op jit(solution)/shard_map/all_to_all | solution.py:27
  49.7 7.8 %collective-permute-start.7 = (f32[3,24,256]{2,1,0:T(8,128)S(1)}, f32[3,24,256]{2,1,0:T(8,128)S(1)}, u32[]{:S(2)}, u32[]{:S(2)}) collective-permute-start(f32[3,24,256]{2,1,0:T(8,128)S(1)} %pad_maximum_fusion), channel_id=1, source_target_pairs={{0,0},{1,64},{2,128},{3,192},{4,256},{5,320},{6,384},{7,448},{64,1... | collective-permute-start | bytes 221192 | tf_op jit(solution)/shard_map/ppermute | solution.py:169
  59.0 30.7 %all-to-all-start.2 = ((bf16[16,24,256]{2,1,0:T(8,128)(2,1)}), bf16[16,24,256]{2,1,0:T(8,128)(2,1)S(1)}, u32[]{:S(2)}, u32[]{:S(2)}) async-start(bf16[16,24,256]{2,1,0:T(8,128)(2,1)} %bitcast.14), calls=%async_computation.2 | async-start | bytes 393216 | tf_op jit(solution)/shard_map/all_to_all | solution.py:27
  124.9 31.6 %copy-start.3 = (f32[24,2048]{1,0:T(8,128)S(1)}, f32[24,2048]{1,0:T(8,128)}, u32[]{:S(2)}) copy-start(f32[24,2048]{1,0:T(8,128)} %first.1) | copy-start | bytes 589828

commit v7 on v6

--- a/solution.py
+++ b/solution.py
@@ -84,17 +84,33 @@
             out[i, at, :] = (term[at] + jnp.where(mine, 1.0, 0.0) * residue).astype(BF16)
 
 
-def sum_blocks(arrived, out):
-    total = arrived[0].astype(F32)
+def sum_blocks(places, arrived, out, total):
+    value = arrived[0].astype(F32)
     for i in range(1, arrived.shape[0]):
-        total = total + arrived[i].astype(F32)
-    members, rows, _ = out.shape
-    part = total.shape[0] // 2
-    own = rows // 2
-    for m in range(members):
-        low, high = m * own, part + m * own
-        block = jnp.concatenate([total[low : low + own], total[high : high + own]], axis=0)
-        out[m] = block.astype(BF16)
+        value = value + arrived[i].astype(F32)
+    total[...] = value
+    blocks, rows, _ = out.shape
+    own, part = rows // 2, total.shape[0] // 2
+    for a in range(blocks):
+        low = pl.multiple_of(lax.rem(places[places.shape[0] - 1] + a, blocks) * own, 8)
+        pieces = [total[pl.ds(k * part + low, own), :] for k in range(2)]
+        out[a] = jnp.concatenate(pieces, axis=0).astype(BF16)
+
+
+def spread(places, packed, sent, row_grad):
+    blocks, pad, size = row_grad.shape
+    own = packed.shape[1] // 2
+    part = blocks * own
+    source = [2 * lax.rem(blocks + m - places[places.shape[0] - 1], blocks) for m in range(blocks)]
+    for k in range(2):
+        rows = [packed[z + k].astype(F32)[:own] for z in source]
+        rows = jnp.concatenate(rows, axis=0).astype(BF16)
+        for i in range(sent.shape[0]):
+            sent[i, k * part : (k + 1) * part, :] = rows
+    zeros = jnp.zeros((pad - own, size), F32)
+    for m, z in enumerate(source):
+        grad = packed[z + places[places.shape[0] - 2]].astype(F32)[own:]
+        row_grad[m] = jnp.concatenate([grad, zeros], axis=0).astype(BF16)
 
 
 def update_rows(parts, states, out):
@@ -161,15 +177,18 @@
     )
     got = exchange(pieces, group)
 
+    me = 2 * y + core
+    head = lax.rem(me + nz - zl, nz)
+
     def columns(a):
-        return lax.dynamic_slice_in_dim(a, zl * HEAD_SIZE, HEAD_SIZE, 1)
+        return lax.dynamic_slice_in_dim(a, head * HEAD_SIZE, HEAD_SIZE, 1)
 
     states = jnp.stack([columns(first), columns(second), columns(weight).astype(F32)])
-    turn = [(a * nz + b, b * nz + a) for a in range(nz) for b in range(nz)]
+    turn = [(a * nz + (a + b) % nz, a * nz + b) for a in range(nz) for b in range(nz)]
     states = lax.ppermute(states, ("zl", "y", "core"), turn)
 
     steps = [(k, m) for m in (core, 1 - core) for k in range(ny)]
-    places = jnp.stack([2 * lax.rem(y + ny - k, ny) + m for k, m in steps] + [x, zh])
+    places = jnp.stack([2 * lax.rem(y + ny - k, ny) + m for k, m in steps] + [x, zh, me])
     places = places.astype(jnp.int32)
     rows = depth // nx
     term = jax.ShapeDtypeStruct((nx, rows, HEAD_SIZE), BF16)
@@ -177,18 +196,18 @@
 
     arrived = exchange(term, "x")
     arrived, states = lax.optimization_barrier((arrived, states))
-    part = call(sum_blocks, jax.ShapeDtypeStruct((nz, nzh * own, HEAD_SIZE), BF16), arrived)
+    part = jax.ShapeDtypeStruct((nz, nzh * own, HEAD_SIZE), BF16)
+    total = pltpu.VMEM((rows, HEAD_SIZE), F32)
+    part = call(sum_blocks, part, places, arrived, scratch=(total,))
 
     parts = exchange(part.reshape(nz * nzh, own, HEAD_SIZE), ("zl", "zh"))
     packed = jax.ShapeDtypeStruct((nz * nzh, 2 * own, HEAD_SIZE), BF16)
     packed = call(update_rows, packed, parts.reshape(nz, nzh * own, HEAD_SIZE), states)
 
-    packed, upper = lax.optimization_barrier((packed, zh > 0))
-    packed = exchange(packed, ("zl", "zh")).reshape(nz, nzh, 2, own, HEAD_SIZE)
-    row_grad = jnp.where(upper, packed[:, 1, 1], packed[:, 0, 1])
-    row_grad = jnp.pad(row_grad, ((0, 0), (0, block - tok - own), (0, 0)))
-    sent = packed[:, :, 0].transpose(1, 0, 2, 3).reshape(rows, HEAD_SIZE)
-    sent = jnp.broadcast_to(sent[None], (nx, rows, HEAD_SIZE))
+    packed = exchange(packed, ("zl", "zh"))
+    sent = jax.ShapeDtypeStruct((nx, rows, HEAD_SIZE), BF16)
+    row_grad = jax.ShapeDtypeStruct((nz, block - tok, HEAD_SIZE), BF16)
+    sent, row_grad = call(spread, (sent, row_grad), places, packed)
     sent, row_grad = lax.optimization_barrier((sent, row_grad))
     head_weight = exchange(sent, "x").reshape(depth, HEAD_SIZE)
 

time: 160 us -> 155 us (0.969)
  blocking collectives: 63.9 us -> 89.2 us
  starting transfers between devices: 59.6 us -> 38.1 us
  waiting for transfers between devices: 20.4 us -> 11.2 us
    all_to_all x3 -> x4, blocking collectives: 63.9 us -> 89.2 us  [exchange(): return lax.all_to_all(pieces, axes, split_axis=0, concat_axis=0, tiled=True)]
    all_to_all x3 -> x2, starting transfers between devices: 30.7 us -> 14 us  [exchange(): return lax.all_to_all(pieces, axes, split_axis=0, concat_axis=0, tiled=True)]
    all_to_all x3 -> x2, waiting for transfers between devices: 18.1 us -> 11.2 us  [exchange(): return lax.all_to_all(pieces, axes, split_axis=0, concat_axis=0, tiled=True)]
    ppermute x1, starting transfers between devices: 5.45 us -> 0.66 us  [relay(): states = lax.ppermute(states, ('zl', 'y', 'core'), turn)]
    ppermute x1, waiting for transfers between devices: 2.32 us -> 0.01 us  [relay(): states = lax.ppermute(states, ('zl', 'y', 'core'), turn)]
    pallas_call x6 -> x7, Pallas kernels: 9.21 us -> 9.73 us  [call(): pl.pallas_call(body, out_shape=shapes, in_specs=[pl.BlockSpec(memory_spac...]
  transfers between devices with their start and end apart: 11 -> 10, of which waited for: 4 -> 2; matrix products, arithmetic and copies ran while one was open for 1% -> 1% of each run, Pallas kernels for 1% -> 1%
where the time goes in v7:
time: 155 us; the launch traced here: 153 us
  blocking collectives  89.2 us (58%)
  starting transfers between devices  38.1 us (25%)
  waiting for transfers between devices  11.2 us (7%)
  Pallas kernels  9.73 us (6%)
  local copies, waits for them, and re-layouts  2.85 us (2%)
    all_to_all x4, blocking collectives, exchange(): return lax.all_to_all(pieces, axes, split_axis=0, concat_axis=0, tiled=True)  89.2 us
    all_to_all x2, starting transfers between devices, exchange(): return lax.all_to_all(pieces, axes, split_axis=0, concat_axis=0, tiled=True)  14 us
    ppermute x4, starting transfers between devices, relay(): acts = near + [lax.ppermute(a, 'core', swap) for a in near]  13.1 us
    all_to_all x2, waiting for transfers between devices, exchange(): return lax.all_to_all(pieces, axes, split_axis=0, concat_axis=0, tiled=True)  11.2 us
    ppermute x3, starting transfers between devices, shift(): return lax.ppermute(a, axis, [(i, (i + k) % n) for i in range(n)])  10.3 us
    pallas_call x7, Pallas kernels, call(): pl.pallas_call(body, out_shape=shapes, in_specs=[pl.BlockSpec(memory_spac...  9.73 us
  transfers between devices with their start and end apart: 10, of which 2 were waited for; matrix products, arithmetic and copies ran while one was open for 1% of the time, Pallas kernels for 1%

profile of v7, /device:TPU:1, one launch (start us, length us, event | category | flops | bytes accessed | tf_op | source)
XLA Modules:
  0.0 152.5 jit_solution(9908208506459914822)
XLA Ops:
  0.6 5.5 %collective-permute-start.2 = (bf16[160,1536]{1,0:T(8,128)(2,1)}, bf16[160,1536]{1,0:T(8,128)(2,1)S(1)}, u32[]{:S(2)}, u32[]{:S(2)}) collective-permute-start(bf16[160,1536]{1,0:T(8,128)(2,1)} %refs_0_.3), channel_id=1, source_target_pairs={{0,6},{2,0},{4,2},{6,4},{1,7},{3,1},{5,3},{7,5},{8,14},{10,8},{12,... | collective-permute-start | bytes 1474568 | tf_op jit(solution)/shard_map/ppermute | solution.py:32
  6.1 2.3 %collective-permute-start.1 = (bf16[160,1536]{1,0:T(8,128)(2,1)}, bf16[160,1536]{1,0:T(8,128)(2,1)S(1)}, u32[]{:S(2)}, u32[]{:S(2)}) collective-permute-start(bf16[160,1536]{1,0:T(8,128)(2,1)} %refs_0_.3), channel_id=1, source_target_pairs={{0,4},{2,6},{4,0},{6,2},{1,5},{3,7},{5,1},{7,3},{8,12},{10,14},{12... | collective-permute-start | bytes 1474568 | tf_op jit(solution)/shard_map/ppermute | solution.py:32
  8.4 2.6 %collective-permute-start = (bf16[160,1536]{1,0:T(8,128)(2,1)}, bf16[160,1536]{1,0:T(8,128)(2,1)S(1)}, u32[]{:S(2)}, u32[]{:S(2)}) collective-permute-start(bf16[160,1536]{1,0:T(8,128)(2,1)} %refs_0_.3), channel_id=1, source_target_pairs={{0,2},{2,4},{4,6},{6,0},{1,3},{3,5},{5,7},{7,1},{8,10},{10,12},{12... | collective-permute-start | bytes 1474568 | tf_op jit(solution)/shard_map/ppermute | solution.py:32
  11.0 0.0 copy-start.1
  11.0 1.1 copy-done.1
  12.1 0.0 copy-start.4
  12.1 0.9 copy-done.4
  13.0 1.2 shard_map.85
  14.2 0.0 copy-start
  14.2 9.9 %all-to-all-start = ((bf16[8,192,256]{2,1,0:T(8,128)(2,1)}), bf16[8,192,256]{2,1,0:T(8,128)(2,1)S(1)}, u32[]{:S(2)}, u32[]{:S(2)}) async-start(bf16[8,192,256]{2,1,0:T(8,128)(2,1)} %shard_map.85), calls=%async_computation | async-start | bytes 1572864 | tf_op jit(solution)/shard_map/all_to_all | solution.py:27
  24.1 0.0 copy-done
  24.1 1.9 %collective-permute-start.3 = (bf16[160,1536]{1,0:T(8,128)(2,1)S(1)}, bf16[160,1536]{1,0:T(8,128)(2,1)S(1)}, u32[]{:S(2)}, u32[]{:S(2)}) collective-permute-start(bf16[160,1536]{1,0:T(8,128)(2,1)S(1)} %copy-done), channel_id=1, source_target_pairs={{0,1},{1,0},{2,3},{3,2},{4,5},{5,4},{6,7},{7,6},{8,9},{9,8},{10,11... | collective-permute-start | bytes 1474568 | tf_op jit(solution)/shard_map/ppermute | solution.py:160
  26.0 0.0 collective-permute-done.2.refs_3_
  26.0 6.8 %collective-permute-start.6 = (bf16[160,1536]{1,0:T(8,128)(2,1)S(1)}, bf16[160,1536]{1,0:T(8,128)(2,1)}, u32[]{:S(2)}, u32[]{:S(2)}) collective-permute-start(bf16[160,1536]{1,0:T(8,128)(2,1)S(1)} %collective-permute-done.2.refs_3_), channel_id=1, source_target_pairs={{0,1},{1,0},{2,3},{3,2},{4,5},{5,4},{6,7},{7,6},{8,9},{9,8},{10,11... | collective-permute-start | bytes 1474568 | tf_op jit(solution)/shard_map/ppermute | solution.py:160
  32.8 0.0 collective-permute-done.1.refs_2_
  32.8 1.9 %collective-permute-start.5 = (bf16[160,1536]{1,0:T(8,128)(2,1)S(1)}, bf16[160,1536]{1,0:T(8,128)(2,1)}, u32[]{:S(2)}, u32[]{:S(2)}) collective-permute-start(bf16[160,1536]{1,0:T(8,128)(2,1)S(1)} %collective-permute-done.1.refs_2_), channel_id=1, source_target_pairs={{0,1},{1,0},{2,3},{3,2},{4,5},{5,4},{6,7},{7,6},{8,9},{9,8},{10,11... | collective-permute-start | bytes 1474568 | tf_op jit(solution)/shard_map/ppermute | solution.py:160
  34.8 0.0 collective-permute-done.refs_1_
  34.8 2.4 %collective-permute-start.4 = (bf16[160,1536]{1,0:T(8,128)(2,1)S(1)}, bf16[160,1536]{1,0:T(8,128)(2,1)}, u32[]{:S(2)}, u32[]{:S(2)}) collective-permute-start(bf16[160,1536]{1,0:T(8,128)(2,1)S(1)} %collective-permute-done.refs_1_), channel_id=1, source_target_pairs={{0,1},{1,0},{2,3},{3,2},{4,5},{5,4},{6,7},{7,6},{8,9},{9,8},{10,11... | collective-permute-start | bytes 1474568 | tf_op jit(solution)/shard_map/ppermute | solution.py:160
  37.2 0.1 stack.62.places
  37.3 0.0 collective-permute-done.3.refs_4_
  37.3 3.3 %all-to-all-done.refs_8_ = bf16[8,192,256]{2,1,0:T(8,128)(2,1)S(1)} async-done(((bf16[8,192,256]{2,1,0:T(8,128)(2,1)}), bf16[8,192,256]{2,1,0:T(8,128)(2,1)S(1)}, u32[]{:S(2)}, u32[]{:S(2)}) %all-to-all-start) | async-done | bytes 786464 | tf_op jit(solution)/shard_map/all_to_all | solution.py:27
  40.6 0.0 collective-permute-done.6.refs_7_
  40.6 0.0 collective-permute-done.5.refs_6_
  40.6 0.0 collective-permute-done.4.refs_5_
  40.6 3.5 %shard_map.86 = bf16[4,384,256]{2,1,0:T(8,128)(2,1)} custom-call(s32[11]{0:T(128)S(1)} %stack.62.places, bf16[160,1536]{1,0:T(8,128)(2,1)S(1)} %copy-done, bf16[160,1536]{1,0:T(8,128)(2,1)S(1)} %collective-permute-done.refs_1_, bf16[160,1536]{1,0:T(8,128)(2,1)S(1)} %collective-permute-done.1.refs_2_, bf16[160,1536]{1,0:T(8,128)(2,1)S(1)} %collective-permute-done.2.refs_3_, ...), custom_call_target="tpu_custom_call" | custom-call | tf_op jit(solution)/shard_map/pallas_call | solution.py:38
  44.1 0.0 copy-start.2
  44.1 4.1 %all-to-all-start.1 = ((bf16[4,384,256]{2,1,0:T(8,128)(2,1)}), bf16[4,384,256]{2,1,0:T(8,128)(2,1)S(1)}, u32[]{:S(2)}, u32[]{:S(2)}) async-start(bf16[4,384,256]{2,1,0:T(8,128)(2,1)} %shard_map.86), calls=%async_computation.1 | async-start | bytes 1572864 | tf_op jit(solution)/shard_map/all_to_all | solution.py:27
  48.2 0.7 bitcast_convert_fusion
  49.0 0.0 copy-done.2
  49.0 0.7 dynamic-slice_bitcast_fusion
  49.7 0.7 collective-permute-start.7
  50.4 0.0 collective-permute-done.7.states
  50.4 7.9 %all-to-all-done.1.arrived = bf16[4,384,256]{2,1,0:T(8,128)(2,1)S(1)} async-done(((bf16[4,384,256]{2,1,0:T(8,128)(2,1)}), bf16[4,384,256]{2,1,0:T(8,128)(2,1)S(1)}, u32[]{:S(2)}, u32[]{:S(2)}) %all-to-all-start.1) | async-done | bytes 786464 | tf_op jit(solution)/shard_map/all_to_all | solution.py:27
  58.2 0.7 shard_map.87
  58.9 28.7 %all_to_all.30 = bf16[16,24,256]{2,1,0:T(8,128)(2,1)S(1)} all-to-all(bf16[16,24,256]{2,1,0:T(8,128)(2,1)S(1)} %bitcast.23), channel_id=1, replica_groups=mesh['zl'=8,'x'=4,'zh'=2,'y'=4,'core'=2] {'zl','zh'}, dimensions={0} | all-to-all | bytes 393216 | tf_op jit(solution)/shard_map/all_to_all | solution.py:27
  87.7 0.2 shard_map.88
  87.8 24.9 %all_to_all.31.packed = bf16[16,48,256]{2,1,0:T(8,128)(2,1)S(1)} all-to-all(bf16[16,48,256]{2,1,0:T(8,128)(2,1)S(1)} %shard_map.88), channel_id=1, replica_groups=mesh['zl'=8,'x'=4,'zh'=2,'y'=4,'core'=2] {'zl','zh'}, dimensions={0} | all-to-all | bytes 786432 | tf_op jit(solution)/shard_map/all_to_all | solution.py:27
  112.7 0.6 shard_map.89
  113.3 10.7 %all_to_all.32 = bf16[4,384,256]{2,1,0:T(8,128)(2,1)S(1)} all-to-all(bf16[4,384,256]{2,1,0:T(8,128)(2,1)S(1)} %get-tuple-element.9), channel_id=1, replica_groups=mesh['zl'=8,'x'=4,'zh'=2,'y'=4,'core'=2] {'x'}, dimensions={0} | all-to-all | bytes 1572864 | tf_op jit(solution)/shard_map/all_to_all | solution.py:27
  124.0 2.5 %shard_map.90 = bf16[8,192,256]{2,1,0:T(8,128)(2,1)S(1)} custom-call(s32[11]{0:T(128)S(1)} %stack.62.places, bf16[160,1536]{1,0:T(8,128)(2,1)S(1)} %copy-done, bf16[160,1536]{1,0:T(8,128)(2,1)S(1)} %collective-permute-done.refs_1_, bf16[160,1536]{1,0:T(8,128)(2,1)S(1)} %collective-permute-done.1.refs_2_, ...), custom_call_target="tpu_custom_call" | custom-call | tf_op jit(solution)/shard_map/pallas_call | solution.py:38
  126.6 0.0 copy-start.3
  126.6 24.8 %all_to_all.33.back = bf16[8,192,256]{2,1,0:T(8,128)(2,1)S(1)} all-to-all(bf16[8,192,256]{2,1,0:T(8,128)(2,1)S(1)} %shard_map.90), channel_id=1, replica_groups=mesh['zl'=8,'x'=4,'zh'=2,'y'=4,'core'=2] {'y','core'}, dimensions={0} | all-to-all | bytes 1572864 | tf_op jit(solution)/shard_map/all_to_all | solution.py:27
  151.4 0.0 copy-done.3
  151.4 1.1 shard_map.91
  (1 shorter events, 0.0 us)
Async XLA Ops:
  0.6 25.4 %collective-permute-start.2 = (bf16[160,1536]{1,0:T(8,128)(2,1)}, bf16[160,1536]{1,0:T(8,128)(2,1)S(1)}, u32[]{:S(2)}, u32[]{:S(2)}) collective-permute-start(bf16[160,1536]{1,0:T(8,128)(2,1)} %refs_0_.3), channel_id=1, source_target_pairs={{0,6},{2,0},{4,2},{6,4},{1,7},{3,1},{5,3},{7,5},{8,14},{10,8},{12,... | collective-permute-start | bytes 1474568 | tf_op jit(solution)/shard_map/ppermute | solution.py:32
  6.1 26.7 %collective-permute-start.1 = (bf16[160,1536]{1,0:T(8,128)(2,1)}, bf16[160,1536]{1,0:T(8,128)(2,1)S(1)}, u32[]{:S(2)}, u32[]{:S(2)}) collective-permute-start(bf16[160,1536]{1,0:T(8,128)(2,1)} %refs_0_.3), channel_id=1, source_target_pairs={{0,4},{2,6},{4,0},{6,2},{1,5},{3,7},{5,1},{7,3},{8,12},{10,14},{12... | collective-permute-start | bytes 1474568 | tf_op jit(solution)/shard_map/ppermute | solution.py:32
  8.4 26.4 %collective-permute-start = (bf16[160,1536]{1,0:T(8,128)(2,1)}, bf16[160,1536]{1,0:T(8,128)(2,1)S(1)}, u32[]{:S(2)}, u32[]{:S(2)}) collective-permute-start(bf16[160,1536]{1,0:T(8,128)(2,1)} %refs_0_.3), channel_id=1, source_target_pairs={{0,2},{2,4},{4,6},{6,0},{1,3},{3,5},{5,7},{7,1},{8,10},{10,12},{12... | collective-permute-start | bytes 1474568 | tf_op jit(solution)/shard_map/ppermute | solution.py:32
  11.0 1.1 copy-start.1
  12.1 0.9 copy-start.4
  14.2 9.9 %copy-start = (bf16[160,1536]{1,0:T(8,128)(2,1)S(1)}, bf16[160,1536]{1,0:T(8,128)(2,1)}, u32[]{:S(2)}) copy-start(bf16[160,1536]{1,0:T(8,128)(2,1)} %refs_0_.3) | copy-start | bytes 1474564
  14.2 26.4 %all-to-all-start = ((bf16[8,192,256]{2,1,0:T(8,128)(2,1)}), bf16[8,192,256]{2,1,0:T(8,128)(2,1)S(1)}, u32[]{:S(2)}, u32[]{:S(2)}) async-start(bf16[8,192,256]{2,1,0:T(8,128)(2,1)} %shard_map.85), calls=%async_computation | async-start | bytes 1572864 | tf_op jit(solution)/shard_map/all_to_all | solution.py:27
  24.1 13.2 %collective-permute-start.3 = (bf16[160,1536]{1,0:T(8,128)(2,1)S(1)}, bf16[160,1536]{1,0:T(8,128)(2,1)S(1)}, u32[]{:S(2)}, u32[]{:S(2)}) collective-permute-start(bf16[160,1536]{1,0:T(8,128)(2,1)S(1)} %copy-done), channel_id=1, source_target_pairs={{0,1},{1,0},{2,3},{3,2},{4,5},{5,4},{6,7},{7,6},{8,9},{9,8},{10,11... | collective-permute-start | bytes 1474568 | tf_op jit(solution)/shard_map/ppermute | solution.py:160
  26.0 14.6 %collective-permute-start.6 = (bf16[160,1536]{1,0:T(8,128)(2,1)S(1)}, bf16[160,1536]{1,0:T(8,128)(2,1)}, u32[]{:S(2)}, u32[]{:S(2)}) collective-permute-start(bf16[160,1536]{1,0:T(8,128)(2,1)S(1)} %collective-permute-done.2.refs_3_), channel_id=1, source_target_pairs={{0,1},{1,0},{2,3},{3,2},{4,5},{5,4},{6,7},{7,6},{8,9},{9,8},{10,11... | collective-permute-start | bytes 1474568 | tf_op jit(solution)/shard_map/ppermute | solution.py:160
  32.8 7.8 %collective-permute-start.5 = (bf16[160,1536]{1,0:T(8,128)(2,1)S(1)}, bf16[160,1536]{1,0:T(8,128)(2,1)}, u32[]{:S(2)}, u32[]{:S(2)}) collective-permute-start(bf16[160,1536]{1,0:T(8,128)(2,1)S(1)} %collective-permute-done.1.refs_2_), channel_id=1, source_target_pairs={{0,1},{1,0},{2,3},{3,2},{4,5},{5,4},{6,7},{7,6},{8,9},{9,8},{10,11... | collective-permute-start | bytes 1474568 | tf_op jit(solution)/shard_map/ppermute | solution.py:160
  34.8 5.8 %collective-permute-start.4 = (bf16[160,1536]{1,0:T(8,128)(2,1)S(1)}, bf16[160,1536]{1,0:T(8,128)(2,1)}, u32[]{:S(2)}, u32[]{:S(2)}) collective-permute-start(bf16[160,1536]{1,0:T(8,128)(2,1)S(1)} %collective-permute-done.refs_1_), channel_id=1, source_target_pairs={{0,1},{1,0},{2,3},{3,2},{4,5},{5,4},{6,7},{7,6},{8,9},{9,8},{10,11... | collective-permute-start | bytes 1474568 | tf_op jit(solution)/shard_map/ppermute | solution.py:160
  44.1 4.9 %copy-start.2 = (f32[24,2048]{1,0:T(8,128)S(1)}, f32[24,2048]{1,0:T(8,128)}, u32[]{:S(2)}) copy-start(f32[24,2048]{1,0:T(8,128)} %second.1) | copy-start | bytes 589828
  44.1 14.1 %all-to-all-start.1 = ((bf16[4,384,256]{2,1,0:T(8,128)(2,1)}), bf16[4,384,256]{2,1,0:T(8,128)(2,1)S(1)}, u32[]{:S(2)}, u32[]{:S(2)}) async-start(bf16[4,384,256]{2,1,0:T(8,128)(2,1)} %shard_map.86), calls=%async_computation.1 | async-start | bytes 1572864 | tf_op jit(solution)/shard_map/all_to_all | solution.py:27
  49.7 0.7 collective-permute-start.7
  126.6 24.8 %copy-start.3 = (f32[24,2048]{1,0:T(8,128)S(1)}, f32[24,2048]{1,0:T(8,128)}, u32[]{:S(2)}) copy-start(f32[24,2048]{1,0:T(8,128)} %first.1) | copy-start | bytes 589828

commit v8 on v7

--- a/solution.py
+++ b/solution.py
@@ -184,8 +184,8 @@
         return lax.dynamic_slice_in_dim(a, head * HEAD_SIZE, HEAD_SIZE, 1)
 
     states = jnp.stack([columns(first), columns(second), columns(weight).astype(F32)])
+    got, states = lax.optimization_barrier((got, states))
     turn = [(a * nz + (a + b) % nz, a * nz + b) for a in range(nz) for b in range(nz)]
-    states = lax.ppermute(states, ("zl", "y", "core"), turn)
 
     steps = [(k, m) for m in (core, 1 - core) for k in range(ny)]
     places = jnp.stack([2 * lax.rem(y + ny - k, ny) + m for k, m in steps] + [x, zh, me])
@@ -195,12 +195,14 @@
     term = call(functools.partial(head_term, own), term, places, *acts, got)
 
     arrived = exchange(term, "x")
-    arrived, states = lax.optimization_barrier((arrived, states))
     part = jax.ShapeDtypeStruct((nz, nzh * own, HEAD_SIZE), BF16)
     total = pltpu.VMEM((rows, HEAD_SIZE), F32)
     part = call(sum_blocks, part, places, arrived, scratch=(total,))
 
+    part, states = lax.optimization_barrier((part, states))
     parts = exchange(part.reshape(nz * nzh, own, HEAD_SIZE), ("zl", "zh"))
+    states = lax.ppermute(states, ("zl", "y", "core"), turn)
+    parts, states = lax.optimization_barrier((parts, states))
     packed = jax.ShapeDtypeStruct((nz * nzh, 2 * own, HEAD_SIZE), BF16)
     packed = call(update_rows, packed, parts.reshape(nz, nzh * own, HEAD_SIZE), states)
 

time: 155 us -> 154 us (level)
  blocking collectives: 89.2 us -> 73.8 us
  starting transfers between devices: 38.1 us -> 48.8 us
  waiting for transfers between devices: 11.2 us -> 15.2 us
    all_to_all x4, blocking collectives: 89.2 us -> 73.8 us  [exchange(): return lax.all_to_all(pieces, axes, split_axis=0, concat_axis=0, tiled=True)]
    all_to_all x2, starting transfers between devices: 14 us -> 24.8 us  [exchange(): return lax.all_to_all(pieces, axes, split_axis=0, concat_axis=0, tiled=True)]
    all_to_all x2, waiting for transfers between devices: 11.2 us -> 15.2 us  [exchange(): return lax.all_to_all(pieces, axes, split_axis=0, concat_axis=0, tiled=True)]
where the time goes in v8:
time: 154 us; the launch traced here: 152 us
  blocking collectives  73.8 us (48%)
  starting transfers between devices  48.8 us (32%)
  waiting for transfers between devices  15.2 us (10%)
  Pallas kernels  9.51 us (6%)
  local copies, waits for them, and re-layouts  2.85 us (2%)
    all_to_all x4, blocking collectives, exchange(): return lax.all_to_all(pieces, axes, split_axis=0, concat_axis=0, tiled=True)  73.8 us
    all_to_all x2, starting transfers between devices, exchange(): return lax.all_to_all(pieces, axes, split_axis=0, concat_axis=0, tiled=True)  24.8 us
    all_to_all x2, waiting for transfers between devices, exchange(): return lax.all_to_all(pieces, axes, split_axis=0, concat_axis=0, tiled=True)  15.2 us
    ppermute x4, starting transfers between devices, relay(): acts = near + [lax.ppermute(a, 'core', swap) for a in near]  13.1 us
    ppermute x3, starting transfers between devices, shift(): return lax.ppermute(a, axis, [(i, (i + k) % n) for i in range(n)])  10.3 us
    pallas_call x7, Pallas kernels, call(): pl.pallas_call(body, out_shape=shapes, in_specs=[pl.BlockSpec(memory_spac...  9.51 us
  transfers between devices with their start and end apart: 10, of which 2 were waited for; matrix products, arithmetic and copies ran while one was open for 1% of the time, Pallas kernels for 1%

profile of v8, /device:TPU:1, one launch (start us, length us, event | category | flops | bytes accessed | tf_op | source)
XLA Modules:
  0.0 151.7 jit_solution(15712172128093882846)
XLA Ops:
  0.6 5.5 %collective-permute-start.2 = (bf16[160,1536]{1,0:T(8,128)(2,1)}, bf16[160,1536]{1,0:T(8,128)(2,1)S(1)}, u32[]{:S(2)}, u32[]{:S(2)}) collective-permute-start(bf16[160,1536]{1,0:T(8,128)(2,1)} %refs_0_.3), channel_id=1, source_target_pairs={{0,6},{2,0},{4,2},{6,4},{1,7},{3,1},{5,3},{7,5},{8,14},{10,8},{12,... | collective-permute-start | bytes 1474568 | tf_op jit(solution)/shard_map/ppermute | solution.py:32
  6.1 2.3 %collective-permute-start.1 = (bf16[160,1536]{1,0:T(8,128)(2,1)}, bf16[160,1536]{1,0:T(8,128)(2,1)S(1)}, u32[]{:S(2)}, u32[]{:S(2)}) collective-permute-start(bf16[160,1536]{1,0:T(8,128)(2,1)} %refs_0_.3), channel_id=1, source_target_pairs={{0,4},{2,6},{4,0},{6,2},{1,5},{3,7},{5,1},{7,3},{8,12},{10,14},{12... | collective-permute-start | bytes 1474568 | tf_op jit(solution)/shard_map/ppermute | solution.py:32
  8.4 2.6 %collective-permute-start = (bf16[160,1536]{1,0:T(8,128)(2,1)}, bf16[160,1536]{1,0:T(8,128)(2,1)S(1)}, u32[]{:S(2)}, u32[]{:S(2)}) collective-permute-start(bf16[160,1536]{1,0:T(8,128)(2,1)} %refs_0_.3), channel_id=1, source_target_pairs={{0,2},{2,4},{4,6},{6,0},{1,3},{3,5},{5,7},{7,1},{8,10},{10,12},{12... | collective-permute-start | bytes 1474568 | tf_op jit(solution)/shard_map/ppermute | solution.py:32
  11.0 0.0 copy-start.1
  11.0 1.1 copy-done.1
  12.1 0.0 copy-start.4
  12.1 0.9 copy-done.4
  13.0 1.2 shard_map.85
  14.2 0.0 copy-start
  14.2 9.9 %all-to-all-start = ((bf16[8,192,256]{2,1,0:T(8,128)(2,1)}), bf16[8,192,256]{2,1,0:T(8,128)(2,1)S(1)}, u32[]{:S(2)}, u32[]{:S(2)}) async-start(bf16[8,192,256]{2,1,0:T(8,128)(2,1)} %shard_map.85), calls=%async_computation | async-start | bytes 1572864 | tf_op jit(solution)/shard_map/all_to_all | solution.py:27
  24.1 0.0 copy-done
  24.1 0.0 copy-start.2
  24.1 2.1 %collective-permute-start.3 = (bf16[160,1536]{1,0:T(8,128)(2,1)S(1)}, bf16[160,1536]{1,0:T(8,128)(2,1)S(1)}, u32[]{:S(2)}, u32[]{:S(2)}) collective-permute-start(bf16[160,1536]{1,0:T(8,128)(2,1)S(1)} %copy-done), channel_id=1, source_target_pairs={{0,1},{1,0},{2,3},{3,2},{4,5},{5,4},{6,7},{7,6},{8,9},{9,8},{10,11... | collective-permute-start | bytes 1474568 | tf_op jit(solution)/shard_map/ppermute | solution.py:160
  26.1 0.0 collective-permute-done.2.refs_3_
  26.2 6.7 %collective-permute-start.6 = (bf16[160,1536]{1,0:T(8,128)(2,1)S(1)}, bf16[160,1536]{1,0:T(8,128)(2,1)}, u32[]{:S(2)}, u32[]{:S(2)}) collective-permute-start(bf16[160,1536]{1,0:T(8,128)(2,1)S(1)} %collective-permute-done.2.refs_3_), channel_id=1, source_target_pairs={{0,1},{1,0},{2,3},{3,2},{4,5},{5,4},{6,7},{7,6},{8,9},{9,8},{10,11... | collective-permute-start | bytes 1474568 | tf_op jit(solution)/shard_map/ppermute | solution.py:160
  32.8 0.0 collective-permute-done.1.refs_2_
  32.8 1.9 %collective-permute-start.5 = (bf16[160,1536]{1,0:T(8,128)(2,1)S(1)}, bf16[160,1536]{1,0:T(8,128)(2,1)}, u32[]{:S(2)}, u32[]{:S(2)}) collective-permute-start(bf16[160,1536]{1,0:T(8,128)(2,1)S(1)} %collective-permute-done.1.refs_2_), channel_id=1, source_target_pairs={{0,1},{1,0},{2,3},{3,2},{4,5},{5,4},{6,7},{7,6},{8,9},{9,8},{10,11... | collective-permute-start | bytes 1474568 | tf_op jit(solution)/shard_map/ppermute | solution.py:160
  34.8 0.0 collective-permute-done.refs_1_
  34.8 2.4 %collective-permute-start.4 = (bf16[160,1536]{1,0:T(8,128)(2,1)S(1)}, bf16[160,1536]{1,0:T(8,128)(2,1)}, u32[]{:S(2)}, u32[]{:S(2)}) collective-permute-start(bf16[160,1536]{1,0:T(8,128)(2,1)S(1)} %collective-permute-done.refs_1_), channel_id=1, source_target_pairs={{0,1},{1,0},{2,3},{3,2},{4,5},{5,4},{6,7},{7,6},{8,9},{9,8},{10,11... | collective-permute-start | bytes 1474568 | tf_op jit(solution)/shard_map/ppermute | solution.py:160
  37.2 0.1 stack.62.places
  37.3 0.7 bitcast_convert_fusion
  38.0 0.0 copy-done.2
  38.0 0.7 dynamic-slice_bitcast_fusion
  38.8 1.8 %all-to-all-done.refs_8_ = bf16[8,192,256]{2,1,0:T(8,128)(2,1)S(1)} async-done(((bf16[8,192,256]{2,1,0:T(8,128)(2,1)}), bf16[8,192,256]{2,1,0:T(8,128)(2,1)S(1)}, u32[]{:S(2)}, u32[]{:S(2)}) %all-to-all-start) | async-done | bytes 786464 | tf_op jit(solution)/shard_map/all_to_all | solution.py:27
  40.6 0.0 collective-permute-done.3.refs_4_
  40.6 0.0 collective-permute-done.6.refs_7_
  40.6 0.0 collective-permute-done.5.refs_6_
  40.6 0.0 collective-permute-done.4.refs_5_
  40.6 2.6 %shard_map.86 = bf16[4,384,256]{2,1,0:T(8,128)(2,1)S(1)} custom-call(s32[11]{0:T(128)S(1)} %stack.62.places, bf16[160,1536]{1,0:T(8,128)(2,1)S(1)} %copy-done, bf16[160,1536]{1,0:T(8,128)(2,1)S(1)} %collective-permute-done.refs_1_, bf16[160,1536]{1,0:T(8,128)(2,1)S(1)} %collective-permute-done.1.refs_2_, ...), custom_call_target="tpu_custom_call" | custom-call | tf_op jit(solution)/shard_map/pallas_call | solution.py:38
  43.2 13.8 %all_to_all.30.arrived = bf16[4,384,256]{2,1,0:T(8,128)(2,1)S(1)} all-to-all(bf16[4,384,256]{2,1,0:T(8,128)(2,1)S(1)} %shard_map.86), channel_id=1, replica_groups=mesh['zl'=8,'x'=4,'zh'=2,'y'=4,'core'=2] {'x'}, dimensions={0} | all-to-all | bytes 1572864 | tf_op jit(solution)/shard_map/all_to_all | solution.py:27
  57.0 1.4 shard_map.87
  58.4 14.9 %all-to-all-start.2 = ((bf16[16,24,256]{2,1,0:T(8,128)(2,1)}), bf16[16,24,256]{2,1,0:T(8,128)(2,1)S(1)}, u32[]{:S(2)}, u32[]{:S(2)}) async-start(bf16[16,24,256]{2,1,0:T(8,128)(2,1)} %bitcast.15), calls=%async_computation.2 | async-start | bytes 393216 | tf_op jit(solution)/shard_map/all_to_all | solution.py:27
  73.3 0.7 collective-permute-start.7
  74.0 0.0 collective-permute-done.7.states
  74.0 13.3 %all-to-all-done.2 = bf16[16,24,256]{2,1,0:T(8,128)(2,1)S(1)} async-done(((bf16[16,24,256]{2,1,0:T(8,128)(2,1)}), bf16[16,24,256]{2,1,0:T(8,128)(2,1)S(1)}, u32[]{:S(2)}, u32[]{:S(2)}) %all-to-all-start.2) | async-done | bytes 196640 | tf_op jit(solution)/shard_map/all_to_all | solution.py:27
  87.3 0.2 shard_map.88
  87.5 23.6 %all_to_all.31.packed = bf16[16,48,256]{2,1,0:T(8,128)(2,1)S(1)} all-to-all(bf16[16,48,256]{2,1,0:T(8,128)(2,1)S(1)} %shard_map.88), channel_id=1, replica_groups=mesh['zl'=8,'x'=4,'zh'=2,'y'=4,'core'=2] {'zl','zh'}, dimensions={0} | all-to-all | bytes 786432 | tf_op jit(solution)/shard_map/all_to_all | solution.py:27
  111.0 0.6 shard_map.89
  111.7 10.7 %all_to_all.32 = bf16[4,384,256]{2,1,0:T(8,128)(2,1)S(1)} all-to-all(bf16[4,384,256]{2,1,0:T(8,128)(2,1)S(1)} %get-tuple-element.17), channel_id=1, replica_groups=mesh['zl'=8,'x'=4,'zh'=2,'y'=4,'core'=2] {'x'}, dimensions={0} | all-to-all | bytes 1572864 | tf_op jit(solution)/shard_map/all_to_all | solution.py:27
  122.4 2.5 %shard_map.90 = bf16[8,192,256]{2,1,0:T(8,128)(2,1)S(1)} custom-call(s32[11]{0:T(128)S(1)} %stack.62.places, bf16[160,1536]{1,0:T(8,128)(2,1)S(1)} %copy-done, bf16[160,1536]{1,0:T(8,128)(2,1)S(1)} %collective-permute-done.refs_1_, bf16[160,1536]{1,0:T(8,128)(2,1)S(1)} %collective-permute-done.1.refs_2_, ...), custom_call_target="tpu_custom_call" | custom-call | tf_op jit(solution)/shard_map/pallas_call | solution.py:38
  125.0 0.0 copy-start.3
  125.0 25.7 %all_to_all.33.back = bf16[8,192,256]{2,1,0:T(8,128)(2,1)S(1)} all-to-all(bf16[8,192,256]{2,1,0:T(8,128)(2,1)S(1)} %shard_map.90), channel_id=1, replica_groups=mesh['zl'=8,'x'=4,'zh'=2,'y'=4,'core'=2] {'y','core'}, dimensions={0} | all-to-all | bytes 1572864 | tf_op jit(solution)/shard_map/all_to_all | solution.py:27
  150.6 0.0 copy-done.3
  150.7 1.1 shard_map.91
  (1 shorter events, 0.0 us)
Async XLA Ops:
  0.6 25.5 %collective-permute-start.2 = (bf16[160,1536]{1,0:T(8,128)(2,1)}, bf16[160,1536]{1,0:T(8,128)(2,1)S(1)}, u32[]{:S(2)}, u32[]{:S(2)}) collective-permute-start(bf16[160,1536]{1,0:T(8,128)(2,1)} %refs_0_.3), channel_id=1, source_target_pairs={{0,6},{2,0},{4,2},{6,4},{1,7},{3,1},{5,3},{7,5},{8,14},{10,8},{12,... | collective-permute-start | bytes 1474568 | tf_op jit(solution)/shard_map/ppermute | solution.py:32
  6.1 26.7 %collective-permute-start.1 = (bf16[160,1536]{1,0:T(8,128)(2,1)}, bf16[160,1536]{1,0:T(8,128)(2,1)S(1)}, u32[]{:S(2)}, u32[]{:S(2)}) collective-permute-start(bf16[160,1536]{1,0:T(8,128)(2,1)} %refs_0_.3), channel_id=1, source_target_pairs={{0,4},{2,6},{4,0},{6,2},{1,5},{3,7},{5,1},{7,3},{8,12},{10,14},{12... | collective-permute-start | bytes 1474568 | tf_op jit(solution)/shard_map/ppermute | solution.py:32
  8.4 26.4 %collective-permute-start = (bf16[160,1536]{1,0:T(8,128)(2,1)}, bf16[160,1536]{1,0:T(8,128)(2,1)S(1)}, u32[]{:S(2)}, u32[]{:S(2)}) collective-permute-start(bf16[160,1536]{1,0:T(8,128)(2,1)} %refs_0_.3), channel_id=1, source_target_pairs={{0,2},{2,4},{4,6},{6,0},{1,3},{3,5},{5,7},{7,1},{8,10},{10,12},{12... | collective-permute-start | bytes 1474568 | tf_op jit(solution)/shard_map/ppermute | solution.py:32
  11.0 1.1 copy-start.1
  12.1 0.9 copy-start.4
  14.2 9.9 %copy-start = (bf16[160,1536]{1,0:T(8,128)(2,1)S(1)}, bf16[160,1536]{1,0:T(8,128)(2,1)}, u32[]{:S(2)}) copy-start(bf16[160,1536]{1,0:T(8,128)(2,1)} %refs_0_.3) | copy-start | bytes 1474564
  14.2 26.4 %all-to-all-start = ((bf16[8,192,256]{2,1,0:T(8,128)(2,1)}), bf16[8,192,256]{2,1,0:T(8,128)(2,1)S(1)}, u32[]{:S(2)}, u32[]{:S(2)}) async-start(bf16[8,192,256]{2,1,0:T(8,128)(2,1)} %shard_map.85), calls=%async_computation | async-start | bytes 1572864 | tf_op jit(solution)/shard_map/all_to_all | solution.py:27
  24.1 14.0 %copy-start.2 = (f32[24,2048]{1,0:T(8,128)S(1)}, f32[24,2048]{1,0:T(8,128)}, u32[]{:S(2)}) copy-start(f32[24,2048]{1,0:T(8,128)} %second.1) | copy-start | bytes 589828
  24.1 16.5 %collective-permute-start.3 = (bf16[160,1536]{1,0:T(8,128)(2,1)S(1)}, bf16[160,1536]{1,0:T(8,128)(2,1)S(1)}, u32[]{:S(2)}, u32[]{:S(2)}) collective-permute-start(bf16[160,1536]{1,0:T(8,128)(2,1)S(1)} %copy-done), channel_id=1, source_target_pairs={{0,1},{1,0},{2,3},{3,2},{4,5},{5,4},{6,7},{7,6},{8,9},{9,8},{10,11... | collective-permute-start | bytes 1474568 | tf_op jit(solution)/shard_map/ppermute | solution.py:160
  26.2 14.5 %collective-permute-start.6 = (bf16[160,1536]{1,0:T(8,128)(2,1)S(1)}, bf16[160,1536]{1,0:T(8,128)(2,1)}, u32[]{:S(2)}, u32[]{:S(2)}) collective-permute-start(bf16[160,1536]{1,0:T(8,128)(2,1)S(1)} %collective-permute-done.2.refs_3_), channel_id=1, source_target_pairs={{0,1},{1,0},{2,3},{3,2},{4,5},{5,4},{6,7},{7,6},{8,9},{9,8},{10,11... | collective-permute-start | bytes 1474568 | tf_op jit(solution)/shard_map/ppermute | solution.py:160
  32.8 7.8 %collective-permute-start.5 = (bf16[160,1536]{1,0:T(8,128)(2,1)S(1)}, bf16[160,1536]{1,0:T(8,128)(2,1)}, u32[]{:S(2)}, u32[]{:S(2)}) collective-permute-start(bf16[160,1536]{1,0:T(8,128)(2,1)S(1)} %collective-permute-done.1.refs_2_), channel_id=1, source_target_pairs={{0,1},{1,0},{2,3},{3,2},{4,5},{5,4},{6,7},{7,6},{8,9},{9,8},{10,11... | collective-permute-start | bytes 1474568 | tf_op jit(solution)/shard_map/ppermute | solution.py:160
  34.8 5.9 %collective-permute-start.4 = (bf16[160,1536]{1,0:T(8,128)(2,1)S(1)}, bf16[160,1536]{1,0:T(8,128)(2,1)}, u32[]{:S(2)}, u32[]{:S(2)}) collective-permute-start(bf16[160,1536]{1,0:T(8,128)(2,1)S(1)} %collective-permute-done.refs_1_), channel_id=1, source_target_pairs={{0,1},{1,0},{2,3},{3,2},{4,5},{5,4},{6,7},{7,6},{8,9},{9,8},{10,11... | collective-permute-start | bytes 1474568 | tf_op jit(solution)/shard_map/ppermute | solution.py:160
  58.4 28.9 %all-to-all-start.2 = ((bf16[16,24,256]{2,1,0:T(8,128)(2,1)}), bf16[16,24,256]{2,1,0:T(8,128)(2,1)S(1)}, u32[]{:S(2)}, u32[]{:S(2)}) async-start(bf16[16,24,256]{2,1,0:T(8,128)(2,1)} %bitcast.15), calls=%async_computation.2 | async-start | bytes 393216 | tf_op jit(solution)/shard_map/all_to_all | solution.py:27
  73.3 0.7 collective-permute-start.7
  125.0 25.7 %copy-start.3 = (f32[24,2048]{1,0:T(8,128)S(1)}, f32[24,2048]{1,0:T(8,128)}, u32[]{:S(2)}) copy-start(f32[24,2048]{1,0:T(8,128)} %first.1) | copy-start | bytes 589828

commit v9 on v8

--- a/solution.py
+++ b/solution.py
@@ -156,9 +156,6 @@
     group = ("y", "core")
     swap = [(0, 1), (1, 0)]
 
-    near = [act] + [shift(act, "y", k) for k in range(1, ny)]
-    acts = near + [lax.ppermute(a, "core", swap) for a in near]
-
     block = -(-(tok + own) // 16) * 16
     dma = pltpu.SemaphoreType.DMA
     pieces = call(
@@ -175,7 +172,11 @@
         ),
         hbm=True,
     )
+    pieces, late = lax.optimization_barrier((pieces, act))
     got = exchange(pieces, group)
+
+    near = [act] + [shift(late if k == 2 else act, "y", k) for k in range(1, ny)]
+    acts = near + [lax.ppermute(a, "core", swap) for a in near]
 
     me = 2 * y + core
     head = lax.rem(me + nz - zl, nz)

time: 154 us -> 154 us (level)
  starting transfers between devices: 48.8 us -> 51 us
    ppermute x4, starting transfers between devices: 13.1 us -> 16 us  [relay(): acts = near + [lax.ppermute(a, 'core', swap) for a in near]]
    all_to_all x2, waiting for transfers between devices: 15.2 us -> 13.4 us  [exchange(): return lax.all_to_all(pieces, axes, split_axis=0, concat_axis=0, tiled=True)]
where the time goes in v9:
time: 154 us; the launch traced here: 152 us
  blocking collectives  73 us (47%)
  starting transfers between devices  51 us (33%)
  waiting for transfers between devices  13.7 us (9%)
  Pallas kernels  9.51 us (6%)
  local copies, waits for them, and re-layouts  2.85 us (2%)
    all_to_all x4, blocking collectives, exchange(): return lax.all_to_all(pieces, axes, split_axis=0, concat_axis=0, tiled=True)  73 us
    all_to_all x2, starting transfers between devices, exchange(): return lax.all_to_all(pieces, axes, split_axis=0, concat_axis=0, tiled=True)  23.4 us
    ppermute x4, starting transfers between devices, relay(): acts = near + [lax.ppermute(a, 'core', swap) for a in near]  16 us
    all_to_all x2, waiting for transfers between devices, exchange(): return lax.all_to_all(pieces, axes, split_axis=0, concat_axis=0, tiled=True)  13.4 us
    ppermute x3, starting transfers between devices, shift(): return lax.ppermute(a, axis, [(i, (i + k) % n) for i in range(n)])  10.9 us
    pallas_call x7, Pallas kernels, call(): pl.pallas_call(body, out_shape=shapes, in_specs=[pl.BlockSpec(memory_spac...  9.51 us
  transfers between devices with their start and end apart: 10, of which 2 were waited for; matrix products, arithmetic and copies ran while one was open for 1% of the time, Pallas kernels for 1%

profile of v9, /device:TPU:1, one launch (start us, length us, event | category | flops | bytes accessed | tf_op | source)
XLA Modules:
  0.0 151.7 jit_solution(10212364152785331296)
XLA Ops:
  0.6 5.5 %collective-permute-start.2 = (bf16[160,1536]{1,0:T(8,128)(2,1)}, bf16[160,1536]{1,0:T(8,128)(2,1)S(1)}, u32[]{:S(2)}, u32[]{:S(2)}) collective-permute-start(bf16[160,1536]{1,0:T(8,128)(2,1)} %refs_0_.3), channel_id=1, source_target_pairs={{0,6},{2,0},{4,2},{6,4},{1,7},{3,1},{5,3},{7,5},{8,14},{10,8},{12,... | collective-permute-start | bytes 1474568 | tf_op jit(solution)/shard_map/ppermute | solution.py:32
  6.1 1.9 %collective-permute-start = (bf16[160,1536]{1,0:T(8,128)(2,1)}, bf16[160,1536]{1,0:T(8,128)(2,1)S(1)}, u32[]{:S(2)}, u32[]{:S(2)}) collective-permute-start(bf16[160,1536]{1,0:T(8,128)(2,1)} %refs_0_.3), channel_id=1, source_target_pairs={{0,2},{2,4},{4,6},{6,0},{1,3},{3,5},{5,7},{7,1},{8,10},{10,12},{12... | collective-permute-start | bytes 1474568 | tf_op jit(solution)/shard_map/ppermute | solution.py:32
  8.0 0.0 copy-start.1
  8.0 1.1 copy-done.1
  9.1 0.0 copy-start.4
  9.1 0.9 copy-done.4
  10.1 0.0 copy-start
  10.1 1.2 shard_map.85
  11.3 0.0 copy-done
  11.3 3.5 %collective-permute-start.1 = (bf16[160,1536]{1,0:T(8,128)(2,1)S(1)}, bf16[160,1536]{1,0:T(8,128)(2,1)S(1)}, u32[]{:S(2)}, u32[]{:S(2)}) collective-permute-start(bf16[160,1536]{1,0:T(8,128)(2,1)S(1)} %copy-done), channel_id=1, source_target_pairs={{0,4},{2,6},{4,0},{6,2},{1,5},{3,7},{5,1},{7,3},{8,12},{10,14},{12... | collective-permute-start | bytes 1474568 | tf_op jit(solution)/shard_map/ppermute | solution.py:32
  14.8 8.5 %all-to-all-start = ((bf16[8,192,256]{2,1,0:T(8,128)(2,1)}), bf16[8,192,256]{2,1,0:T(8,128)(2,1)S(1)}, u32[]{:S(2)}, u32[]{:S(2)}) async-start(bf16[8,192,256]{2,1,0:T(8,128)(2,1)} %shard_map.85), calls=%async_computation | async-start | bytes 1572864 | tf_op jit(solution)/shard_map/all_to_all | solution.py:27
  23.3 0.0 copy-start.2
  23.3 2.0 %collective-permute-start.3 = (bf16[160,1536]{1,0:T(8,128)(2,1)S(1)}, bf16[160,1536]{1,0:T(8,128)(2,1)S(1)}, u32[]{:S(2)}, u32[]{:S(2)}) collective-permute-start(bf16[160,1536]{1,0:T(8,128)(2,1)S(1)} %copy-done), channel_id=1, source_target_pairs={{0,1},{1,0},{2,3},{3,2},{4,5},{5,4},{6,7},{7,6},{8,9},{9,8},{10,11... | collective-permute-start | bytes 1474568 | tf_op jit(solution)/shard_map/ppermute | solution.py:179
  25.4 0.0 collective-permute-done.2.refs_3_
  25.4 4.7 %collective-permute-start.6 = (bf16[160,1536]{1,0:T(8,128)(2,1)S(1)}, bf16[160,1536]{1,0:T(8,128)(2,1)}, u32[]{:S(2)}, u32[]{:S(2)}) collective-permute-start(bf16[160,1536]{1,0:T(8,128)(2,1)S(1)} %collective-permute-done.2.refs_3_), channel_id=1, source_target_pairs={{0,1},{1,0},{2,3},{3,2},{4,5},{5,4},{6,7},{7,6},{8,9},{9,8},{10,11... | collective-permute-start | bytes 1474568 | tf_op jit(solution)/shard_map/ppermute | solution.py:179
  30.1 0.0 collective-permute-done.refs_1_
  30.1 7.3 %collective-permute-start.4 = (bf16[160,1536]{1,0:T(8,128)(2,1)S(1)}, bf16[160,1536]{1,0:T(8,128)(2,1)}, u32[]{:S(2)}, u32[]{:S(2)}) collective-permute-start(bf16[160,1536]{1,0:T(8,128)(2,1)S(1)} %collective-permute-done.refs_1_), channel_id=1, source_target_pairs={{0,1},{1,0},{2,3},{3,2},{4,5},{5,4},{6,7},{7,6},{8,9},{9,8},{10,11... | collective-permute-start | bytes 1474568 | tf_op jit(solution)/shard_map/ppermute | solution.py:179
  37.4 0.0 collective-permute-done.1.refs_2_
  37.4 1.9 %collective-permute-start.5 = (bf16[160,1536]{1,0:T(8,128)(2,1)S(1)}, bf16[160,1536]{1,0:T(8,128)(2,1)}, u32[]{:S(2)}, u32[]{:S(2)}) collective-permute-start(bf16[160,1536]{1,0:T(8,128)(2,1)S(1)} %collective-permute-done.1.refs_2_), channel_id=1, source_target_pairs={{0,1},{1,0},{2,3},{3,2},{4,5},{5,4},{6,7},{7,6},{8,9},{9,8},{10,11... | collective-permute-start | bytes 1474568 | tf_op jit(solution)/shard_map/ppermute | solution.py:179
  39.4 0.1 stack.62.places
  39.5 0.7 bitcast_convert_fusion
  40.2 0.0 copy-done.2
  40.2 0.7 dynamic-slice_bitcast_fusion
  40.9 0.0 all-to-all-done.refs_8_
  40.9 0.0 collective-permute-done.3.refs_4_
  41.0 0.0 collective-permute-done.6.refs_7_
  41.0 0.0 collective-permute-done.4.refs_5_
  41.0 0.3 collective-permute-done.5.refs_6_
  41.3 2.6 %shard_map.86 = bf16[4,384,256]{2,1,0:T(8,128)(2,1)S(1)} custom-call(s32[11]{0:T(128)S(1)} %stack.62.places, bf16[160,1536]{1,0:T(8,128)(2,1)S(1)} %copy-done, bf16[160,1536]{1,0:T(8,128)(2,1)S(1)} %collective-permute-done.refs_1_, bf16[160,1536]{1,0:T(8,128)(2,1)S(1)} %collective-permute-done.1.refs_2_, ...), custom_call_target="tpu_custom_call" | custom-call | tf_op jit(solution)/shard_map/pallas_call | solution.py:38
  43.9 15.1 %all_to_all.30.arrived = bf16[4,384,256]{2,1,0:T(8,128)(2,1)S(1)} all-to-all(bf16[4,384,256]{2,1,0:T(8,128)(2,1)S(1)} %shard_map.86), channel_id=1, replica_groups=mesh['zl'=8,'x'=4,'zh'=2,'y'=4,'core'=2] {'x'}, dimensions={0} | all-to-all | bytes 1572864 | tf_op jit(solution)/shard_map/all_to_all | solution.py:27
  59.0 1.4 shard_map.87
  60.4 14.9 %all-to-all-start.2 = ((bf16[16,24,256]{2,1,0:T(8,128)(2,1)}), bf16[16,24,256]{2,1,0:T(8,128)(2,1)S(1)}, u32[]{:S(2)}, u32[]{:S(2)}) async-start(bf16[16,24,256]{2,1,0:T(8,128)(2,1)} %bitcast.15), calls=%async_computation.2 | async-start | bytes 393216 | tf_op jit(solution)/shard_map/all_to_all | solution.py:27
  75.3 0.7 collective-permute-start.7
  76.0 0.0 collective-permute-done.7.states
  76.0 13.3 %all-to-all-done.2 = bf16[16,24,256]{2,1,0:T(8,128)(2,1)S(1)} async-done(((bf16[16,24,256]{2,1,0:T(8,128)(2,1)}), bf16[16,24,256]{2,1,0:T(8,128)(2,1)S(1)}, u32[]{:S(2)}, u32[]{:S(2)}) %all-to-all-start.2) | async-done | bytes 196640 | tf_op jit(solution)/shard_map/all_to_all | solution.py:27
  89.3 0.2 shard_map.88
  89.5 25.4 %all_to_all.31.packed = bf16[16,48,256]{2,1,0:T(8,128)(2,1)S(1)} all-to-all(bf16[16,48,256]{2,1,0:T(8,128)(2,1)S(1)} %shard_map.88), channel_id=1, replica_groups=mesh['zl'=8,'x'=4,'zh'=2,'y'=4,'core'=2] {'zl','zh'}, dimensions={0} | all-to-all | bytes 786432 | tf_op jit(solution)/shard_map/all_to_all | solution.py:27
  114.9 0.6 shard_map.89
  115.5 10.7 %all_to_all.32 = bf16[4,384,256]{2,1,0:T(8,128)(2,1)S(1)} all-to-all(bf16[4,384,256]{2,1,0:T(8,128)(2,1)S(1)} %get-tuple-element.21), channel_id=1, replica_groups=mesh['zl'=8,'x'=4,'zh'=2,'y'=4,'core'=2] {'x'}, dimensions={0} | all-to-all | bytes 1572864 | tf_op jit(solution)/shard_map/all_to_all | solution.py:27
  126.3 2.5 %shard_map.90 = bf16[8,192,256]{2,1,0:T(8,128)(2,1)S(1)} custom-call(s32[11]{0:T(128)S(1)} %stack.62.places, bf16[160,1536]{1,0:T(8,128)(2,1)S(1)} %copy-done, bf16[160,1536]{1,0:T(8,128)(2,1)S(1)} %collective-permute-done.refs_1_, bf16[160,1536]{1,0:T(8,128)(2,1)S(1)} %collective-permute-done.1.refs_2_, ...), custom_call_target="tpu_custom_call" | custom-call | tf_op jit(solution)/shard_map/pallas_call | solution.py:38
  128.8 0.0 copy-start.3
  128.8 21.8 %all_to_all.33.back = bf16[8,192,256]{2,1,0:T(8,128)(2,1)S(1)} all-to-all(bf16[8,192,256]{2,1,0:T(8,128)(2,1)S(1)} %shard_map.90), channel_id=1, replica_groups=mesh['zl'=8,'x'=4,'zh'=2,'y'=4,'core'=2] {'y','core'}, dimensions={0} | all-to-all | bytes 1572864 | tf_op jit(solution)/shard_map/all_to_all | solution.py:27
  150.6 0.0 copy-done.3
  150.6 1.1 shard_map.91
  (1 shorter events, 0.0 us)
Async XLA Ops:
  0.6 24.8 %collective-permute-start.2 = (bf16[160,1536]{1,0:T(8,128)(2,1)}, bf16[160,1536]{1,0:T(8,128)(2,1)S(1)}, u32[]{:S(2)}, u32[]{:S(2)}) collective-permute-start(bf16[160,1536]{1,0:T(8,128)(2,1)} %refs_0_.3), channel_id=1, source_target_pairs={{0,6},{2,0},{4,2},{6,4},{1,7},{3,1},{5,3},{7,5},{8,14},{10,8},{12,... | collective-permute-start | bytes 1474568 | tf_op jit(solution)/shard_map/ppermute | solution.py:32
  6.1 24.0 %collective-permute-start = (bf16[160,1536]{1,0:T(8,128)(2,1)}, bf16[160,1536]{1,0:T(8,128)(2,1)S(1)}, u32[]{:S(2)}, u32[]{:S(2)}) collective-permute-start(bf16[160,1536]{1,0:T(8,128)(2,1)} %refs_0_.3), channel_id=1, source_target_pairs={{0,2},{2,4},{4,6},{6,0},{1,3},{3,5},{5,7},{7,1},{8,10},{10,12},{12... | collective-permute-start | bytes 1474568 | tf_op jit(solution)/shard_map/ppermute | solution.py:32
  8.0 1.1 copy-start.1
  9.1 0.9 copy-start.4
  10.1 1.2 copy-start
  11.3 26.1 %collective-permute-start.1 = (bf16[160,1536]{1,0:T(8,128)(2,1)S(1)}, bf16[160,1536]{1,0:T(8,128)(2,1)S(1)}, u32[]{:S(2)}, u32[]{:S(2)}) collective-permute-start(bf16[160,1536]{1,0:T(8,128)(2,1)S(1)} %copy-done), channel_id=1, source_target_pairs={{0,4},{2,6},{4,0},{6,2},{1,5},{3,7},{5,1},{7,3},{8,12},{10,14},{12... | collective-permute-start | bytes 1474568 | tf_op jit(solution)/shard_map/ppermute | solution.py:32
  14.8 26.1 %all-to-all-start = ((bf16[8,192,256]{2,1,0:T(8,128)(2,1)}), bf16[8,192,256]{2,1,0:T(8,128)(2,1)S(1)}, u32[]{:S(2)}, u32[]{:S(2)}) async-start(bf16[8,192,256]{2,1,0:T(8,128)(2,1)} %shard_map.85), calls=%async_computation | async-start | bytes 1572864 | tf_op jit(solution)/shard_map/all_to_all | solution.py:27
  23.3 16.8 %copy-start.2 = (f32[24,2048]{1,0:T(8,128)S(1)}, f32[24,2048]{1,0:T(8,128)}, u32[]{:S(2)}) copy-start(f32[24,2048]{1,0:T(8,128)} %second.1) | copy-start | bytes 589828
  23.3 17.6 %collective-permute-start.3 = (bf16[160,1536]{1,0:T(8,128)(2,1)S(1)}, bf16[160,1536]{1,0:T(8,128)(2,1)S(1)}, u32[]{:S(2)}, u32[]{:S(2)}) collective-permute-start(bf16[160,1536]{1,0:T(8,128)(2,1)S(1)} %copy-done), channel_id=1, source_target_pairs={{0,1},{1,0},{2,3},{3,2},{4,5},{5,4},{6,7},{7,6},{8,9},{9,8},{10,11... | collective-permute-start | bytes 1474568 | tf_op jit(solution)/shard_map/ppermute | solution.py:179
  25.4 15.6 %collective-permute-start.6 = (bf16[160,1536]{1,0:T(8,128)(2,1)S(1)}, bf16[160,1536]{1,0:T(8,128)(2,1)}, u32[]{:S(2)}, u32[]{:S(2)}) collective-permute-start(bf16[160,1536]{1,0:T(8,128)(2,1)S(1)} %collective-permute-done.2.refs_3_), channel_id=1, source_target_pairs={{0,1},{1,0},{2,3},{3,2},{4,5},{5,4},{6,7},{7,6},{8,9},{9,8},{10,11... | collective-permute-start | bytes 1474568 | tf_op jit(solution)/shard_map/ppermute | solution.py:179
  30.1 10.8 %collective-permute-start.4 = (bf16[160,1536]{1,0:T(8,128)(2,1)S(1)}, bf16[160,1536]{1,0:T(8,128)(2,1)}, u32[]{:S(2)}, u32[]{:S(2)}) collective-permute-start(bf16[160,1536]{1,0:T(8,128)(2,1)S(1)} %collective-permute-done.refs_1_), channel_id=1, source_target_pairs={{0,1},{1,0},{2,3},{3,2},{4,5},{5,4},{6,7},{7,6},{8,9},{9,8},{10,11... | collective-permute-start | bytes 1474568 | tf_op jit(solution)/shard_map/ppermute | solution.py:179
  37.4 3.9 %collective-permute-start.5 = (bf16[160,1536]{1,0:T(8,128)(2,1)S(1)}, bf16[160,1536]{1,0:T(8,128)(2,1)}, u32[]{:S(2)}, u32[]{:S(2)}) collective-permute-start(bf16[160,1536]{1,0:T(8,128)(2,1)S(1)} %collective-permute-done.1.refs_2_), channel_id=1, source_target_pairs={{0,1},{1,0},{2,3},{3,2},{4,5},{5,4},{6,7},{7,6},{8,9},{9,8},{10,11... | collective-permute-start | bytes 1474568 | tf_op jit(solution)/shard_map/ppermute | solution.py:179
  60.4 29.0 %all-to-all-start.2 = ((bf16[16,24,256]{2,1,0:T(8,128)(2,1)}), bf16[16,24,256]{2,1,0:T(8,128)(2,1)S(1)}, u32[]{:S(2)}, u32[]{:S(2)}) async-start(bf16[16,24,256]{2,1,0:T(8,128)(2,1)} %bitcast.15), calls=%async_computation.2 | async-start | bytes 393216 | tf_op jit(solution)/shard_map/all_to_all | solution.py:27
  75.3 0.7 collective-permute-start.7
  128.8 21.8 %copy-start.3 = (f32[24,2048]{1,0:T(8,128)S(1)}, f32[24,2048]{1,0:T(8,128)}, u32[]{:S(2)}) copy-start(f32[24,2048]{1,0:T(8,128)} %first.1) | copy-start | bytes 589828

commit v10 on v8

--- a/solution.py
+++ b/solution.py
@@ -32,8 +32,9 @@
     return lax.ppermute(a, axis, [(i, (i + k) % n) for i in range(n)])
 
 
-def call(body, shapes, *args, scratch=(), hbm=False):
+def call(body, shapes, *args, scratch=(), hbm=False, stay=()):
     spaces = [pltpu.SMEM if a.dtype == jnp.int32 else pltpu.HBM if hbm else pltpu.VMEM for a in args]
+    spaces = [pl.ANY if n in stay else m for n, m in enumerate(spaces)]
     out = pl.BlockSpec(memory_space=pltpu.HBM if hbm else pltpu.VMEM)
     return pl.pallas_call(
         body,
@@ -130,12 +131,23 @@
 
 
 def project(places, *refs):
-    *acts, weight, grad, out = refs
+    *acts, weight, grad, out, fetched, sems = refs
+    here = len(acts) - fetched.shape[0]
+    copies = [
+        pltpu.make_async_copy(a, fetched.at[n], sems.at[n]) for n, a in enumerate(acts[here:])
+    ]
+    for copy in copies:
+        copy.start()
     tok = acts[0].shape[0]
-    for j, a in enumerate(acts):
-        block = jnp.dot(a[...], weight[...], preferred_element_type=F32)
+    out[:, tok:, :] = grad[...]
+    for j in range(len(acts)):
+        if j < here:
+            act = acts[j][...]
+        else:
+            copies[j - here].wait()
+            act = fetched[j - here]
+        block = jnp.dot(act, weight[...], preferred_element_type=F32)
         out[places[j], :tok, :] = block.astype(BF16)
-    out[:, tok:, :] = grad[...]
 
 
 def finish(back, first, second, projected, new_first, new_second):
@@ -214,7 +226,9 @@
     head_weight = exchange(sent, "x").reshape(depth, HEAD_SIZE)
 
     out = jax.ShapeDtypeStruct((nz, block, HEAD_SIZE), BF16)
-    out = call(project, out, places, *acts, head_weight, row_grad)
+    fetch = (pltpu.VMEM((ny, tok, depth), BF16), dma((ny,)))
+    stay = range(1 + ny, 1 + 2 * ny)
+    out = call(project, out, places, *acts, head_weight, row_grad, scratch=fetch, stay=stay)
     back = exchange(out, group)
     state = jax.ShapeDtypeStruct(first.shape, F32)
     shapes = (jax.ShapeDtypeStruct(cot.shape, BF16), state, state)

time: 154 us -> 155 us (level)
  no operation moved by 1% of the time
where the time goes in v10:
time: 155 us; the launch traced here: 153 us
  blocking collectives  73.8 us (48%)
  starting transfers between devices  48.8 us (31%)
  waiting for transfers between devices  15.2 us (10%)
  Pallas kernels  10.4 us (7%)
  local copies, waits for them, and re-layouts  2.85 us (2%)
    all_to_all x4, blocking collectives, exchange(): return lax.all_to_all(pieces, axes, split_axis=0, concat_axis=0, tiled=True)  73.8 us
    all_to_all x2, starting transfers between devices, exchange(): return lax.all_to_all(pieces, axes, split_axis=0, concat_axis=0, tiled=True)  24.8 us
    all_to_all x2, waiting for transfers between devices, exchange(): return lax.all_to_all(pieces, axes, split_axis=0, concat_axis=0, tiled=True)  15.2 us
    ppermute x4, starting transfers between devices, relay(): acts = near + [lax.ppermute(a, 'core', swap) for a in near]  13.1 us
    pallas_call x7, Pallas kernels, call(): pl.pallas_call(body, out_shape=shapes, in_specs=[pl.BlockSpec(memory_spac...  10.4 us
    ppermute x3, starting transfers between devices, shift(): return lax.ppermute(a, axis, [(i, (i + k) % n) for i in range(n)])  10.3 us
  transfers between devices with their start and end apart: 10, of which 2 were waited for; matrix products, arithmetic and copies ran while one was open for 1% of the time, Pallas kernels for 1%

profile of v10, /device:TPU:1, one launch (start us, length us, event | category | flops | bytes accessed | tf_op | source)
XLA Modules:
  0.0 152.6 jit_solution(7135954512231689494)
XLA Ops:
  0.6 5.5 %collective-permute-start.2 = (bf16[160,1536]{1,0:T(8,128)(2,1)}, bf16[160,1536]{1,0:T(8,128)(2,1)S(1)}, u32[]{:S(2)}, u32[]{:S(2)}) collective-permute-start(bf16[160,1536]{1,0:T(8,128)(2,1)} %refs_0_.3), channel_id=1, source_target_pairs={{0,6},{2,0},{4,2},{6,4},{1,7},{3,1},{5,3},{7,5},{8,14},{10,8},{12,... | collective-permute-start | bytes 1474568 | tf_op jit(solution)/shard_map/ppermute | solution.py:32
  6.1 2.3 %collective-permute-start.1 = (bf16[160,1536]{1,0:T(8,128)(2,1)}, bf16[160,1536]{1,0:T(8,128)(2,1)S(1)}, u32[]{:S(2)}, u32[]{:S(2)}) collective-permute-start(bf16[160,1536]{1,0:T(8,128)(2,1)} %refs_0_.3), channel_id=1, source_target_pairs={{0,4},{2,6},{4,0},{6,2},{1,5},{3,7},{5,1},{7,3},{8,12},{10,14},{12... | collective-permute-start | bytes 1474568 | tf_op jit(solution)/shard_map/ppermute | solution.py:32
  8.4 2.6 %collective-permute-start = (bf16[160,1536]{1,0:T(8,128)(2,1)}, bf16[160,1536]{1,0:T(8,128)(2,1)S(1)}, u32[]{:S(2)}, u32[]{:S(2)}) collective-permute-start(bf16[160,1536]{1,0:T(8,128)(2,1)} %refs_0_.3), channel_id=1, source_target_pairs={{0,2},{2,4},{4,6},{6,0},{1,3},{3,5},{5,7},{7,1},{8,10},{10,12},{12... | collective-permute-start | bytes 1474568 | tf_op jit(solution)/shard_map/ppermute | solution.py:32
  11.0 0.0 copy-start.1
  11.0 1.1 copy-done.1
  12.1 0.0 copy-start.4
  12.1 0.9 copy-done.4
  13.0 1.2 shard_map.85
  14.2 0.0 copy-start
  14.2 9.9 %all-to-all-start = ((bf16[8,192,256]{2,1,0:T(8,128)(2,1)}), bf16[8,192,256]{2,1,0:T(8,128)(2,1)S(1)}, u32[]{:S(2)}, u32[]{:S(2)}) async-start(bf16[8,192,256]{2,1,0:T(8,128)(2,1)} %shard_map.85), calls=%async_computation | async-start | bytes 1572864 | tf_op jit(solution)/shard_map/all_to_all | solution.py:27
  24.1 0.0 copy-done
  24.1 0.0 copy-start.2
  24.1 2.1 %collective-permute-start.3 = (bf16[160,1536]{1,0:T(8,128)(2,1)S(1)}, bf16[160,1536]{1,0:T(8,128)(2,1)S(1)}, u32[]{:S(2)}, u32[]{:S(2)}) collective-permute-start(bf16[160,1536]{1,0:T(8,128)(2,1)S(1)} %copy-done), channel_id=1, source_target_pairs={{0,1},{1,0},{2,3},{3,2},{4,5},{5,4},{6,7},{7,6},{8,9},{9,8},{10,11... | collective-permute-start | bytes 1474568 | tf_op jit(solution)/shard_map/ppermute | solution.py:172
  26.1 0.0 collective-permute-done.2.refs_3_
  26.2 6.7 %collective-permute-start.6 = (bf16[160,1536]{1,0:T(8,128)(2,1)S(1)}, bf16[160,1536]{1,0:T(8,128)(2,1)}, u32[]{:S(2)}, u32[]{:S(2)}) collective-permute-start(bf16[160,1536]{1,0:T(8,128)(2,1)S(1)} %collective-permute-done.2.refs_3_), channel_id=1, source_target_pairs={{0,1},{1,0},{2,3},{3,2},{4,5},{5,4},{6,7},{7,6},{8,9},{9,8},{10,11... | collective-permute-start | bytes 1474568 | tf_op jit(solution)/shard_map/ppermute | solution.py:172
  32.8 0.0 collective-permute-done.1.refs_2_
  32.8 1.9 %collective-permute-start.5 = (bf16[160,1536]{1,0:T(8,128)(2,1)S(1)}, bf16[160,1536]{1,0:T(8,128)(2,1)}, u32[]{:S(2)}, u32[]{:S(2)}) collective-permute-start(bf16[160,1536]{1,0:T(8,128)(2,1)S(1)} %collective-permute-done.1.refs_2_), channel_id=1, source_target_pairs={{0,1},{1,0},{2,3},{3,2},{4,5},{5,4},{6,7},{7,6},{8,9},{9,8},{10,11... | collective-permute-start | bytes 1474568 | tf_op jit(solution)/shard_map/ppermute | solution.py:172
  34.8 0.0 collective-permute-done.refs_1_
  34.8 2.4 %collective-permute-start.4 = (bf16[160,1536]{1,0:T(8,128)(2,1)S(1)}, bf16[160,1536]{1,0:T(8,128)(2,1)}, u32[]{:S(2)}, u32[]{:S(2)}) collective-permute-start(bf16[160,1536]{1,0:T(8,128)(2,1)S(1)} %collective-permute-done.refs_1_), channel_id=1, source_target_pairs={{0,1},{1,0},{2,3},{3,2},{4,5},{5,4},{6,7},{7,6},{8,9},{9,8},{10,11... | collective-permute-start | bytes 1474568 | tf_op jit(solution)/shard_map/ppermute | solution.py:172
  37.2 0.1 stack.62.places
  37.3 0.7 bitcast_convert_fusion
  38.0 0.0 copy-done.2
  38.0 0.7 dynamic-slice_bitcast_fusion
  38.8 1.8 %all-to-all-done.refs_8_ = bf16[8,192,256]{2,1,0:T(8,128)(2,1)S(1)} async-done(((bf16[8,192,256]{2,1,0:T(8,128)(2,1)}), bf16[8,192,256]{2,1,0:T(8,128)(2,1)S(1)}, u32[]{:S(2)}, u32[]{:S(2)}) %all-to-all-start) | async-done | bytes 786464 | tf_op jit(solution)/shard_map/all_to_all | solution.py:27
  40.6 0.0 collective-permute-done.3.refs_4_
  40.6 0.0 collective-permute-done.6.refs_7_
  40.6 0.0 collective-permute-done.5.refs_6_
  40.6 0.0 collective-permute-done.4.refs_5_
  40.6 2.6 %shard_map.86 = bf16[4,384,256]{2,1,0:T(8,128)(2,1)S(1)} custom-call(s32[11]{0:T(128)S(1)} %stack.62.places, bf16[160,1536]{1,0:T(8,128)(2,1)S(1)} %copy-done, bf16[160,1536]{1,0:T(8,128)(2,1)S(1)} %collective-permute-done.refs_1_, bf16[160,1536]{1,0:T(8,128)(2,1)S(1)} %collective-permute-done.1.refs_2_, ...), custom_call_target="tpu_custom_call" | custom-call | tf_op jit(solution)/shard_map/pallas_call | solution.py:39
  43.2 13.8 %all_to_all.30.arrived = bf16[4,384,256]{2,1,0:T(8,128)(2,1)S(1)} all-to-all(bf16[4,384,256]{2,1,0:T(8,128)(2,1)S(1)} %shard_map.86), channel_id=1, replica_groups=mesh['zl'=8,'x'=4,'zh'=2,'y'=4,'core'=2] {'x'}, dimensions={0} | all-to-all | bytes 1572864 | tf_op jit(solution)/shard_map/all_to_all | solution.py:27
  57.0 1.4 shard_map.87
  58.4 14.9 %all-to-all-start.2 = ((bf16[16,24,256]{2,1,0:T(8,128)(2,1)}), bf16[16,24,256]{2,1,0:T(8,128)(2,1)S(1)}, u32[]{:S(2)}, u32[]{:S(2)}) async-start(bf16[16,24,256]{2,1,0:T(8,128)(2,1)} %bitcast.15), calls=%async_computation.2 | async-start | bytes 393216 | tf_op jit(solution)/shard_map/all_to_all | solution.py:27
  73.3 0.7 collective-permute-start.7
  74.0 0.0 collective-permute-done.7.states
  74.0 13.3 %all-to-all-done.2 = bf16[16,24,256]{2,1,0:T(8,128)(2,1)S(1)} async-done(((bf16[16,24,256]{2,1,0:T(8,128)(2,1)}), bf16[16,24,256]{2,1,0:T(8,128)(2,1)S(1)}, u32[]{:S(2)}, u32[]{:S(2)}) %all-to-all-start.2) | async-done | bytes 196640 | tf_op jit(solution)/shard_map/all_to_all | solution.py:27
  87.3 0.2 shard_map.88
  87.5 23.6 %all_to_all.31.packed = bf16[16,48,256]{2,1,0:T(8,128)(2,1)S(1)} all-to-all(bf16[16,48,256]{2,1,0:T(8,128)(2,1)S(1)} %shard_map.88), channel_id=1, replica_groups=mesh['zl'=8,'x'=4,'zh'=2,'y'=4,'core'=2] {'zl','zh'}, dimensions={0} | all-to-all | bytes 786432 | tf_op jit(solution)/shard_map/all_to_all | solution.py:27
  111.0 0.6 shard_map.89
  111.7 10.7 %all_to_all.32 = bf16[4,384,256]{2,1,0:T(8,128)(2,1)S(1)} all-to-all(bf16[4,384,256]{2,1,0:T(8,128)(2,1)S(1)} %get-tuple-element.17), channel_id=1, replica_groups=mesh['zl'=8,'x'=4,'zh'=2,'y'=4,'core'=2] {'x'}, dimensions={0} | all-to-all | bytes 1572864 | tf_op jit(solution)/shard_map/all_to_all | solution.py:27
  122.4 3.4 %shard_map.90 = bf16[8,192,256]{2,1,0:T(8,128)(2,1)S(1)} custom-call(s32[11]{0:T(128)S(1)} %stack.62.places, bf16[160,1536]{1,0:T(8,128)(2,1)S(1)} %copy-done, bf16[160,1536]{1,0:T(8,128)(2,1)S(1)} %collective-permute-done.refs_1_, bf16[160,1536]{1,0:T(8,128)(2,1)S(1)} %collective-permute-done.1.refs_2_, ...), custom_call_target="tpu_custom_call" | custom-call | tf_op jit(solution)/shard_map/pallas_call | solution.py:39
  125.8 0.0 copy-start.3
  125.8 25.7 %all_to_all.33.back = bf16[8,192,256]{2,1,0:T(8,128)(2,1)S(1)} all-to-all(bf16[8,192,256]{2,1,0:T(8,128)(2,1)S(1)} %shard_map.90), channel_id=1, replica_groups=mesh['zl'=8,'x'=4,'zh'=2,'y'=4,'core'=2] {'y','core'}, dimensions={0} | all-to-all | bytes 1572864 | tf_op jit(solution)/shard_map/all_to_all | solution.py:27
  151.5 0.0 copy-done.3
  151.5 1.1 shard_map.91
  (1 shorter events, 0.0 us)
Async XLA Ops:
  0.6 25.5 %collective-permute-start.2 = (bf16[160,1536]{1,0:T(8,128)(2,1)}, bf16[160,1536]{1,0:T(8,128)(2,1)S(1)}, u32[]{:S(2)}, u32[]{:S(2)}) collective-permute-start(bf16[160,1536]{1,0:T(8,128)(2,1)} %refs_0_.3), channel_id=1, source_target_pairs={{0,6},{2,0},{4,2},{6,4},{1,7},{3,1},{5,3},{7,5},{8,14},{10,8},{12,... | collective-permute-start | bytes 1474568 | tf_op jit(solution)/shard_map/ppermute | solution.py:32
  6.1 26.7 %collective-permute-start.1 = (bf16[160,1536]{1,0:T(8,128)(2,1)}, bf16[160,1536]{1,0:T(8,128)(2,1)S(1)}, u32[]{:S(2)}, u32[]{:S(2)}) collective-permute-start(bf16[160,1536]{1,0:T(8,128)(2,1)} %refs_0_.3), channel_id=1, source_target_pairs={{0,4},{2,6},{4,0},{6,2},{1,5},{3,7},{5,1},{7,3},{8,12},{10,14},{12... | collective-permute-start | bytes 1474568 | tf_op jit(solution)/shard_map/ppermute | solution.py:32
  8.4 26.4 %collective-permute-start = (bf16[160,1536]{1,0:T(8,128)(2,1)}, bf16[160,1536]{1,0:T(8,128)(2,1)S(1)}, u32[]{:S(2)}, u32[]{:S(2)}) collective-permute-start(bf16[160,1536]{1,0:T(8,128)(2,1)} %refs_0_.3), channel_id=1, source_target_pairs={{0,2},{2,4},{4,6},{6,0},{1,3},{3,5},{5,7},{7,1},{8,10},{10,12},{12... | collective-permute-start | bytes 1474568 | tf_op jit(solution)/shard_map/ppermute | solution.py:32
  11.0 1.1 copy-start.1
  12.1 0.9 copy-start.4
  14.2 9.9 %copy-start = (bf16[160,1536]{1,0:T(8,128)(2,1)S(1)}, bf16[160,1536]{1,0:T(8,128)(2,1)}, u32[]{:S(2)}) copy-start(bf16[160,1536]{1,0:T(8,128)(2,1)} %refs_0_.3) | copy-start | bytes 1474564
  14.2 26.4 %all-to-all-start = ((bf16[8,192,256]{2,1,0:T(8,128)(2,1)}), bf16[8,192,256]{2,1,0:T(8,128)(2,1)S(1)}, u32[]{:S(2)}, u32[]{:S(2)}) async-start(bf16[8,192,256]{2,1,0:T(8,128)(2,1)} %shard_map.85), calls=%async_computation | async-start | bytes 1572864 | tf_op jit(solution)/shard_map/all_to_all | solution.py:27
  24.1 14.0 %copy-start.2 = (f32[24,2048]{1,0:T(8,128)S(1)}, f32[24,2048]{1,0:T(8,128)}, u32[]{:S(2)}) copy-start(f32[24,2048]{1,0:T(8,128)} %second.1) | copy-start | bytes 589828
  24.1 16.5 %collective-permute-start.3 = (bf16[160,1536]{1,0:T(8,128)(2,1)S(1)}, bf16[160,1536]{1,0:T(8,128)(2,1)S(1)}, u32[]{:S(2)}, u32[]{:S(2)}) collective-permute-start(bf16[160,1536]{1,0:T(8,128)(2,1)S(1)} %copy-done), channel_id=1, source_target_pairs={{0,1},{1,0},{2,3},{3,2},{4,5},{5,4},{6,7},{7,6},{8,9},{9,8},{10,11... | collective-permute-start | bytes 1474568 | tf_op jit(solution)/shard_map/ppermute | solution.py:172
  26.2 14.5 %collective-permute-start.6 = (bf16[160,1536]{1,0:T(8,128)(2,1)S(1)}, bf16[160,1536]{1,0:T(8,128)(2,1)}, u32[]{:S(2)}, u32[]{:S(2)}) collective-permute-start(bf16[160,1536]{1,0:T(8,128)(2,1)S(1)} %collective-permute-done.2.refs_3_), channel_id=1, source_target_pairs={{0,1},{1,0},{2,3},{3,2},{4,5},{5,4},{6,7},{7,6},{8,9},{9,8},{10,11... | collective-permute-start | bytes 1474568 | tf_op jit(solution)/shard_map/ppermute | solution.py:172
  32.8 7.8 %collective-permute-start.5 = (bf16[160,1536]{1,0:T(8,128)(2,1)S(1)}, bf16[160,1536]{1,0:T(8,128)(2,1)}, u32[]{:S(2)}, u32[]{:S(2)}) collective-permute-start(bf16[160,1536]{1,0:T(8,128)(2,1)S(1)} %collective-permute-done.1.refs_2_), channel_id=1, source_target_pairs={{0,1},{1,0},{2,3},{3,2},{4,5},{5,4},{6,7},{7,6},{8,9},{9,8},{10,11... | collective-permute-start | bytes 1474568 | tf_op jit(solution)/shard_map/ppermute | solution.py:172
  34.8 5.9 %collective-permute-start.4 = (bf16[160,1536]{1,0:T(8,128)(2,1)S(1)}, bf16[160,1536]{1,0:T(8,128)(2,1)}, u32[]{:S(2)}, u32[]{:S(2)}) collective-permute-start(bf16[160,1536]{1,0:T(8,128)(2,1)S(1)} %collective-permute-done.refs_1_), channel_id=1, source_target_pairs={{0,1},{1,0},{2,3},{3,2},{4,5},{5,4},{6,7},{7,6},{8,9},{9,8},{10,11... | collective-permute-start | bytes 1474568 | tf_op jit(solution)/shard_map/ppermute | solution.py:172
  58.4 28.9 %all-to-all-start.2 = ((bf16[16,24,256]{2,1,0:T(8,128)(2,1)}), bf16[16,24,256]{2,1,0:T(8,128)(2,1)S(1)}, u32[]{:S(2)}, u32[]{:S(2)}) async-start(bf16[16,24,256]{2,1,0:T(8,128)(2,1)} %bitcast.15), calls=%async_computation.2 | async-start | bytes 393216 | tf_op jit(solution)/shard_map/all_to_all | solution.py:27
  73.3 0.7 collective-permute-start.7
  125.8 25.7 %copy-start.3 = (f32[24,2048]{1,0:T(8,128)S(1)}, f32[24,2048]{1,0:T(8,128)}, u32[]{:S(2)}) copy-start(f32[24,2048]{1,0:T(8,128)} %first.1) | copy-start | bytes 589828
